TPU v7x, 256 devices: a whole 4x4x8 slice. The times are simulated.
256 devices in a mesh: row: 64 (over y_hi, z, x), col: 4 (over y_lo, core).
Axes of the slice: x: 4, y: 4 (y_hi: 2, y_lo: 2; y = y_hi * 2 + y_lo), z: 8, core: 2. Of those that a mesh axis runs over, the one named last changes fastest.
Arguments:
- diagonal_inverses: bfloat16 [192, 2048, 2048], P('row', 'col'), may hold values from -0.125 to 0.125
- column_basis: bfloat16 [192, 2048, 256], P('row', 'col'), may hold values from -6 to 6
- row_basis: bfloat16 [192, 2048, 256], P('row', 'col'), may hold values from -0.125 to 0.125
- transfer: float32 [192, 256, 256], P('row', 'col'), may hold values from -0.375 to 0.375
- coupling: float32 [192, 256, 256], P('row', 'col'), may hold values from -6 to 6
- ranks: int32 [192], P('row'), may hold values from 128 to 256, as said below
Outputs:
- merged: float32 [192, 256, 256], P('row', 'col')
- parent_skeleton: float32 [192, 256, 256], P('row', 'col')
Inputs may be any that keep to these rules, and one draw needn't show every extreme that they name: `ranks`: each rank is 128 or 256; both occur in every draw.
All inputs are finite; a program needn't handle non-finite values.
Results may differ from a plain program's by a relative error of at most 0.0021.
Values may be sent and summed in bfloat16 or wider, within the bound.
No kernel may reach another device: no remote copies, remote signals or barrier semaphores. Data moves between devices by JAX's collectives and lax.ppermute only.
A program may use at most 64 MiB of HBM per device.

v0:
```python
import jax
import jax.numpy as jnp
from jax import lax
from jax.sharding import PartitionSpec as P

BIT = 2


def swapped(block, axis, bit):
    count = lax.axis_size(axis)
    route = []
    for low in range(count):
        high = low | 1 << bit
        if high != low and high < count:
            route += [(low, high), (high, low)]
    return lax.ppermute(block, axis, route)


def shards(diagonal_inverses, column_basis, row_basis, transfer, coupling, ranks):
    rank_width = transfer.shape[2]
    part_rows = transfer.shape[1]
    highest = lax.Precision.HIGHEST
    live_cols = jnp.arange(rank_width, dtype=jnp.int32)[None, :] < ranks[:, None]
    left_factor_basis = jnp.where(live_cols[:, None, :], column_basis, jnp.zeros_like(column_basis))
    right_factor_basis = jnp.where(live_cols[:, None, :], row_basis, jnp.zeros_like(row_basis))
    eliminated_part = jnp.einsum(
        "nmp,npr->nmr",
        diagonal_inverses,
        lax.all_gather(left_factor_basis, "col", axis=1, tiled=True),
        preferred_element_type=jnp.float32,
    ).astype(jnp.bfloat16)
    skeleton = jnp.transpose(
        lax.psum_scatter(
            jnp.einsum(
                "hgp,hgd->phd",
                right_factor_basis,
                eliminated_part,
                preferred_element_type=jnp.float32,
            ),
            "col",
            scatter_dimension=0,
            tiled=True,
        ),
        (1, 0, 2),
    )
    offset_rows = lax.axis_index("col") * part_rows
    active_rows = lax.dynamic_slice_in_dim(live_cols, offset_rows, part_rows, 1)
    masked = transfer * active_rows[:, :, None].astype(jnp.float32)
    complete_local_block = lax.all_gather(masked, "col", axis=1, tiled=True)
    whole_sib = swapped(complete_local_block, "row", BIT)
    merged = jnp.einsum("nij,njk->nik", skeleton, complete_local_block, precision=highest)
    merged = merged + jnp.einsum("nij,njk->nik", coupling, whole_sib, precision=highest)
    own_term = jnp.transpose(
        lax.psum_scatter(
            jnp.einsum("nji,njk->ink", masked, merged, precision=highest),
            "col",
            scatter_dimension=0,
            tiled=True,
        ),
        (1, 0, 2),
    )
    parent = own_term + swapped(own_term, "row", BIT)
    return (merged, parent)


def solution(mesh):
    placed = (
        P("row", "col", None),
        P("row", "col", None),
        P("row", "col", None),
        P("row", "col", None),
        P("row", "col", None),
        P("row"),
    )
    return jax.shard_map(
        shards,
        mesh=mesh,
        in_specs=placed,
        out_specs=(P("row", "col", None), P("row", "col", None)),
        check_vma=False,
    )
```

profile of v0, /device:TPU:8, one launch (start us, length us, event | category | flops | bytes accessed | tf_op | source)
XLA Modules:
  0.0 157.3 jit_solution(8034371410100171927)
XLA Ops:
  7.2 0.0 all-gather.2.cloned.1.call-start
  7.2 0.8 iota_compare_fusion
  8.0 2.1 %broadcast_select_fusion = bf16[3,512,256]{2,1,0:T(8,128)(2,1)} fusion(bf16[3,512,256]{2,1,0:T(8,128)(2,1)} %param.7, pred[3,256]{1,0:T(4,128)(4,1)S(1)} %iota_compare_fusion), kind=kLoop, calls=%fused_computation.7 | loop fusion | flops 393216 | bytes 1573632 | tf_op jit(solution)/shard_map/jit(_where)/select_n | solution.py:24
  10.1 0.0 reduce-scatter.2.cloned.1.call-start
  10.2 41.6 %all-gather.2.cloned.1.call-done = bf16[3,2048,256]{2,1,0:T(8,128)(2,1)} async-done(((bf16[3,512,256]{2,1,0:T(8,128)(2,1)}), bf16[3,2048,256]{2,1,0:T(8,128)(2,1)}) %all-gather.2.cloned.1.call-update) | async-done | bytes 3145744 | tf_op jit(solution)/shard_map/all_gather | solution.py:29
  51.8 7.1 %convolution_bitcast_fusion = f32[256,3,256]{2,0,1:T(8,128)} fusion(bf16[3,2048,256]{2,1,0:T(8,128)(2,1)} %all-gather.2.cloned.1.call-done, bf16[3,512,2048]{2,1,0:T(8,128)(2,1)} %param.6, bf16[3,512,256]{2,1,0:T(8,128)(2,1)} %param.8, pred[3,256]{1,0:T(4,128)(4,1)S(1)} %iota_compare_fusion), kind=kOutput, calls=%fused_computation.1 | convolution fusion | flops 1812725760 | bytes 11010816 | tf_op jit(solution)/shard_map/hgp,hgd->phd/dot_general | solution.py:34
  58.9 0.0 all-reduce.3.cloned.1.call-start
  59.0 0.1 dynamic-slice_convert_fusion
  59.1 0.1 broadcast_multiply_fusion
  59.2 9.2 %all_gather.7 = f32[3,256,256]{2,1,0:T(8,128)S(1)} all-gather(f32[3,64,256]{2,1,0:T(8,128)S(1)} %broadcast_multiply_fusion), channel_id=1, replica_groups=mesh['row'=64,'col'=4] {'col'}, dimensions={1}, use_global_device_ids=true | all-gather | bytes 983040 | tf_op jit(solution)/shard_map/all_gather | solution.py:49
  68.3 1.8 %collective-permute-start = (f32[3,256,256]{2,1,0:T(8,128)S(1)}, f32[3,256,256]{2,1,0:T(8,128)S(1)}, u32[]{:S(2)}, u32[]{:S(2)}) collective-permute-start(f32[3,256,256]{2,1,0:T(8,128)S(1)} %all_gather.7), channel_id=1, source_target_pairs={{0,16},{16,0},{4,20},{20,4},{8,24},{24,8},{12,28},{28,12},{32,48},... | collective-permute-start | bytes 2359304 | tf_op jit(solution)/shard_map/ppermute | solution.py:16
  70.1 11.8 %reduce-scatter.2.cloned.1.call-done = f32[64,3,256]{2,0,1:T(8,128)} async-done(((f32[256,3,256]{2,0,1:T(8,128)}), f32[64,3,256]{2,0,1:T(8,128)}) %reduce-scatter.2.cloned.1.call-update) | async-done | bytes 196624 | tf_op jit(solution)/shard_map/reduce_scatter | solution.py:33
  82.0 1.5 fusion.4
  83.5 4.7 %collective-permute-done = f32[3,256,256]{2,1,0:T(8,128)S(1)} collective-permute-done((f32[3,256,256]{2,1,0:T(8,128)S(1)}, f32[3,256,256]{2,1,0:T(8,128)S(1)}, u32[]{:S(2)}, u32[]{:S(2)}) %collective-permute-start) | collective-permute-done | bytes 786464 | tf_op jit(solution)/shard_map/ppermute | solution.py:16
  88.2 0.6 fusion
  88.8 0.8 convolution_bitcast_fusion.1
  89.6 1.4 copy.9
  91.0 0.6 dynamic-slice
  92.3 47.2 %all-reduce.3.cloned.1.call-done = f32[256,3,256]{2,1,0:T(4,128)} async-done(((f32[256,3,256]{2,1,0:T(4,128)}), f32[256,3,256]{2,1,0:T(4,128)}) %all-reduce.3.cloned.1.call-update) | async-done | bytes 786448
  139.5 1.0 dynamic-slice_bitcast_fusion
  140.5 1.6 %collective-permute-start.1 = (f32[3,64,256]{2,0,1:T(4,128)S(1)}, f32[3,64,256]{2,0,1:T(4,128)S(1)}, u32[]{:S(2)}, u32[]{:S(2)}) collective-permute-start(f32[3,64,256]{2,0,1:T(4,128)S(1)} %dynamic-slice_bitcast_fusion), channel_id=1, source_target_pairs={{0,16},{16,0},{4,20},{20,4},{8,24},{24,8},{12,28},{28,12},{32,48},... | collective-permute-start | bytes 589832 | tf_op jit(solution)/shard_map/ppermute | solution.py:16
  142.1 6.9 %collective-permute-done.1 = f32[3,64,256]{2,0,1:T(4,128)S(1)} collective-permute-done((f32[3,64,256]{2,0,1:T(4,128)S(1)}, f32[3,64,256]{2,0,1:T(4,128)S(1)}, u32[]{:S(2)}, u32[]{:S(2)}) %collective-permute-start.1) | collective-permute-done | bytes 196640 | tf_op jit(solution)/shard_map/ppermute | solution.py:16
  149.0 1.0 fusion.14
  150.0 0.7 copy.10
  (11 shorter events, 0.1 us)
Async XLA Ops:
  7.2 81.0 %copy-start = (f32[3,64,256]{2,1,0:T(8,128)S(1)}, f32[3,64,256]{2,1,0:T(8,128)}, u32[]{:S(2)}) copy-start(f32[3,64,256]{2,1,0:T(8,128)} %param.10) | copy-start | bytes 589828
  7.2 44.6 %all-gather.2.cloned.1.call-start = ((), (), s32[]{:S(2)}) async-start(), calls=%async_computation.1 | async-start | bytes 3932160 | tf_op jit(solution)/shard_map/all_gather | solution.py:29
  10.1 49.0 %copy-start.2 = (f32[3,64,256]{2,1,0:T(8,128)S(1)}, f32[3,64,256]{2,1,0:T(8,128)}, u32[]{:S(2)}) copy-start(f32[3,64,256]{2,1,0:T(8,128)} %param.9) | copy-start | bytes 589828
  10.1 71.9 %reduce-scatter.2.cloned.1.call-start = ((), (), s32[]{:S(2)}) async-start(), calls=%async_computation.2 | async-start | bytes 983040 | tf_op jit(solution)/shard_map/reduce_scatter | solution.py:33
  58.9 80.6 %all-reduce.3.cloned.1.call-start = ((), (), s32[]{:S(2)}) async-start(), calls=%async_computation.3 | async-start | bytes 2097152
  68.3 22.7 %copy-start.3 = (u32[256]{0:T(256)S(1)}, u32[256]{0:T(256)}, u32[]{:S(2)}) copy-start(u32[256]{0:T(256)} %constant.20) | copy-start | bytes 3076
  68.3 19.8 %collective-permute-start = (f32[3,256,256]{2,1,0:T(8,128)S(1)}, f32[3,256,256]{2,1,0:T(8,128)S(1)}, u32[]{:S(2)}, u32[]{:S(2)}) collective-permute-start(f32[3,256,256]{2,1,0:T(8,128)S(1)} %all_gather.7), channel_id=1, source_target_pairs={{0,16},{16,0},{4,20},{20,4},{8,24},{24,8},{12,28},{28,12},{32,48},... | collective-permute-start | bytes 2359304 | tf_op jit(solution)/shard_map/ppermute | solution.py:16
  88.8 62.0 %copy-start.1 = (f32[3,64,256]{2,1,0:T(8,128)}, f32[3,64,256]{2,1,0:T(8,128)S(1)}, u32[]{:S(2)}) copy-start(f32[3,64,256]{2,1,0:T(8,128)S(1)} %fusion) | copy-start | bytes 589828
  140.5 8.5 %collective-permute-start.1 = (f32[3,64,256]{2,0,1:T(4,128)S(1)}, f32[3,64,256]{2,0,1:T(4,128)S(1)}, u32[]{:S(2)}, u32[]{:S(2)}) collective-permute-start(f32[3,64,256]{2,0,1:T(4,128)S(1)} %dynamic-slice_bitcast_fusion), channel_id=1, source_target_pairs={{0,16},{16,0},{4,20},{20,4},{8,24},{24,8},{12,28},{28,12},{32,48},... | collective-permute-start | bytes 589832 | tf_op jit(solution)/shard_map/ppermute | solution.py:16
Sparse Core Ops, SparseCore 0:
  10.2 41.5 all-gather.1
  59.0 22.8 reduce-scatter.1
  91.2 48.2 all-reduce.2
where the time goes:
time: 158 us; the launch traced here: 157 us
  waiting for transfers between devices  112 us (71%)
  between operations  14.5 us (9%)
  matrix products  10.1 us (6%)
  blocking collectives  9.16 us (6%)
  other arithmetic  4.03 us (3%)
  local copies, waits for them, and re-layouts  3.68 us (2%)
  starting transfers between devices  3.56 us (2%)
    unnamed x4, waiting for transfers between devices  47.3 us
    all_gather x1, waiting for transfers between devices, shards(): lax.all_gather(left_factor_basis, 'col', axis=1, tiled=True)  41.6 us
    reduce_scatter x1, waiting for transfers between devices, shards(): lax.psum_scatter(jnp.einsum('hgp,hgd->phd', right_factor_basis, eliminate...  11.8 us
    ppermute x2, waiting for transfers between devices, swapped(): return lax.ppermute(block, axis, route)  11.6 us
    all_gather x1, blocking collectives, shards(): complete_local_block = lax.all_gather(masked, 'col', axis=1, tiled=True)  9.16 us
    dot_general x1, matrix products, shards(): jnp.einsum('hgp,hgd->phd', right_factor_basis, eliminated_part, preferred...  7.11 us
    ppermute x2, starting transfers between devices, swapped(): return lax.ppermute(block, axis, route)  3.44 us
  transfers between devices with their start and end apart: 5, of which 5 were waited for; matrix products, arithmetic and copies ran while one was open for 1% of the time, Pallas kernels for 0%

commit v1 on v0

v1 whole, which is shorter than its diff:
```python
import functools

import jax
import jax.numpy as jnp
from jax import lax
from jax.experimental import pallas as pl
from jax.experimental.pallas import tpu as pltpu
from jax.sharding import PartitionSpec as P

BIT = 2
F32 = jnp.float32
BF16 = jnp.bfloat16
HIGH = lax.Precision.HIGHEST
WIDTH = 2.0**17
CORE = [(0, 1), (1, 0), (2, 3), (3, 2)]
CHIP = [(0, 2), (2, 0), (1, 3), (3, 1)]


def siblings():
    count = lax.axis_size("row")
    return [(low, low ^ 1 << BIT) for low in range(count)]


def to_core(block):
    return lax.ppermute(block, "col", CORE)


def to_chip(block):
    return lax.ppermute(block, "col", CHIP)


def to_sibling(block):
    return lax.ppermute(block, "row", siblings())


def params(mib):
    return pltpu.CompilerParams(vmem_limit_bytes=mib << 20)


def dot(a, b, dims=((1,), (0,)), precision=None):
    return lax.dot_general(a, b, (dims, ((), ())), precision=precision, preferred_element_type=F32)


def eliminate_kernel(info, d, own, core, chip, cross, right, out):
    depth = own.shape[1]
    q = info[0]

    def term(k, part):
        start = pl.multiple_of((q ^ k) * depth, depth)
        return dot(d[0, :, pl.ds(start, depth)], part)

    elim = term(0, own[0]) + term(1, core[0]) + term(2, chip[...]) + term(3, cross[...])
    piece = dot(right[0], elim.astype(BF16), ((0,), (0,)))

    @pl.when(pl.program_id(0) == 0)
    def _():
        out[...] = piece

    @pl.when(pl.program_id(0) != 0)
    def _():
        out[...] += piece


def eliminate(n, info, d, own, core, chip, cross, right, steps=2):
    rows, depth, width = d.shape[1], own.shape[1], own.shape[2]
    tile = rows // steps
    whole = pl.BlockSpec((1, depth, width), lambda i, s: (n, 0, 0))
    flat = pl.BlockSpec((depth, width), lambda i, s: (0, 0))
    return pl.pallas_call(
        eliminate_kernel,
        grid_spec=pltpu.PrefetchScalarGridSpec(
            num_scalar_prefetch=1,
            grid=(steps,),
            in_specs=[
                pl.BlockSpec((1, tile, d.shape[2]), lambda i, s: (n, i, 0)),
                whole,
                whole,
                flat,
                flat,
                pl.BlockSpec((1, tile, width), lambda i, s: (n, i, 0)),
            ],
            out_specs=pl.BlockSpec((width, width), lambda i, s: (0, 0)),
        ),
        out_shape=jax.ShapeDtypeStruct((width, width), F32),
        compiler_params=params(16),
        cost_estimate=pl.CostEstimate(flops=2 * rows * width * (d.shape[2] + width), bytes_accessed=4 << 20, transcendentals=0),
        name=f"eliminate{n}",
    )(info, d, own, core, chip, cross, right)


def couple_kernel(info, blocks, c_own, c_core, m_out, cm_out, sib, c_all):
    q = info[0]
    part = blocks.shape[3]
    for k in range(4):
        rows = pl.ds(pl.multiple_of((q ^ k) * part, part), part)
        m_out[0, rows, :] = blocks[k, 0, 0]
        sib[rows, :] = blocks[k, 1, 0]
    half = q & 1
    c_all[pl.ds(pl.multiple_of(half * part, part), part), :] = c_own[0]
    c_all[pl.ds(pl.multiple_of((1 - half) * part, part), part), :] = c_core[0]
    cm_out[0] = dot(c_all[...], sib[...], precision=HIGH)


def couple(info, blocks, c_own, c_core):
    nodes, part, width = c_own.shape
    one = pl.BlockSpec((1, part, width), lambda n, s: (n, 0, 0))
    return pl.pallas_call(
        couple_kernel,
        grid_spec=pltpu.PrefetchScalarGridSpec(
            num_scalar_prefetch=1,
            grid=(nodes,),
            in_specs=[pl.BlockSpec((4, 2, 1, part, width), lambda n, s: (0, 0, n, 0, 0)), one, one],
            out_specs=[
                pl.BlockSpec((1, width, width), lambda n, s: (n, 0, 0)),
                pl.BlockSpec((1, 2 * part, width), lambda n, s: (n, 0, 0)),
            ],
            scratch_shapes=[pltpu.VMEM((width, width), F32), pltpu.VMEM((2 * part, width), F32)],
        ),
        out_shape=[
            jax.ShapeDtypeStruct((nodes, width, width), F32),
            jax.ShapeDtypeStruct((nodes, 2 * part, width), F32),
        ],
        compiler_params=params(16),
        cost_estimate=pl.CostEstimate(flops=12 * nodes * 2 * part * width * width, bytes_accessed=4 << 20, transcendentals=0),
        name="couple",
    )(info, blocks, c_own, c_core)


def merge_kernel(n, info, s_own, s_core, m, cm, t_own, p_own, send, t_all, p_all):
    q = info[0]
    rank = info[1 + n]
    part = t_own.shape[0]
    width = t_own.shape[1]
    row = lax.broadcasted_iota(jnp.int32, (width, width), 0)
    col = lax.broadcasted_iota(jnp.int32, (width, width), 1)
    s = jnp.where((row < rank) & (col < rank), s_own[...] + s_core[...], 0.0)
    t_all[...] = dot(s, m[0], precision=HIGH)
    t_all[pl.ds(pl.multiple_of((q >> 1) * (2 * part), 2 * part), 2 * part), :] += cm[0]
    p_all[...] = dot(m[0], t_all[...], ((0,), (0,)), precision=HIGH)
    mine = pl.ds(pl.multiple_of(q * part, part), part)
    other = pl.ds(pl.multiple_of((q ^ 2) * part, part), part)
    t_own[...] = t_all[mine, :]
    p_own[...] = p_all[mine, :]
    send[0:part, :] = t_all[other, :].astype(BF16)
    send[part : 2 * part, :] = p_all[other, :].astype(BF16)


def merge(n, info, s_own, s_core, m, cm):
    width = m.shape[2]
    part = cm.shape[1] // 2
    flat = pl.BlockSpec((width, width), lambda i, s: (0, 0))
    piece = pl.BlockSpec((part, width), lambda i, s: (0, 0))
    return pl.pallas_call(
        functools.partial(merge_kernel, n),
        grid_spec=pltpu.PrefetchScalarGridSpec(
            num_scalar_prefetch=1,
            grid=(1,),
            in_specs=[
                flat,
                flat,
                pl.BlockSpec((1, width, width), lambda i, s: (n, 0, 0)),
                pl.BlockSpec((1, 2 * part, width), lambda i, s: (n, 0, 0)),
            ],
            out_specs=[piece, piece, pl.BlockSpec((2 * part, width), lambda i, s: (0, 0))],
            scratch_shapes=[pltpu.VMEM((width, width), F32), pltpu.VMEM((width, width), F32)],
        ),
        out_shape=[
            jax.ShapeDtypeStruct((part, width), F32),
            jax.ShapeDtypeStruct((part, width), F32),
            jax.ShapeDtypeStruct((2 * part, width), BF16),
        ],
        compiler_params=params(16),
        cost_estimate=pl.CostEstimate(flops=24 * width**3, bytes_accessed=1 << 20, transcendentals=0),
        name=f"merge{n}",
    )(info, s_own, s_core, m, cm)


def shards(diagonal_inverses, column_basis, row_basis, transfer, coupling, ranks):
    nodes, part, width = transfer.shape
    q = lax.axis_index("col").astype(jnp.int32)
    info = jnp.concatenate([q[None], ranks.astype(jnp.int32)])

    chip_left = [to_chip(column_basis[n]) for n in range(nodes)]
    core_left = to_core(column_basis)
    cross_left = [to_core(block) for block in chip_left]

    rows = q * part + jnp.arange(part, dtype=jnp.int32)
    masked = jnp.where((rows[None, :] < ranks[:, None])[:, :, None], transfer, 0.0)
    m_own = (masked * WIDTH).astype(jnp.float16)
    m_pair = jnp.stack([m_own, to_chip(m_own)])
    m_sib = to_sibling(m_pair)
    m_mine = jnp.stack([m_pair, m_sib], 1)
    m_core = to_core(m_mine)
    blocks = jnp.stack([m_mine[0], m_core[0], m_mine[1], m_core[1]]).astype(F32) * (1 / WIDTH)
    whole, coupled = couple(info, blocks, coupling, to_core(coupling))

    merged, parent = [], []
    for n in range(nodes):
        s = eliminate(n, info, diagonal_inverses, column_basis, core_left, chip_left[n], cross_left[n], row_basis)
        t_own, p_own, send = merge(n, info, s, to_core(s), whole, coupled)
        got = to_chip(send).astype(F32)
        merged.append(t_own + got[:part])
        p_pair = p_own + got[part:]
        parent.append(p_pair + to_sibling(p_pair))
    return jnp.stack(merged), jnp.stack(parent)


def solution(mesh):
    block = P("row", "col", None)
    return jax.shard_map(
        shards,
        mesh=mesh,
        in_specs=(block, block, block, block, block, P("row")),
        out_specs=(block, block),
        check_vma=False,
    )
```

time: 158 us -> 56.1 us (0.36)
  waiting for transfers between devices: 112 us -> 21 us
  between operations: 14.5 us -> 0.92 us
  Pallas kernels: 0 us -> 12.6 us
  matrix products: 10.1 us -> 0 us
  starting transfers between devices: 3.56 us -> 13.4 us
  blocking collectives: 9.16 us -> 0 us
    unnamed x4 -> x0, waiting for transfers between devices: 47.3 us -> none
    all_gather x1 -> x0, waiting for transfers between devices: 41.6 us -> none  [shards(): lax.all_gather(left_factor_basis, 'col', axis=1, tiled=True)]
    pallas_call x0 -> x7, Pallas kernels: none -> 12.6 us  [the longest x3 5.78 us: eliminate(): pl.pallas_call(eliminate_kernel, grid_spec=pltpu.PrefetchScalarGridSpec(n...]
    reduce_scatter x1 -> x0, waiting for transfers between devices: 11.8 us -> none  [shards(): lax.psum_scatter(jnp.einsum('hgp,hgd->phd', right_factor_basis, eliminate...]
    dot_general x4 -> x0, matrix products: 10.1 us -> none  [the longest x1 7.11 us: shards(): jnp.einsum('hgp,hgd->phd', right_factor_basis, eliminated_part, preferred...]
    ppermute x2 -> x20, starting transfers between devices: 3.44 us -> 13.4 us  [the longest x7 7.28 us: to_chip(): return lax.ppermute(block, 'col', CHIP)]
    ppermute x2 -> x20, waiting for transfers between devices: 11.6 us -> 21 us  [the longest x7 17.6 us: to_chip(): return lax.ppermute(block, 'col', CHIP)]
    all_gather x1 -> x0, blocking collectives: 9.16 us -> none  [shards(): complete_local_block = lax.all_gather(masked, 'col', axis=1, tiled=True)]
  transfers between devices with their start and end apart: 5 -> 20, of which waited for: 5 -> 6; matrix products, arithmetic and copies ran while one was open for 1% -> 5% of each run, Pallas kernels for 0% -> 23%
where the time goes in v1:
time: 56.1 us; the launch traced here: 55.9 us
  waiting for transfers between devices  21 us (37%)
  starting transfers between devices  13.4 us (24%)
  Pallas kernels  12.6 us (22%)
  local copies, waits for them, and re-layouts  4.06 us (7%)
  other arithmetic  3.95 us (7%)
  between operations  0.92 us (2%)
    ppermute x7, waiting for transfers between devices, to_chip(): return lax.ppermute(block, 'col', CHIP)  17.6 us
    ppermute x7, starting transfers between devices, to_chip(): return lax.ppermute(block, 'col', CHIP)  7.28 us
    pallas_call x3, Pallas kernels, eliminate(): pl.pallas_call(eliminate_kernel, grid_spec=pltpu.PrefetchScalarGridSpec(n...  5.78 us
    pallas_call x3, Pallas kernels, merge(): pl.pallas_call(functools.partial(merge_kernel, n), grid_spec=pltpu.Prefet...  5.15 us
    ppermute x4, starting transfers between devices, to_sibling(): return lax.ppermute(block, 'row', siblings())  4.17 us
    ppermute x4, waiting for transfers between devices, to_sibling(): return lax.ppermute(block, 'row', siblings())  3.37 us
    unnamed x12, local copies, waits for them, and re-layouts  2.81 us
    ppermute x9, starting transfers between devices, to_core(): return lax.ppermute(block, 'col', CORE)  1.96 us
  transfers between devices with their start and end apart: 20, of which 6 were waited for; matrix products, arithmetic and copies ran while one was open for 5% of the time, Pallas kernels for 23%

profile of v1, /device:TPU:8, one launch (start us, length us, event | category | flops | bytes accessed | tf_op | source)
XLA Modules:
  0.0 55.9 jit_solution(14158758730299899606)
XLA Ops:
  0.7 0.8 %broadcast_compare_fusion = pred[3,64]{1,0:T(4,128)(4,1)S(1)} fusion(s32[64]{0:T(128)S(1)} %iota_add_fusion, s32[3]{0:T(128)} %param.11), kind=kLoop, calls=%fused_computation.27 | loop fusion | flops 192 | bytes 460 | tf_op jit(solution)/shard_map/lt | solution.py:188
  1.4 1.0 %multiply_convert_fusion = f16[3,64,256]{2,1,0:T(8,128)(2,1)S(1)} fusion(f32[3,64,256]{2,1,0:T(8,128)} %param.9, pred[3,64]{1,0:T(4,128)(4,1)S(1)} %broadcast_compare_fusion), kind=kLoop, calls=%fused_computation.14 | loop fusion | flops 147456 | bytes 295104 | tf_op jit(solution)/shard_map/convert_element_type | solution.py:189
  2.5 2.3 %collective-permute-start.4 = (f16[3,64,256]{2,1,0:T(8,128)(2,1)S(1)}, f16[3,64,256]{2,1,0:T(8,128)(2,1)S(1)}, u32[]{:S(2)}, u32[]{:S(2)}) collective-permute-start(f16[3,64,256]{2,1,0:T(8,128)(2,1)S(1)} %multiply_convert_fusion), channel_id=1, source_target_pairs={{0,2},{2,0},{1,3},{3,1},{4,6},{6,4},{5,7},{7,5},{8,10},{10,8},{9,1... | collective-permute-start | bytes 294920 | tf_op jit(solution)/shard_map/ppermute | solution.py:29
  4.7 1.2 %slice_bitcast_fusion.2 = (bf16[512,256]{1,0:T(8,128)(2,1)S(1)}, bf16[512,256]{1,0:T(8,128)(2,1)S(1)}, bf16[512,256]{1,0:T(8,128)(2,1)S(1)}) fusion(bf16[3,512,256]{2,1,0:T(8,128)(2,1)} %own.5), kind=kLoop, calls=%fused_computation.8 | loop fusion | bytes 1572864 | tf_op jit(solution)/shard_map/squeeze | solution.py:183
  6.2 1.9 %collective-permute-start.9 = (bf16[512,256]{1,0:T(8,128)(2,1)S(1)}, bf16[512,256]{1,0:T(8,128)(2,1)S(1)}, u32[]{:S(2)}, u32[]{:S(2)}) collective-permute-start(bf16[512,256]{1,0:T(8,128)(2,1)S(1)} %get-tuple-element.25), channel_id=1, source_target_pairs={{0,2},{2,0},{1,3},{3,1},{4,6},{6,4},{5,7},{7,5},{8,10},{10,8},{9,1... | collective-permute-start | bytes 786440 | tf_op jit(solution)/shard_map/ppermute | solution.py:29
  8.4 1.7 %collective-permute-start.5 = (f16[2,3,64,256]{3,2,1,0:T(8,128)(2,1)S(1)}, f16[2,3,64,256]{3,2,1,0:T(8,128)(2,1)S(1)}, u32[]{:S(2)}, u32[]{:S(2)}) collective-permute-start(f16[2,3,64,256]{3,2,1,0:T(8,128)(2,1)S(1)} %get-tuple-element.32), channel_id=1, source_target_pairs={{0,16},{4,20},{8,24},{12,28},{16,0},{20,4},{24,8},{28,12},{32,48},... | collective-permute-start | bytes 589832 | tf_op jit(solution)/shard_map/ppermute | solution.py:33
  10.1 5.1 %collective-permute-done.1.chip = bf16[512,256]{1,0:T(8,128)(2,1)S(1)} collective-permute-done((bf16[512,256]{1,0:T(8,128)(2,1)S(1)}, bf16[512,256]{1,0:T(8,128)(2,1)S(1)}, u32[]{:S(2)}, u32[]{:S(2)}) %collective-permute-start.1) | collective-permute-done | bytes 262176 | tf_op jit(solution)/shard_map/ppermute | solution.py:29
  15.1 5.6 %collective-permute-done.9.chip = bf16[512,256]{1,0:T(8,128)(2,1)S(1)} collective-permute-done((bf16[512,256]{1,0:T(8,128)(2,1)S(1)}, bf16[512,256]{1,0:T(8,128)(2,1)S(1)}, u32[]{:S(2)}, u32[]{:S(2)}) %collective-permute-start.9) | collective-permute-done | bytes 262176 | tf_op jit(solution)/shard_map/ppermute | solution.py:29
  20.8 5.2 %collective-permute-done.13.chip = bf16[512,256]{1,0:T(8,128)(2,1)S(1)} collective-permute-done((bf16[512,256]{1,0:T(8,128)(2,1)S(1)}, bf16[512,256]{1,0:T(8,128)(2,1)S(1)}, u32[]{:S(2)}, u32[]{:S(2)}) %collective-permute-start.13) | collective-permute-done | bytes 262176 | tf_op jit(solution)/shard_map/ppermute | solution.py:29
  27.0 2.8 %copy-done = bf16[3,512,2048]{2,1,0:T(8,128)(2,1)S(1)} copy-done((bf16[3,512,2048]{2,1,0:T(8,128)(2,1)S(1)}, bf16[3,512,2048]{2,1,0:T(8,128)(2,1)}, u32[]{:S(2)}) %copy-start) | copy-done | bytes 6291480
  29.8 1.9 %eliminate0.1.s_own = f32[256,256]{1,0:T(8,128)S(1)} custom-call(s32[4]{0:T(128)S(1)} %pad_add_fusion.info, bf16[3,512,2048]{2,1,0:T(8,128)(2,1)S(1)} %copy-done, bf16[3,512,256]{2,1,0:T(8,128)(2,1)S(1)} %copy-done.1, bf16[3,512,256]{2,1,0:T(8,128)(2,1)S(1)} %collective-permute-done.core, bf16[512,256]{1,0:T(8,128)(2,1)S(1)} %collective-permute-done.1.chip, ...), custom_call_target="tpu_custom_call" | custom-call | flops 603979776 | bytes 4194304 | tf_op jit(solution)/shard_map/eliminate0/pallas_call | solution.py:69
  32.3 1.9 %eliminate1.1.s_own = f32[256,256]{1,0:T(8,128)S(1)} custom-call(s32[4]{0:T(128)S(1)} %pad_add_fusion.info, bf16[3,512,2048]{2,1,0:T(8,128)(2,1)S(1)} %copy-done, bf16[3,512,256]{2,1,0:T(8,128)(2,1)S(1)} %copy-done.1, bf16[3,512,256]{2,1,0:T(8,128)(2,1)S(1)} %collective-permute-done.core, bf16[512,256]{1,0:T(8,128)(2,1)S(1)} %collective-permute-done.9.chip, ...), custom_call_target="tpu_custom_call" | custom-call | flops 603979776 | bytes 4194304 | tf_op jit(solution)/shard_map/eliminate1/pallas_call | solution.py:69
  34.4 1.9 %eliminate2.1.s_own = f32[256,256]{1,0:T(8,128)S(1)} custom-call(s32[4]{0:T(128)S(1)} %pad_add_fusion.info, bf16[3,512,2048]{2,1,0:T(8,128)(2,1)S(1)} %copy-done, bf16[3,512,256]{2,1,0:T(8,128)(2,1)S(1)} %copy-done.1, bf16[3,512,256]{2,1,0:T(8,128)(2,1)S(1)} %collective-permute-done.core, bf16[512,256]{1,0:T(8,128)(2,1)S(1)} %collective-permute-done.13.chip, ...), custom_call_target="tpu_custom_call" | custom-call | flops 603979776 | bytes 4194304 | tf_op jit(solution)/shard_map/eliminate2/pallas_call | solution.py:69
  37.2 1.7 %couple.1 = (f32[3,256,256]{2,1,0:T(8,128)S(1)}, f32[3,128,256]{2,1,0:T(8,128)S(1)}) custom-call(s32[4]{0:T(128)S(1)} %pad_add_fusion.info, f32[4,2,3,64,256]{4,3,2,1,0:T(8,128)S(1)} %convert_multiply_fusion.blocks, f32[3,64,256]{2,1,0:T(8,128)S(1)} %copy-done.3, f32[3,64,256]{2,1,0:T(8,128)S(1)} %collective-permute-done.7.c_core), custom_call_target="tpu_custom_call" | custom-call | flops 301989888 | bytes 4194304 | tf_op jit(solution)/shard_map/couple/pallas_call | solution.py:107
  38.9 1.7 %merge0.1 = (f32[64,256]{1,0:T(8,128)S(1)}, f32[64,256]{1,0:T(8,128)S(1)}, bf16[128,256]{1,0:T(8,128)(2,1)S(1)}) custom-call(s32[4]{0:T(128)S(1)} %pad_add_fusion.info, f32[256,256]{1,0:T(8,128)S(1)} %eliminate0.1.s_own, f32[256,256]{1,0:T(8,128)S(1)} %collective-permute-done.3.s_core, f32[3,256,256]{2,1,0:T(8,128)S(1)} %get-tuple-element.13.m, ...), custom_call_target="tpu_custom_call" | custom-call | flops 402653184 | bytes 1048576 | tf_op jit(solution)/shard_map/merge0/pallas_call | solution.py:153
  41.2 1.7 %merge1.1 = (f32[64,256]{1,0:T(8,128)S(1)}, f32[64,256]{1,0:T(8,128)S(1)}, bf16[128,256]{1,0:T(8,128)(2,1)S(1)}) custom-call(s32[4]{0:T(128)S(1)} %pad_add_fusion.info, f32[256,256]{1,0:T(8,128)S(1)} %eliminate1.1.s_own, f32[256,256]{1,0:T(8,128)S(1)} %collective-permute-done.11.s_core, f32[3,256,256]{2,1,0:T(8,128)S(1)} %get-tuple-element.13.m, ...), custom_call_target="tpu_custom_call" | custom-call | flops 402653184 | bytes 1048576 | tf_op jit(solution)/shard_map/merge1/pallas_call | solution.py:153
  42.9 1.8 %collective-permute-start.12 = (bf16[128,256]{1,0:T(8,128)(2,1)S(1)}, bf16[128,256]{1,0:T(8,128)(2,1)S(1)}, u32[]{:S(2)}, u32[]{:S(2)}) collective-permute-start(bf16[128,256]{1,0:T(8,128)(2,1)S(1)} %get-tuple-element.18), channel_id=1, source_target_pairs={{0,2},{2,0},{1,3},{3,1},{4,6},{6,4},{5,7},{7,5},{8,10},{10,8},{9,1... | collective-permute-start | bytes 196616 | tf_op jit(solution)/shard_map/ppermute | solution.py:29
  44.7 1.7 %merge2.1 = (f32[64,256]{1,0:T(8,128)S(1)}, f32[64,256]{1,0:T(8,128)S(1)}, bf16[128,256]{1,0:T(8,128)(2,1)S(1)}) custom-call(s32[4]{0:T(128)S(1)} %pad_add_fusion.info, f32[256,256]{1,0:T(8,128)S(1)} %eliminate2.1.s_own, f32[256,256]{1,0:T(8,128)S(1)} %collective-permute-done.15.s_core, f32[3,256,256]{2,1,0:T(8,128)S(1)} %get-tuple-element.13.m, ...), custom_call_target="tpu_custom_call" | custom-call | flops 402653184 | bytes 1048576 | tf_op jit(solution)/shard_map/merge2/pallas_call | solution.py:153
  46.9 1.6 %collective-permute-start.17 = (f32[64,256]{1,0:T(8,128)S(1)}, f32[64,256]{1,0:T(8,128)S(1)}, u32[]{:S(2)}, u32[]{:S(2)}) collective-permute-start(f32[64,256]{1,0:T(8,128)S(1)} %get-tuple-element.33), channel_id=1, source_target_pairs={{0,16},{4,20},{8,24},{12,28},{16,0},{20,4},{24,8},{28,12},{32,48},... | collective-permute-start | bytes 196616 | tf_op jit(solution)/shard_map/ppermute | solution.py:33
  49.1 1.7 %collective-permute-done.16 = bf16[128,256]{1,0:T(8,128)(2,1)S(1)} collective-permute-done((bf16[128,256]{1,0:T(8,128)(2,1)S(1)}, bf16[128,256]{1,0:T(8,128)(2,1)S(1)}, u32[]{:S(2)}, u32[]{:S(2)}) %collective-permute-start.16) | collective-permute-done | bytes 65568 | tf_op jit(solution)/shard_map/ppermute | solution.py:29
  51.1 0.7 %pad_maximum_fusion.2 = f32[3,64,256]{2,1,0:T(8,128)} fusion(f32[1,64,256]{2,1,0:T(8,128)S(1)} %get-tuple-element.38, f32[1,64,256]{2,1,0:T(8,128)S(1)} %get-tuple-element.36, f32[1,64,256]{2,1,0:T(8,128)S(1)} %get-tuple-element.34), kind=kLoop, calls=%fused_computation.12 | loop fusion | flops 98304 | bytes 393216 | tf_op jit(solution)/shard_map/stack | solution.py:205
  51.8 1.4 %collective-permute-done.18 = f32[64,256]{1,0:T(8,128)S(1)} collective-permute-done((f32[64,256]{1,0:T(8,128)S(1)}, f32[64,256]{1,0:T(8,128)S(1)}, u32[]{:S(2)}, u32[]{:S(2)}) %collective-permute-start.18) | collective-permute-done | bytes 65568 | tf_op jit(solution)/shard_map/ppermute | solution.py:33
  53.3 1.9 %collective-permute-done.19 = f32[64,256]{1,0:T(8,128)S(1)} collective-permute-done((f32[64,256]{1,0:T(8,128)S(1)}, f32[64,256]{1,0:T(8,128)S(1)}, u32[]{:S(2)}, u32[]{:S(2)}) %collective-permute-start.19) | collective-permute-done | bytes 65568 | tf_op jit(solution)/shard_map/ppermute | solution.py:33
  55.2 0.7 %pad_maximum_fusion.3 = f32[3,64,256]{2,1,0:T(8,128)} fusion(f32[1,64,256]{2,1,0:T(8,128)S(1)} %add_bitcast_fusion, f32[1,64,256]{2,1,0:T(8,128)S(1)} %add_bitcast_fusion.1, f32[1,64,256]{2,1,0:T(8,128)S(1)} %add_bitcast_fusion.2), kind=kLoop, calls=%fused_computation.13 | loop fusion | flops 98304 | bytes 393216 | tf_op jit(solution)/shard_map/stack | solution.py:205
  (57 shorter events, 5.1 us)
Async XLA Ops:
  2.5 24.2 %copy-start.5 = (s32[3]{0:T(128)S(1)}, s32[3]{0:T(128)}, u32[]{:S(2)}) copy-start(s32[3]{0:T(128)} %param.11) | copy-start | bytes 40
  2.5 5.8 %collective-permute-start.4 = (f16[3,64,256]{2,1,0:T(8,128)(2,1)S(1)}, f16[3,64,256]{2,1,0:T(8,128)(2,1)S(1)}, u32[]{:S(2)}, u32[]{:S(2)}) collective-permute-start(f16[3,64,256]{2,1,0:T(8,128)(2,1)S(1)} %multiply_convert_fusion), channel_id=1, source_target_pairs={{0,2},{2,0},{1,3},{3,1},{4,6},{6,4},{5,7},{7,5},{8,10},{10,8},{9,1... | collective-permute-start | bytes 294920 | tf_op jit(solution)/shard_map/ppermute | solution.py:29
  4.7 22.3 %collective-permute-start = (bf16[3,512,256]{2,1,0:T(8,128)(2,1)}, bf16[3,512,256]{2,1,0:T(8,128)(2,1)S(1)}, u32[]{:S(2)}, u32[]{:S(2)}) collective-permute-start(bf16[3,512,256]{2,1,0:T(8,128)(2,1)} %own.5), channel_id=1, source_target_pairs={{0,1},{1,0},{2,3},{3,2},{4,5},{5,4},{6,7},{7,6},{8,9},{9,8},{10,11... | collective-permute-start | bytes 2359304 | tf_op jit(solution)/shard_map/ppermute | solution.py:25
  5.9 21.0 %copy-start.3 = (f32[3,64,256]{2,1,0:T(8,128)S(1)}, f32[3,64,256]{2,1,0:T(8,128)}, u32[]{:S(2)}) copy-start(f32[3,64,256]{2,1,0:T(8,128)} %c_own.1) | copy-start | bytes 589828
  5.9 21.1 %copy-start.1 = (bf16[3,512,256]{2,1,0:T(8,128)(2,1)S(1)}, bf16[3,512,256]{2,1,0:T(8,128)(2,1)}, u32[]{:S(2)}) copy-start(bf16[3,512,256]{2,1,0:T(8,128)(2,1)} %own.5) | copy-start | bytes 2359300
  5.9 21.1 %copy-start.2 = (bf16[3,512,256]{2,1,0:T(8,128)(2,1)S(1)}, bf16[3,512,256]{2,1,0:T(8,128)(2,1)}, u32[]{:S(2)}) copy-start(bf16[3,512,256]{2,1,0:T(8,128)(2,1)} %right.5) | copy-start | bytes 2359300
  5.9 9.2 %collective-permute-start.1 = (bf16[512,256]{1,0:T(8,128)(2,1)S(1)}, bf16[512,256]{1,0:T(8,128)(2,1)S(1)}, u32[]{:S(2)}, u32[]{:S(2)}) collective-permute-start(bf16[512,256]{1,0:T(8,128)(2,1)S(1)} %get-tuple-element.24), channel_id=1, source_target_pairs={{0,2},{2,0},{1,3},{3,1},{4,6},{6,4},{5,7},{7,5},{8,10},{10,8},{9,1... | collective-permute-start | bytes 786440 | tf_op jit(solution)/shard_map/ppermute | solution.py:29
  6.2 14.6 %collective-permute-start.9 = (bf16[512,256]{1,0:T(8,128)(2,1)S(1)}, bf16[512,256]{1,0:T(8,128)(2,1)S(1)}, u32[]{:S(2)}, u32[]{:S(2)}) collective-permute-start(bf16[512,256]{1,0:T(8,128)(2,1)S(1)} %get-tuple-element.25), channel_id=1, source_target_pairs={{0,2},{2,0},{1,3},{3,1},{4,6},{6,4},{5,7},{7,5},{8,10},{10,8},{9,1... | collective-permute-start | bytes 786440 | tf_op jit(solution)/shard_map/ppermute | solution.py:29
  8.1 17.9 %collective-permute-start.13 = (bf16[512,256]{1,0:T(8,128)(2,1)S(1)}, bf16[512,256]{1,0:T(8,128)(2,1)S(1)}, u32[]{:S(2)}, u32[]{:S(2)}) collective-permute-start(bf16[512,256]{1,0:T(8,128)(2,1)S(1)} %get-tuple-element.26), channel_id=1, source_target_pairs={{0,2},{2,0},{1,3},{3,1},{4,6},{6,4},{5,7},{7,5},{8,10},{10,8},{9,1... | collective-permute-start | bytes 786440 | tf_op jit(solution)/shard_map/ppermute | solution.py:29
  8.4 17.6 %collective-permute-start.5 = (f16[2,3,64,256]{3,2,1,0:T(8,128)(2,1)S(1)}, f16[2,3,64,256]{3,2,1,0:T(8,128)(2,1)S(1)}, u32[]{:S(2)}, u32[]{:S(2)}) collective-permute-start(f16[2,3,64,256]{3,2,1,0:T(8,128)(2,1)S(1)} %get-tuple-element.32), channel_id=1, source_target_pairs={{0,16},{4,20},{8,24},{12,28},{16,0},{20,4},{24,8},{28,12},{32,48},... | collective-permute-start | bytes 589832 | tf_op jit(solution)/shard_map/ppermute | solution.py:33
  15.1 11.7 %collective-permute-start.2 = (bf16[512,256]{1,0:T(8,128)(2,1)S(1)}, bf16[512,256]{1,0:T(8,128)(2,1)S(1)}, u32[]{:S(2)}, u32[]{:S(2)}) collective-permute-start(bf16[512,256]{1,0:T(8,128)(2,1)S(1)} %collective-permute-done.1.chip), channel_id=1, source_target_pairs={{0,1},{1,0},{2,3},{3,2},{4,5},{5,4},{6,7},{7,6},{8,9},{9,8},{10,11... | collective-permute-start | bytes 786440 | tf_op jit(solution)/shard_map/ppermute | solution.py:25
  20.8 11.6 %collective-permute-start.10 = (bf16[512,256]{1,0:T(8,128)(2,1)S(1)}, bf16[512,256]{1,0:T(8,128)(2,1)S(1)}, u32[]{:S(2)}, u32[]{:S(2)}) collective-permute-start(bf16[512,256]{1,0:T(8,128)(2,1)S(1)} %collective-permute-done.9.chip), channel_id=1, source_target_pairs={{0,1},{1,0},{2,3},{3,2},{4,5},{5,4},{6,7},{7,6},{8,9},{9,8},{10,11... | collective-permute-start | bytes 786440 | tf_op jit(solution)/shard_map/ppermute | solution.py:25
  26.0 8.4 %collective-permute-start.14 = (bf16[512,256]{1,0:T(8,128)(2,1)S(1)}, bf16[512,256]{1,0:T(8,128)(2,1)S(1)}, u32[]{:S(2)}, u32[]{:S(2)}) collective-permute-start(bf16[512,256]{1,0:T(8,128)(2,1)S(1)} %collective-permute-done.13.chip), channel_id=1, source_target_pairs={{0,1},{1,0},{2,3},{3,2},{4,5},{5,4},{6,7},{7,6},{8,9},{9,8},{10,11... | collective-permute-start | bytes 786440 | tf_op jit(solution)/shard_map/ppermute | solution.py:25
  26.1 10.8 %collective-permute-start.6 = (f16[2,2,3,64,256]{4,3,2,1,0:T(8,128)(2,1)S(1)}, f16[2,2,3,64,256]{4,3,2,1,0:T(8,128)(2,1)S(1)}, u32[]{:S(2)}, u32[]{:S(2)}) collective-permute-start(f16[2,2,3,64,256]{4,3,2,1,0:T(8,128)(2,1)S(1)} %pad_maximum_fusion), channel_id=1, source_target_pairs={{0,1},{1,0},{2,3},{3,2},{4,5},{5,4},{6,7},{7,6},{8,9},{9,8},{10,11... | collective-permute-start | bytes 1179656 | tf_op jit(solution)/shard_map/ppermute | solution.py:25
  26.9 10.3 %collective-permute-start.7 = (f32[3,64,256]{2,1,0:T(8,128)S(1)}, f32[3,64,256]{2,1,0:T(8,128)S(1)}, u32[]{:S(2)}, u32[]{:S(2)}) collective-permute-start(f32[3,64,256]{2,1,0:T(8,128)S(1)} %copy-done.3), channel_id=1, source_target_pairs={{0,1},{1,0},{2,3},{3,2},{4,5},{5,4},{6,7},{7,6},{8,9},{9,8},{10,11... | collective-permute-start | bytes 589832 | tf_op jit(solution)/shard_map/ppermute | solution.py:25
  31.8 7.1 %collective-permute-start.3 = (f32[256,256]{1,0:T(8,128)S(1)}, f32[256,256]{1,0:T(8,128)S(1)}, u32[]{:S(2)}, u32[]{:S(2)}) collective-permute-start(f32[256,256]{1,0:T(8,128)S(1)} %eliminate0.1.s_own), channel_id=1, source_target_pairs={{0,1},{1,0},{2,3},{3,2},{4,5},{5,4},{6,7},{7,6},{8,9},{9,8},{10,11... | collective-permute-start | bytes 786440 | tf_op jit(solution)/shard_map/ppermute | solution.py:25
  34.3 6.9 %collective-permute-start.11 = (f32[256,256]{1,0:T(8,128)S(1)}, f32[256,256]{1,0:T(8,128)S(1)}, u32[]{:S(2)}, u32[]{:S(2)}) collective-permute-start(f32[256,256]{1,0:T(8,128)S(1)} %eliminate1.1.s_own), channel_id=1, source_target_pairs={{0,1},{1,0},{2,3},{3,2},{4,5},{5,4},{6,7},{7,6},{8,9},{9,8},{10,11... | collective-permute-start | bytes 786440 | tf_op jit(solution)/shard_map/ppermute | solution.py:25
  36.3 8.4 %collective-permute-start.15 = (f32[256,256]{1,0:T(8,128)S(1)}, f32[256,256]{1,0:T(8,128)S(1)}, u32[]{:S(2)}, u32[]{:S(2)}) collective-permute-start(f32[256,256]{1,0:T(8,128)S(1)} %eliminate2.1.s_own), channel_id=1, source_target_pairs={{0,1},{1,0},{2,3},{3,2},{4,5},{5,4},{6,7},{7,6},{8,9},{9,8},{10,11... | collective-permute-start | bytes 786440 | tf_op jit(solution)/shard_map/ppermute | solution.py:25
  40.6 6.2 %collective-permute-start.8 = (bf16[128,256]{1,0:T(8,128)(2,1)S(1)}, bf16[128,256]{1,0:T(8,128)(2,1)S(1)}, u32[]{:S(2)}, u32[]{:S(2)}) collective-permute-start(bf16[128,256]{1,0:T(8,128)(2,1)S(1)} %get-tuple-element.16), channel_id=1, source_target_pairs={{0,2},{2,0},{1,3},{3,1},{4,6},{6,4},{5,7},{7,5},{8,10},{10,8},{9,1... | collective-permute-start | bytes 196616 | tf_op jit(solution)/shard_map/ppermute | solution.py:29
  42.9 5.5 %collective-permute-start.12 = (bf16[128,256]{1,0:T(8,128)(2,1)S(1)}, bf16[128,256]{1,0:T(8,128)(2,1)S(1)}, u32[]{:S(2)}, u32[]{:S(2)}) collective-permute-start(bf16[128,256]{1,0:T(8,128)(2,1)S(1)} %get-tuple-element.18), channel_id=1, source_target_pairs={{0,2},{2,0},{1,3},{3,1},{4,6},{6,4},{5,7},{7,5},{8,10},{10,8},{9,1... | collective-permute-start | bytes 196616 | tf_op jit(solution)/shard_map/ppermute | solution.py:29
  46.5 4.4 %collective-permute-start.16 = (bf16[128,256]{1,0:T(8,128)(2,1)S(1)}, bf16[128,256]{1,0:T(8,128)(2,1)S(1)}, u32[]{:S(2)}, u32[]{:S(2)}) collective-permute-start(bf16[128,256]{1,0:T(8,128)(2,1)S(1)} %get-tuple-element.20), channel_id=1, source_target_pairs={{0,2},{2,0},{1,3},{3,1},{4,6},{6,4},{5,7},{7,5},{8,10},{10,8},{9,1... | collective-permute-start | bytes 196616 | tf_op jit(solution)/shard_map/ppermute | solution.py:29
  46.9 4.9 %collective-permute-start.17 = (f32[64,256]{1,0:T(8,128)S(1)}, f32[64,256]{1,0:T(8,128)S(1)}, u32[]{:S(2)}, u32[]{:S(2)}) collective-permute-start(f32[64,256]{1,0:T(8,128)S(1)} %get-tuple-element.33), channel_id=1, source_target_pairs={{0,16},{4,20},{8,24},{12,28},{16,0},{20,4},{24,8},{28,12},{32,48},... | collective-permute-start | bytes 196616 | tf_op jit(solution)/shard_map/ppermute | solution.py:33
  48.5 4.8 %collective-permute-start.18 = (f32[64,256]{1,0:T(8,128)S(1)}, f32[64,256]{1,0:T(8,128)S(1)}, u32[]{:S(2)}, u32[]{:S(2)}) collective-permute-start(f32[64,256]{1,0:T(8,128)S(1)} %get-tuple-element.35), channel_id=1, source_target_pairs={{0,16},{4,20},{8,24},{12,28},{16,0},{20,4},{24,8},{28,12},{32,48},... | collective-permute-start | bytes 196616 | tf_op jit(solution)/shard_map/ppermute | solution.py:33
  50.9 4.4 %collective-permute-start.19 = (f32[64,256]{1,0:T(8,128)S(1)}, f32[64,256]{1,0:T(8,128)S(1)}, u32[]{:S(2)}, u32[]{:S(2)}) collective-permute-start(f32[64,256]{1,0:T(8,128)S(1)} %get-tuple-element.37), channel_id=1, source_target_pairs={{0,16},{4,20},{8,24},{12,28},{16,0},{20,4},{24,8},{28,12},{32,48},... | collective-permute-start | bytes 196616 | tf_op jit(solution)/shard_map/ppermute | solution.py:33
  (2 other events, 10.4 us)

commit v2 on v0

v2 whole, which is shorter than its diff:
```python
import functools

import jax
import jax.numpy as jnp
from jax import lax
from jax.experimental import pallas as pl
from jax.experimental.pallas import tpu as pltpu
from jax.sharding import PartitionSpec as P

BIT = 2
F32 = jnp.float32
BF16 = jnp.bfloat16
F16 = jnp.float16
SCALE = 2.0**17
CORE = [(0, 1), (1, 0), (2, 3), (3, 2)]
CHIP = [(0, 2), (2, 0), (1, 3), (3, 1)]
VMEM = pl.BlockSpec(memory_space=pltpu.VMEM)
SMEM = pl.BlockSpec(memory_space=pltpu.SMEM)


def to_core(block):
    return lax.ppermute(block, "col", CORE)


def to_chip(block):
    return lax.ppermute(block, "col", CHIP)


def to_sibling(block):
    return lax.ppermute(block, "row", [(n, n ^ 1 << BIT) for n in range(lax.axis_size("row"))])


def after(block, *earlier):
    return lax.optimization_barrier((block, *earlier))[0]


def dot(a, b):
    return lax.dot_general(a, b, (((1,), (0,)), ((), ())), preferred_element_type=F32)


def band(index, size):
    return pl.ds(pl.multiple_of(index * size, size), size)


def split(x):
    high = x.astype(BF16)
    return high, (x - high.astype(F32)).astype(BF16)


def across(x):
    high, low = split(x)
    return jnp.concatenate([high, high, low], 1)


def down(x):
    high, low = split(x)
    return jnp.concatenate([high, low, high], 0)


def call(body, shapes, specs, flops, name, scratch=()):
    return pl.pallas_call(
        body,
        out_shape=shapes,
        in_specs=specs,
        out_specs=jax.tree.map(lambda _: VMEM, shapes),
        scratch_shapes=scratch,
        compiler_params=pltpu.CompilerParams(vmem_limit_bytes=8 << 20),
        cost_estimate=pl.CostEstimate(flops=1, bytes_accessed=1, transcendentals=0),
        name=name,
    )


def begin_kernel(d, own, core, right, e_out, rt_out):
    q = lax.axis_index("col")
    nodes, depth, _ = own.shape
    for n in range(nodes):
        e_out[n] = dot(d[n, :, band(q, depth)], own[n]) + dot(d[n, :, band(q ^ 1, depth)], core[n])
        rt_out[n] = right[n].T


def eliminate_kernel(n, e, d, chip, cross, rt, s_out):
    q = lax.axis_index("col")
    depth = chip.shape[0]
    elim = e[n] + dot(d[n, :, band(q ^ 2, depth)], chip[...]) + dot(d[n, :, band(q ^ 3, depth)], cross[...])
    s_out[...] = dot(rt[n], elim.astype(BF16))


def couple_kernel(blocks, c_own, c_core, m_out, mt_out, cm_out, m, sib, c_all):
    q = lax.axis_index("col")
    nodes, part, width = c_own.shape
    for n in range(nodes):
        for k in range(4):
            m[band(q ^ k, part), :] = blocks[k, 0, n]
            sib[band(q ^ k, part), :] = blocks[k, 1, n]
        c_all[band(q & 1, part), :] = c_own[n]
        c_all[band(1 - (q & 1), part), :] = c_core[n]
        cm_out[n] = dot(across(c_all[...]), down(sib[...]))
        m_out[n] = down(m[...])
        m[...] = m[...].T
        mt_out[n] = across(jnp.concatenate([m[band(q, part), :], m[band(q ^ 2, part), :]], 0))


def merge_kernel(n, ranks, s_own, s_core, m, mt, cm, own_out, send_out, t_all):
    q = lax.axis_index("col")
    rank = ranks[n]
    part = cm.shape[1] // 2
    width = m.shape[2]
    row = lax.broadcasted_iota(jnp.int32, (width, width), 0)
    col = lax.broadcasted_iota(jnp.int32, (width, width), 1)
    s = jnp.where((row < rank) & (col < rank), s_own[...] + s_core[...], 0.0)
    t_all[...] = dot(across(s), m[n])
    t_all[band(q >> 1, 2 * part), :] += cm[n]
    high, low = split(t_all[...])
    p = dot(mt[n], jnp.concatenate([high, low, high], 0))
    own_out[0] = t_all[band(q, part), :]
    own_out[1] = p[:part]
    send_out[0] = t_all[band(q ^ 2, part), :].astype(BF16)
    send_out[1] = p[part:].astype(BF16)


def shards(diagonal_inverses, column_basis, row_basis, transfer, coupling, ranks):
    nodes, part, width = transfer.shape
    depth = column_basis.shape[1]
    q = lax.axis_index("col").astype(jnp.int32)
    shape = jax.ShapeDtypeStruct

    first = column_basis[0]
    chip_left = [to_chip(first)]
    transfer, ranks_late = lax.optimization_barrier((transfer, ranks, first))[:2]
    rows = q * part + jnp.arange(part, dtype=jnp.int32)
    live = (rows[None, :] < ranks_late[:, None])[:, :, None]
    m_own = jnp.where(live, transfer * SCALE, 0.0).astype(F16)
    m_chip = to_chip(m_own)
    rest = after(column_basis, m_own)
    pieces = lax.optimization_barrier(tuple(rest[n] for n in range(1, nodes)))
    chip_left += [to_chip(piece) for piece in pieces]
    own_left = after(column_basis, *pieces)
    core_left = to_core(column_basis)
    c_core = to_core(coupling)

    e, rt = call(
        begin_kernel,
        [shape((nodes, depth, width), F32), shape((nodes, width, depth), BF16)],
        [VMEM] * 4,
        2 * nodes * depth * 2 * depth * width,
        "begin",
    )(diagonal_inverses, own_left, core_left, row_basis)
    left0, m_chip = lax.optimization_barrier((chip_left[0], m_chip, e))[:2]

    def eliminate(n, chip, cross):
        return call(
            functools.partial(eliminate_kernel, n),
            shape((width, width), F32),
            [VMEM] * 5,
            2 * depth * 2 * depth * width,
            f"eliminate{n}",
        )(e, diagonal_inverses, chip, cross, rt)

    def merge(n, s, s_core):
        return call(
            functools.partial(merge_kernel, n),
            [shape((2, part, width), F32), shape((2, part, width), BF16)],
            [SMEM] + [VMEM] * 5,
            12 * width**3,
            f"merge{n}",
            [pltpu.VMEM((width, width), F32)],
        )(ranks, s, s_core, m, mt, cm)

    s0 = eliminate(0, left0, to_core(left0))
    s0_core = to_core(s0)

    m_pair = jnp.stack([m_own, m_chip])
    m_sib = to_sibling(m_pair)
    m_mine = jnp.stack([m_pair, m_sib], 1)
    m_core = to_core(m_mine)

    left1 = after(chip_left[1], s0)
    s1 = eliminate(1, left1, to_core(left1))
    s1_core = to_core(s1)

    blocks = jnp.stack([m_mine[0], m_core[0], m_mine[1], m_core[1]]).astype(F32) * (1 / SCALE)
    m, mt, cm = call(
        couple_kernel,
        [
            shape((nodes, 3 * width, width), BF16),
            shape((nodes, 2 * part, 3 * width), BF16),
            shape((nodes, 2 * part, width), F32),
        ],
        [VMEM] * 3,
        6 * nodes * 2 * part * width * width,
        "couple",
        [pltpu.VMEM((width, width), F32), pltpu.VMEM((width, width), F32), pltpu.VMEM((2 * part, width), F32)],
    )(blocks, coupling, c_core)

    own0, send0 = merge(0, s0, s0_core)
    left2 = after(chip_left[2], own0)
    s1, s1_core = lax.optimization_barrier((s1, s1_core, left2))[:2]
    own1, send1 = merge(1, s1, s1_core)
    s2 = eliminate(2, left2, to_core(left2))
    got0 = to_chip(jnp.stack([send0, send1]))
    own2, send2 = merge(2, s2, to_core(s2))
    got2 = to_chip(send2)
    p01 = jnp.stack([own0[1], own1[1]]) + got0[:, 1].astype(F32)
    p01_sib = to_sibling(p01)
    p2 = own2[1] + got2[1].astype(F32)
    p2_sib = to_sibling(p2)
    merged = jnp.stack([own0[0], own1[0], own2[0]]) + jnp.concatenate([got0[:, 0], got2[:1]]).astype(F32)
    parent = jnp.concatenate([p01 + p01_sib, (p2 + p2_sib)[None]])
    return merged, parent


def solution(mesh):
    block = P("row", "col", None)
    return jax.shard_map(
        shards,
        mesh=mesh,
        in_specs=(block, block, block, block, block, P("row")),
        out_specs=(block, block),
        check_vma=False,
    )
```

time: 158 us -> 51 us (0.32)
  waiting for transfers between devices: 112 us -> 22.8 us
  between operations: 14.5 us -> 0.93 us
  matrix products: 10.1 us -> 0 us
  blocking collectives: 9.16 us -> 0 us
  starting transfers between devices: 3.56 us -> 11 us
  Pallas kernels: 0 us -> 7.2 us
    unnamed x4 -> x0, waiting for transfers between devices: 47.3 us -> none
    all_gather x1 -> x0, waiting for transfers between devices: 41.6 us -> none  [shards(): lax.all_gather(left_factor_basis, 'col', axis=1, tiled=True)]
    reduce_scatter x1 -> x0, waiting for transfers between devices: 11.8 us -> none  [shards(): lax.psum_scatter(jnp.einsum('hgp,hgd->phd', right_factor_basis, eliminate...]
    ppermute x2 -> x18, waiting for transfers between devices: 11.6 us -> 22.8 us  [the longest x6 14.1 us: to_chip(): return lax.ppermute(block, 'col', CHIP)]
    dot_general x4 -> x0, matrix products: 10.1 us -> none  [the longest x1 7.11 us: shards(): jnp.einsum('hgp,hgd->phd', right_factor_basis, eliminated_part, preferred...]
    all_gather x1 -> x0, blocking collectives: 9.16 us -> none  [shards(): complete_local_block = lax.all_gather(masked, 'col', axis=1, tiled=True)]
    ppermute x2 -> x18, starting transfers between devices: 3.44 us -> 11 us  [the longest x6 5.88 us: to_chip(): return lax.ppermute(block, 'col', CHIP)]
    pallas_call x0 -> x8, Pallas kernels: none -> 7.2 us  [the longest x3 3.45 us: merge(): call(functools.partial(merge_kernel, n), [shape((2, part, width), F32), s...]
  transfers between devices with their start and end apart: 5 -> 18, of which waited for: 5 -> 9; matrix products, arithmetic and copies ran while one was open for 1% -> 10% of each run, Pallas kernels for 0% -> 14%
where the time goes in v2:
time: 51 us; the launch traced here: 50.8 us
  waiting for transfers between devices  22.8 us (45%)
  starting transfers between devices  11 us (22%)
  Pallas kernels  7.2 us (14%)
  local copies, waits for them, and re-layouts  5.06 us (10%)
  other arithmetic  3.79 us (7%)
  between operations  0.93 us (2%)
    ppermute x6, waiting for transfers between devices, to_chip(): return lax.ppermute(block, 'col', CHIP)  14.1 us
    ppermute x3, waiting for transfers between devices, to_sibling(): lax.ppermute(block, 'row', [(n, n ^ 1 << BIT) for n in range(lax.axis_siz...  8.33 us
    ppermute x6, starting transfers between devices, to_chip(): return lax.ppermute(block, 'col', CHIP)  5.88 us
    ppermute x3, starting transfers between devices, to_sibling(): lax.ppermute(block, 'row', [(n, n ^ 1 << BIT) for n in range(lax.axis_siz...  3.76 us
    pallas_call x3, Pallas kernels, merge(): call(functools.partial(merge_kernel, n), [shape((2, part, width), F32), s...  3.45 us
    unnamed x14, local copies, waits for them, and re-layouts  2.81 us
    pallas_call x3, Pallas kernels, eliminate(): call(functools.partial(eliminate_kernel, n), shape((width, width), F32),...  2.03 us
    ppermute x9, starting transfers between devices, to_core(): return lax.ppermute(block, 'col', CORE)  1.34 us
  transfers between devices with their start and end apart: 18, of which 9 were waited for; matrix products, arithmetic and copies ran while one was open for 10% of the time, Pallas kernels for 14%

profile of v2, /device:TPU:8, one launch (start us, length us, event | category | flops | bytes accessed | tf_op | source)
XLA Modules:
  0.0 50.8 jit_solution(2809873572018399563)
XLA Ops:
  0.8 1.1 %slice_bitcast_fusion.2 = bf16[512,256]{1,0:T(8,128)(2,1)S(1)} fusion(bf16[3,512,256]{2,1,0:T(8,128)(2,1)} %own), kind=kLoop, calls=%fused_computation.8 | loop fusion | bytes 524288 | tf_op jit(solution)/shard_map/squeeze | solution.py:127
  1.8 2.3 %collective-permute-start.1 = (bf16[512,256]{1,0:T(8,128)(2,1)S(1)}, bf16[512,256]{1,0:T(8,128)(2,1)S(1)}, u32[]{:S(2)}, u32[]{:S(2)}) collective-permute-start(bf16[512,256]{1,0:T(8,128)(2,1)S(1)} %slice_bitcast_fusion.2), channel_id=1, source_target_pairs={{0,2},{2,0},{1,3},{3,1},{4,6},{6,4},{5,7},{7,5},{8,10},{10,8},{9,1... | collective-permute-start | bytes 786440 | tf_op jit(solution)/shard_map/ppermute | solution.py:26
  4.1 0.7 %broadcast_compare_fusion = pred[3,64]{1,0:T(4,128)(4,1)S(1)} fusion(s32[64]{0:T(128)S(1)} %iota_add_fusion, s32[3]{0:T(128)} %ranks.5), kind=kLoop, calls=%fused_computation.21 | loop fusion | flops 192 | bytes 460 | tf_op jit(solution)/shard_map/lt | solution.py:131
  4.9 1.0 %select_convert_fusion = f16[3,64,256]{2,1,0:T(8,128)(2,1)S(1)} fusion(f32[3,64,256]{2,1,0:T(8,128)} %param.9, pred[3,64]{1,0:T(4,128)(4,1)S(1)} %broadcast_compare_fusion), kind=kLoop, calls=%fused_computation.14 | loop fusion | flops 147456 | bytes 295104 | tf_op jit(solution)/shard_map/convert_element_type | solution.py:132
  6.0 1.1 %slice_bitcast_fusion = (bf16[512,256]{1,0:T(8,128)(2,1)S(1)}, bf16[512,256]{1,0:T(8,128)(2,1)S(1)}) fusion(bf16[3,512,256]{2,1,0:T(8,128)(2,1)} %own), kind=kLoop, calls=%fused_computation.6 | loop fusion | bytes 1048576 | tf_op jit(solution)/shard_map/squeeze | solution.py:135
  7.2 2.8 %copy-done = bf16[3,512,2048]{2,1,0:T(8,128)(2,1)S(1)} copy-done((bf16[3,512,2048]{2,1,0:T(8,128)(2,1)S(1)}, bf16[3,512,2048]{2,1,0:T(8,128)(2,1)}, u32[]{:S(2)}) %copy-start) | copy-done | bytes 6291480
  10.0 1.0 %begin.1 = (f32[3,512,256]{2,1,0:T(8,128)S(1)}, bf16[3,256,512]{2,1,0:T(8,128)(2,1)S(1)}) custom-call(bf16[3,512,2048]{2,1,0:T(8,128)(2,1)S(1)} %copy-done, bf16[3,512,256]{2,1,0:T(8,128)(2,1)S(1)} %copy-done.2, bf16[3,512,256]{2,1,0:T(8,128)(2,1)S(1)} %collective-permute-done.core, bf16[3,512,256]{2,1,0:T(8,128)(2,1)S(1)} %copy-done.3), custom_call_target="tpu_custom_call" | custom-call | flops 1 | bytes 1 | tf_op jit(solution)/shard_map/begin/pallas_call | solution.py:141
  11.0 2.1 %collective-permute-done.2 = f16[3,64,256]{2,1,0:T(8,128)(2,1)S(1)} collective-permute-done((f16[3,64,256]{2,1,0:T(8,128)(2,1)S(1)}, f16[3,64,256]{2,1,0:T(8,128)(2,1)S(1)}, u32[]{:S(2)}, u32[]{:S(2)}) %collective-permute-start.2) | collective-permute-done | bytes 98336 | tf_op jit(solution)/shard_map/ppermute | solution.py:26
  13.1 1.6 %collective-permute-start.5 = (f16[2,3,64,256]{3,2,1,0:T(8,128)(2,1)S(1)}, f16[2,3,64,256]{3,2,1,0:T(8,128)(2,1)S(1)}, u32[]{:S(2)}, u32[]{:S(2)}) collective-permute-start(f16[2,3,64,256]{3,2,1,0:T(8,128)(2,1)S(1)} %get-tuple-element.55), channel_id=1, source_target_pairs={{0,16},{4,20},{8,24},{12,28},{16,0},{20,4},{24,8},{28,12},{32,48},... | collective-permute-start | bytes 589832 | tf_op jit(solution)/shard_map/ppermute | solution.py:30
  15.2 4.7 %collective-permute-done.5 = f16[2,3,64,256]{3,2,1,0:T(8,128)(2,1)S(1)} collective-permute-done((f16[2,3,64,256]{3,2,1,0:T(8,128)(2,1)S(1)}, f16[2,3,64,256]{3,2,1,0:T(8,128)(2,1)S(1)}, u32[]{:S(2)}, u32[]{:S(2)}) %collective-permute-start.5) | collective-permute-done | bytes 196640 | tf_op jit(solution)/shard_map/ppermute | solution.py:30
  20.8 2.7 %collective-permute-done.8.chip = bf16[512,256]{1,0:T(8,128)(2,1)S(1)} collective-permute-done((bf16[512,256]{1,0:T(8,128)(2,1)S(1)}, bf16[512,256]{1,0:T(8,128)(2,1)S(1)}, u32[]{:S(2)}, u32[]{:S(2)}) %collective-permute-start.8) | collective-permute-done | bytes 262176 | tf_op jit(solution)/shard_map/ppermute | solution.py:26
  26.2 0.7 %couple.1 = (bf16[3,768,256]{2,1,0:T(8,128)(2,1)S(1)}, bf16[3,128,768]{2,1,0:T(8,128)(2,1)S(1)}, f32[3,128,256]{2,1,0:T(8,128)S(1)}) custom-call(f32[4,2,3,64,256]{4,3,2,1,0:T(8,128)S(1)} %convert_multiply_fusion.blocks, f32[3,64,256]{2,1,0:T(8,128)S(1)} %copy-done.4, f32[3,64,256]{2,1,0:T(8,128)S(1)} %collective-permute-done.7.c_core), custom_call_target="tpu_custom_call" | custom-call | flops 1 | bytes 1 | tf_op jit(solution)/shard_map/couple/pallas_call | solution.py:182
  27.0 1.2 %merge0.1 = (f32[2,64,256]{2,1,0:T(8,128)S(1)}, bf16[2,64,256]{2,1,0:T(8,128)(2,1)S(1)}) custom-call(s32[3]{0:T(128)S(1)} %copy-done.5, f32[256,256]{1,0:T(8,128)S(1)} %eliminate0.1.s_own, f32[256,256]{1,0:T(8,128)S(1)} %collective-permute-done.4.s_core, bf16[3,768,256]{2,1,0:T(8,128)(2,1)S(1)} %get-tuple-element.35.m, ...), custom_call_target="tpu_custom_call" | custom-call | flops 1 | bytes 1 | tf_op jit(solution)/shard_map/merge0/pallas_call | solution.py:160
  28.1 4.0 %collective-permute-done.11.chip = bf16[512,256]{1,0:T(8,128)(2,1)S(1)} collective-permute-done((bf16[512,256]{1,0:T(8,128)(2,1)S(1)}, bf16[512,256]{1,0:T(8,128)(2,1)S(1)}, u32[]{:S(2)}, u32[]{:S(2)}) %collective-permute-start.11) | collective-permute-done | bytes 262176 | tf_op jit(solution)/shard_map/ppermute | solution.py:26
  32.2 1.1 %merge1.1 = (f32[2,64,256]{2,1,0:T(8,128)S(1)}, bf16[2,64,256]{2,1,0:T(8,128)(2,1)S(1)}) custom-call(s32[3]{0:T(128)S(1)} %copy-done.5, f32[256,256]{1,0:T(8,128)S(1)} %eliminate1.1.s_own, f32[256,256]{1,0:T(8,128)S(1)} %collective-permute-done.10.s_core, bf16[3,768,256]{2,1,0:T(8,128)(2,1)S(1)} %get-tuple-element.35.m, ...), custom_call_target="tpu_custom_call" | custom-call | flops 1 | bytes 1 | tf_op jit(solution)/shard_map/merge1/pallas_call | solution.py:160
  33.3 0.7 %collective-permute-start.14 = (bf16[2,2,64,256]{3,2,0,1:T(8,128)(2,1)S(1)}, bf16[2,2,64,256]{3,2,0,1:T(8,128)(2,1)S(1)}, u32[]{:S(2)}, u32[]{:S(2)}) collective-permute-start(bf16[2,2,64,256]{3,2,0,1:T(8,128)(2,1)S(1)} %pad_maximum_fusion.3), channel_id=1, source_target_pairs={{0,2},{2,0},{1,3},{3,1},{4,6},{6,4},{5,7},{7,5},{8,10},{10,8},{9,1... | collective-permute-start | bytes 393224 | tf_op jit(solution)/shard_map/ppermute | solution.py:26
  35.1 4.4 %collective-permute-done.14 = bf16[2,2,64,256]{3,2,0,1:T(8,128)(2,1)S(1)} collective-permute-done((bf16[2,2,64,256]{3,2,0,1:T(8,128)(2,1)S(1)}, bf16[2,2,64,256]{3,2,0,1:T(8,128)(2,1)S(1)}, u32[]{:S(2)}, u32[]{:S(2)}) %collective-permute-start.14) | collective-permute-done | bytes 131104 | tf_op jit(solution)/shard_map/ppermute | solution.py:26
  40.2 1.2 %merge2.1 = (f32[2,64,256]{2,1,0:T(8,128)S(1)}, bf16[2,64,256]{2,1,0:T(8,128)(2,1)S(1)}) custom-call(s32[3]{0:T(128)S(1)} %copy-done.5, f32[256,256]{1,0:T(8,128)S(1)} %eliminate2.1.s_own, f32[256,256]{1,0:T(8,128)S(1)} %collective-permute-done.13.s_core, bf16[3,768,256]{2,1,0:T(8,128)(2,1)S(1)} %get-tuple-element.35.m, ...), custom_call_target="tpu_custom_call" | custom-call | flops 1 | bytes 1 | tf_op jit(solution)/shard_map/merge2/pallas_call | solution.py:160
  41.3 1.8 %collective-permute-start.15 = (bf16[2,64,256]{2,1,0:T(8,128)(2,1)S(1)}, bf16[2,64,256]{2,1,0:T(8,128)(2,1)S(1)}, u32[]{:S(2)}, u32[]{:S(2)}) collective-permute-start(bf16[2,64,256]{2,1,0:T(8,128)(2,1)S(1)} %get-tuple-element.47), channel_id=1, source_target_pairs={{0,2},{2,0},{1,3},{3,1},{4,6},{6,4},{5,7},{7,5},{8,10},{10,8},{9,1... | collective-permute-start | bytes 196616 | tf_op jit(solution)/shard_map/ppermute | solution.py:26
  43.2 1.6 %collective-permute-done.16 = f32[2,64,256]{2,1,0:T(8,128)S(1)} collective-permute-done((f32[2,64,256]{2,1,0:T(8,128)S(1)}, f32[2,64,256]{2,1,0:T(8,128)S(1)}, u32[]{:S(2)}, u32[]{:S(2)}) %collective-permute-start.16) | collective-permute-done | bytes 131104 | tf_op jit(solution)/shard_map/ppermute | solution.py:30
  44.8 0.9 %collective-permute-done.15 = bf16[2,64,256]{2,1,0:T(8,128)(2,1)S(1)} collective-permute-done((bf16[2,64,256]{2,1,0:T(8,128)(2,1)S(1)}, bf16[2,64,256]{2,1,0:T(8,128)(2,1)S(1)}, u32[]{:S(2)}, u32[]{:S(2)}) %collective-permute-start.15) | collective-permute-done | bytes 65568 | tf_op jit(solution)/shard_map/ppermute | solution.py:26
  45.7 1.6 %collective-permute-start.17 = (f32[64,256]{1,0:T(8,128)S(1)}, f32[64,256]{1,0:T(8,128)S(1)}, u32[]{:S(2)}, u32[]{:S(2)}) collective-permute-start(f32[64,256]{1,0:T(8,128)S(1)} %get-tuple-element.60), channel_id=1, source_target_pairs={{0,16},{4,20},{8,24},{12,28},{16,0},{20,4},{24,8},{28,12},{32,48},... | collective-permute-start | bytes 196616 | tf_op jit(solution)/shard_map/ppermute | solution.py:30
  47.3 0.7 %maximum_add_fusion = f32[3,64,256]{2,1,0:T(8,128)} fusion(f32[1,64,256]{2,1,0:T(8,128)S(1)} %get-tuple-element.61, f32[1,64,256]{2,1,0:T(8,128)S(1)} %get-tuple-element.62, f32[1,64,256]{2,1,0:T(8,128)S(1)} %get-tuple-element.57, bf16[1,64,256]{2,1,0:T(8,128)(2,1)S(1)} %slice.75, bf16[2,64,256]{2,1,0:T(8,128)(2,1)S(1)} %slice_bitcast_fusion.4), kind=kLoop, calls=%fused_computation.12 | loop fusion | flops 245760 | bytes 491520 | tf_op jit(solution)/shard_map/add | solution.py:207
  48.0 2.1 %collective-permute-done.17 = f32[64,256]{1,0:T(8,128)S(1)} collective-permute-done((f32[64,256]{1,0:T(8,128)S(1)}, f32[64,256]{1,0:T(8,128)S(1)}, u32[]{:S(2)}, u32[]{:S(2)}) %collective-permute-start.17) | collective-permute-done | bytes 65568 | tf_op jit(solution)/shard_map/ppermute | solution.py:30
  (55 shorter events, 7.0 us)
Async XLA Ops:
  0.6 6.6 %copy-start.2 = (bf16[3,512,256]{2,1,0:T(8,128)(2,1)S(1)}, bf16[3,512,256]{2,1,0:T(8,128)(2,1)}, u32[]{:S(2)}) copy-start(bf16[3,512,256]{2,1,0:T(8,128)(2,1)} %own) | copy-start | bytes 2359300
  0.6 6.4 %copy-start.6 = (f32[3,64,256]{2,1,0:T(8,128)S(1)}, f32[3,64,256]{2,1,0:T(8,128)}, u32[]{:S(2)}) copy-start(f32[3,64,256]{2,1,0:T(8,128)} %param.9) | copy-start | bytes 589828
  0.7 6.6 %copy-start.3 = (bf16[3,512,256]{2,1,0:T(8,128)(2,1)S(1)}, bf16[3,512,256]{2,1,0:T(8,128)(2,1)}, u32[]{:S(2)}) copy-start(bf16[3,512,256]{2,1,0:T(8,128)(2,1)} %right.1) | copy-start | bytes 2359300
  0.7 6.5 %collective-permute-start = (bf16[3,512,256]{2,1,0:T(8,128)(2,1)}, bf16[3,512,256]{2,1,0:T(8,128)(2,1)S(1)}, u32[]{:S(2)}, u32[]{:S(2)}) collective-permute-start(bf16[3,512,256]{2,1,0:T(8,128)(2,1)} %own), channel_id=1, source_target_pairs={{0,1},{1,0},{2,3},{3,2},{4,5},{5,4},{6,7},{7,6},{8,9},{9,8},{10,11... | collective-permute-start | bytes 2359304 | tf_op jit(solution)/shard_map/ppermute | solution.py:22
  1.8 11.2 %collective-permute-start.1 = (bf16[512,256]{1,0:T(8,128)(2,1)S(1)}, bf16[512,256]{1,0:T(8,128)(2,1)S(1)}, u32[]{:S(2)}, u32[]{:S(2)}) collective-permute-start(bf16[512,256]{1,0:T(8,128)(2,1)S(1)} %slice_bitcast_fusion.2), channel_id=1, source_target_pairs={{0,2},{2,0},{1,3},{3,1},{4,6},{6,4},{5,7},{7,5},{8,10},{10,8},{9,1... | collective-permute-start | bytes 786440 | tf_op jit(solution)/shard_map/ppermute | solution.py:26
  5.9 7.2 %collective-permute-start.2 = (f16[3,64,256]{2,1,0:T(8,128)(2,1)S(1)}, f16[3,64,256]{2,1,0:T(8,128)(2,1)S(1)}, u32[]{:S(2)}, u32[]{:S(2)}) collective-permute-start(f16[3,64,256]{2,1,0:T(8,128)(2,1)S(1)} %select_convert_fusion), channel_id=1, source_target_pairs={{0,2},{2,0},{1,3},{3,1},{4,6},{6,4},{5,7},{7,5},{8,10},{10,8},{9,1... | collective-permute-start | bytes 294920 | tf_op jit(solution)/shard_map/ppermute | solution.py:26
  7.2 2.8 %copy-start = (bf16[3,512,2048]{2,1,0:T(8,128)(2,1)S(1)}, bf16[3,512,2048]{2,1,0:T(8,128)(2,1)}, u32[]{:S(2)}) copy-start(bf16[3,512,2048]{2,1,0:T(8,128)(2,1)} %d.7) | copy-start | bytes 18874372
  10.0 10.0 %copy-start.1 = (bf16[3,512,2048]{2,1,0:T(8,128)(2,1)S(1)}, bf16[3,512,2048]{2,1,0:T(8,128)(2,1)}, u32[]{:S(2)}) copy-start(bf16[3,512,2048]{2,1,0:T(8,128)(2,1)} %d.7) | copy-start | bytes 18874372
  13.1 6.7 %collective-permute-start.5 = (f16[2,3,64,256]{3,2,1,0:T(8,128)(2,1)S(1)}, f16[2,3,64,256]{3,2,1,0:T(8,128)(2,1)S(1)}, u32[]{:S(2)}, u32[]{:S(2)}) collective-permute-start(f16[2,3,64,256]{3,2,1,0:T(8,128)(2,1)S(1)} %get-tuple-element.55), channel_id=1, source_target_pairs={{0,16},{4,20},{8,24},{12,28},{16,0},{20,4},{24,8},{28,12},{32,48},... | collective-permute-start | bytes 589832 | tf_op jit(solution)/shard_map/ppermute | solution.py:30
  14.7 5.3 %collective-permute-start.3 = (bf16[512,256]{1,0:T(8,128)(2,1)S(1)}, bf16[512,256]{1,0:T(8,128)(2,1)S(1)}, u32[]{:S(2)}, u32[]{:S(2)}) collective-permute-start(bf16[512,256]{1,0:T(8,128)(2,1)S(1)} %collective-permute-done.1.chip), channel_id=1, source_target_pairs={{0,1},{1,0},{2,3},{3,2},{4,5},{5,4},{6,7},{7,6},{8,9},{9,8},{10,11... | collective-permute-start | bytes 786440 | tf_op jit(solution)/shard_map/ppermute | solution.py:22
  14.7 8.7 %collective-permute-start.8 = (bf16[512,256]{1,0:T(8,128)(2,1)S(1)}, bf16[512,256]{1,0:T(8,128)(2,1)S(1)}, u32[]{:S(2)}, u32[]{:S(2)}) collective-permute-start(bf16[512,256]{1,0:T(8,128)(2,1)S(1)} %get-tuple-element.28), channel_id=1, source_target_pairs={{0,2},{2,0},{1,3},{3,1},{4,6},{6,4},{5,7},{7,5},{8,10},{10,8},{9,1... | collective-permute-start | bytes 786440 | tf_op jit(solution)/shard_map/ppermute | solution.py:26
  19.9 5.9 %collective-permute-start.6 = (f16[2,2,3,64,256]{4,3,2,1,0:T(8,128)(2,1)S(1)}, f16[2,2,3,64,256]{4,3,2,1,0:T(8,128)(2,1)S(1)}, u32[]{:S(2)}, u32[]{:S(2)}) collective-permute-start(f16[2,2,3,64,256]{4,3,2,1,0:T(8,128)(2,1)S(1)} %pad_maximum_fusion), channel_id=1, source_target_pairs={{0,1},{1,0},{2,3},{3,2},{4,5},{5,4},{6,7},{7,6},{8,9},{9,8},{10,11... | collective-permute-start | bytes 1179656 | tf_op jit(solution)/shard_map/ppermute | solution.py:22
  20.1 3.8 %copy-start.4 = (f32[3,64,256]{2,1,0:T(8,128)S(1)}, f32[3,64,256]{2,1,0:T(8,128)}, u32[]{:S(2)}) copy-start(f32[3,64,256]{2,1,0:T(8,128)} %c_own.1) | copy-start | bytes 589828
  23.4 1.5 %collective-permute-start.9 = (bf16[512,256]{1,0:T(8,128)(2,1)S(1)}, bf16[512,256]{1,0:T(8,128)(2,1)S(1)}, u32[]{:S(2)}, u32[]{:S(2)}) collective-permute-start(bf16[512,256]{1,0:T(8,128)(2,1)S(1)} %collective-permute-done.8.chip), channel_id=1, source_target_pairs={{0,1},{1,0},{2,3},{3,2},{4,5},{5,4},{6,7},{7,6},{8,9},{9,8},{10,11... | collective-permute-start | bytes 786440 | tf_op jit(solution)/shard_map/ppermute | solution.py:22
  23.4 8.7 %collective-permute-start.11 = (bf16[512,256]{1,0:T(8,128)(2,1)S(1)}, bf16[512,256]{1,0:T(8,128)(2,1)S(1)}, u32[]{:S(2)}, u32[]{:S(2)}) collective-permute-start(bf16[512,256]{1,0:T(8,128)(2,1)S(1)} %get-tuple-element.29), channel_id=1, source_target_pairs={{0,2},{2,0},{1,3},{3,1},{4,6},{6,4},{5,7},{7,5},{8,10},{10,8},{9,1... | collective-permute-start | bytes 786440 | tf_op jit(solution)/shard_map/ppermute | solution.py:26
  23.9 2.4 %collective-permute-start.7 = (f32[3,64,256]{2,1,0:T(8,128)S(1)}, f32[3,64,256]{2,1,0:T(8,128)S(1)}, u32[]{:S(2)}, u32[]{:S(2)}) collective-permute-start(f32[3,64,256]{2,1,0:T(8,128)S(1)} %copy-done.4), channel_id=1, source_target_pairs={{0,1},{1,0},{2,3},{3,2},{4,5},{5,4},{6,7},{7,6},{8,9},{9,8},{10,11... | collective-permute-start | bytes 589832 | tf_op jit(solution)/shard_map/ppermute | solution.py:22
  24.2 2.8 %collective-permute-start.4 = (f32[256,256]{1,0:T(8,128)S(1)}, f32[256,256]{1,0:T(8,128)S(1)}, u32[]{:S(2)}, u32[]{:S(2)}) collective-permute-start(f32[256,256]{1,0:T(8,128)S(1)} %eliminate0.1.s_own), channel_id=1, source_target_pairs={{0,1},{1,0},{2,3},{3,2},{4,5},{5,4},{6,7},{7,6},{8,9},{9,8},{10,11... | collective-permute-start | bytes 786440 | tf_op jit(solution)/shard_map/ppermute | solution.py:22
  25.6 6.5 %collective-permute-start.10 = (f32[256,256]{1,0:T(8,128)S(1)}, f32[256,256]{1,0:T(8,128)S(1)}, u32[]{:S(2)}, u32[]{:S(2)}) collective-permute-start(f32[256,256]{1,0:T(8,128)S(1)} %eliminate1.1.s_own), channel_id=1, source_target_pairs={{0,1},{1,0},{2,3},{3,2},{4,5},{5,4},{6,7},{7,6},{8,9},{9,8},{10,11... | collective-permute-start | bytes 786440 | tf_op jit(solution)/shard_map/ppermute | solution.py:22
  32.1 1.9 %collective-permute-start.12 = (bf16[512,256]{1,0:T(8,128)(2,1)S(1)}, bf16[512,256]{1,0:T(8,128)(2,1)S(1)}, u32[]{:S(2)}, u32[]{:S(2)}) collective-permute-start(bf16[512,256]{1,0:T(8,128)(2,1)S(1)} %collective-permute-done.11.chip), channel_id=1, source_target_pairs={{0,1},{1,0},{2,3},{3,2},{4,5},{5,4},{6,7},{7,6},{8,9},{9,8},{10,11... | collective-permute-start | bytes 786440 | tf_op jit(solution)/shard_map/ppermute | solution.py:22
  33.3 6.2 %collective-permute-start.14 = (bf16[2,2,64,256]{3,2,0,1:T(8,128)(2,1)S(1)}, bf16[2,2,64,256]{3,2,0,1:T(8,128)(2,1)S(1)}, u32[]{:S(2)}, u32[]{:S(2)}) collective-permute-start(bf16[2,2,64,256]{3,2,0,1:T(8,128)(2,1)S(1)} %pad_maximum_fusion.3), channel_id=1, source_target_pairs={{0,2},{2,0},{1,3},{3,1},{4,6},{6,4},{5,7},{7,5},{8,10},{10,8},{9,1... | collective-permute-start | bytes 393224 | tf_op jit(solution)/shard_map/ppermute | solution.py:26
  34.8 5.4 %collective-permute-start.13 = (f32[256,256]{1,0:T(8,128)S(1)}, f32[256,256]{1,0:T(8,128)S(1)}, u32[]{:S(2)}, u32[]{:S(2)}) collective-permute-start(f32[256,256]{1,0:T(8,128)S(1)} %eliminate2.1.s_own), channel_id=1, source_target_pairs={{0,1},{1,0},{2,3},{3,2},{4,5},{5,4},{6,7},{7,6},{8,9},{9,8},{10,11... | collective-permute-start | bytes 786440 | tf_op jit(solution)/shard_map/ppermute | solution.py:22
  39.5 5.2 %collective-permute-start.16 = (f32[2,64,256]{2,1,0:T(8,128)S(1)}, f32[2,64,256]{2,1,0:T(8,128)S(1)}, u32[]{:S(2)}, u32[]{:S(2)}) collective-permute-start(f32[2,64,256]{2,1,0:T(8,128)S(1)} %maximum_add_fusion.1), channel_id=1, source_target_pairs={{0,16},{4,20},{8,24},{12,28},{16,0},{20,4},{24,8},{28,12},{32,48},... | collective-permute-start | bytes 393224 | tf_op jit(solution)/shard_map/ppermute | solution.py:30
  41.3 4.4 %collective-permute-start.15 = (bf16[2,64,256]{2,1,0:T(8,128)(2,1)S(1)}, bf16[2,64,256]{2,1,0:T(8,128)(2,1)S(1)}, u32[]{:S(2)}, u32[]{:S(2)}) collective-permute-start(bf16[2,64,256]{2,1,0:T(8,128)(2,1)S(1)} %get-tuple-element.47), channel_id=1, source_target_pairs={{0,2},{2,0},{1,3},{3,1},{4,6},{6,4},{5,7},{7,5},{8,10},{10,8},{9,1... | collective-permute-start | bytes 196616 | tf_op jit(solution)/shard_map/ppermute | solution.py:26
  45.7 4.4 %collective-permute-start.17 = (f32[64,256]{1,0:T(8,128)S(1)}, f32[64,256]{1,0:T(8,128)S(1)}, u32[]{:S(2)}, u32[]{:S(2)}) collective-permute-start(f32[64,256]{1,0:T(8,128)S(1)} %get-tuple-element.60), channel_id=1, source_target_pairs={{0,16},{4,20},{8,24},{12,28},{16,0},{20,4},{24,8},{28,12},{32,48},... | collective-permute-start | bytes 196616 | tf_op jit(solution)/shard_map/ppermute | solution.py:30
  (1 other events, 0.8 us)

commit v3 on v2

--- a/solution.py
+++ b/solution.py
@@ -78,10 +78,11 @@
         rt_out[n] = right[n].T
 
 
-def eliminate_kernel(n, e, d, chip, cross, rt, s_out):
+def eliminate_kernel(n, e, d, chip, cross_a, cross_b, rt, s_out):
     q = lax.axis_index("col")
     depth = chip.shape[0]
-    elim = e[n] + dot(d[n, :, band(q ^ 2, depth)], chip[...]) + dot(d[n, :, band(q ^ 3, depth)], cross[...])
+    cross = jnp.concatenate([cross_a[...], cross_b[...]], 0)
+    elim = e[n] + dot(d[n, :, band(q ^ 2, depth)], chip[...]) + dot(d[n, :, band(q ^ 3, depth)], cross)
     s_out[...] = dot(rt[n], elim.astype(BF16))
 
 
@@ -131,10 +132,7 @@
     live = (rows[None, :] < ranks_late[:, None])[:, :, None]
     m_own = jnp.where(live, transfer * SCALE, 0.0).astype(F16)
     m_chip = to_chip(m_own)
-    rest = after(column_basis, m_own)
-    pieces = lax.optimization_barrier(tuple(rest[n] for n in range(1, nodes)))
-    chip_left += [to_chip(piece) for piece in pieces]
-    own_left = after(column_basis, *pieces)
+    chip_left.append(to_chip(after(column_basis, m_own)[1]))
     core_left = to_core(column_basis)
     c_core = to_core(coupling)
 
@@ -144,17 +142,22 @@
         [VMEM] * 4,
         2 * nodes * depth * 2 * depth * width,
         "begin",
-    )(diagonal_inverses, own_left, core_left, row_basis)
-    left0, m_chip = lax.optimization_barrier((chip_left[0], m_chip, e))[:2]
-
-    def eliminate(n, chip, cross):
+    )(diagonal_inverses, column_basis, core_left, row_basis)
+    chip_left[0], m_chip, last = lax.optimization_barrier((chip_left[0], m_chip, column_basis, e))[:3]
+    chip_left.append(to_chip(last[2]))
+
+    def cross(left):
+        half = depth // 2
+        return to_core(left[:half]), to_core(left[half:])
+
+    def eliminate(n, chip):
         return call(
             functools.partial(eliminate_kernel, n),
             shape((width, width), F32),
-            [VMEM] * 5,
+            [VMEM] * 6,
             2 * depth * 2 * depth * width,
             f"eliminate{n}",
-        )(e, diagonal_inverses, chip, cross, rt)
+        )(e, diagonal_inverses, chip, *cross(chip), rt)
 
     def merge(n, s, s_core):
         return call(
@@ -166,19 +169,13 @@
             [pltpu.VMEM((width, width), F32)],
         )(ranks, s, s_core, m, mt, cm)
 
-    s0 = eliminate(0, left0, to_core(left0))
-    s0_core = to_core(s0)
-
-    m_pair = jnp.stack([m_own, m_chip])
-    m_sib = to_sibling(m_pair)
-    m_mine = jnp.stack([m_pair, m_sib], 1)
-    m_core = to_core(m_mine)
-
-    left1 = after(chip_left[1], s0)
-    s1 = eliminate(1, left1, to_core(left1))
-    s1_core = to_core(s1)
-
-    blocks = jnp.stack([m_mine[0], m_core[0], m_mine[1], m_core[1]]).astype(F32) * (1 / SCALE)
+    s0 = eliminate(0, chip_left[0])
+    s1 = eliminate(1, after(chip_left[1], s0))
+    s0_core, s1_core = to_core(s0), to_core(s1)
+
+    sib_own, sib_chip = to_sibling(m_own), to_sibling(m_chip)
+    pieces = [m_own, sib_own, to_core(m_own), to_core(sib_own), m_chip, sib_chip, to_core(m_chip), to_core(sib_chip)]
+    blocks = (jnp.stack(pieces).astype(F32) * (1 / SCALE)).reshape((4, 2) + m_own.shape)
     m, mt, cm = call(
         couple_kernel,
         [
@@ -192,14 +189,14 @@
         [pltpu.VMEM((width, width), F32), pltpu.VMEM((width, width), F32), pltpu.VMEM((2 * part, width), F32)],
     )(blocks, coupling, c_core)
 
+    left2 = after(chip_left[2], s0, s1)
+    s2 = eliminate(2, left2)
     own0, send0 = merge(0, s0, s0_core)
-    left2 = after(chip_left[2], own0)
-    s1, s1_core = lax.optimization_barrier((s1, s1_core, left2))[:2]
     own1, send1 = merge(1, s1, s1_core)
-    s2 = eliminate(2, left2, to_core(left2))
     got0 = to_chip(jnp.stack([send0, send1]))
     own2, send2 = merge(2, s2, to_core(s2))
     got2 = to_chip(send2)
+    got0 = after(got0, own2)
     p01 = jnp.stack([own0[1], own1[1]]) + got0[:, 1].astype(F32)
     p01_sib = to_sibling(p01)
     p2 = own2[1] + got2[1].astype(F32)

time: 51 us -> 47.1 us (0.924)
  waiting for transfers between devices: 22.8 us -> 14.8 us
  starting transfers between devices: 11 us -> 15.5 us
    ppermute x6, waiting for transfers between devices: 14.1 us -> 3.55 us  [to_chip(): return lax.ppermute(block, 'col', CHIP)]
    ppermute x9 -> x15, waiting for transfers between devices: 0.4 us -> 3.19 us  [to_core(): return lax.ppermute(block, 'col', CORE)]
    ppermute x9 -> x15, starting transfers between devices: 1.34 us -> 4.02 us  [to_core(): return lax.ppermute(block, 'col', CORE)]
    ppermute x6, starting transfers between devices: 5.88 us -> 7.84 us  [to_chip(): return lax.ppermute(block, 'col', CHIP)]
    unnamed x0 -> x1, other arithmetic: none -> 1.02 us
    convert_element_type x1 -> x0, other arithmetic: 1.02 us -> none  [shards(): m_own = jnp.where(live, transfer * SCALE, 0.0).astype(F16)]
    ppermute x3 -> x4, waiting for transfers between devices: 8.33 us -> 8.02 us  [to_sibling(): lax.ppermute(block, 'row', [(n, n ^ 1 << BIT) for n in range(lax.axis_siz...]
    ppermute x3 -> x4, starting transfers between devices: 3.76 us -> 3.64 us  [to_sibling(): lax.ppermute(block, 'row', [(n, n ^ 1 << BIT) for n in range(lax.axis_siz...]
  transfers between devices with their start and end apart: 18 -> 25, of which waited for: 9 -> 12; matrix products, arithmetic and copies ran while one was open for 10% -> 11% of each run, Pallas kernels for 14% -> 15%
where the time goes in v3:
time: 47.1 us; the launch traced here: 46.9 us
  starting transfers between devices  15.5 us (33%)
  waiting for transfers between devices  14.8 us (31%)
  Pallas kernels  7.19 us (15%)
  local copies, waits for them, and re-layouts  5.09 us (11%)
  other arithmetic  3.38 us (7%)
  between operations  0.96 us (2%)
    ppermute x4, waiting for transfers between devices, to_sibling(): lax.ppermute(block, 'row', [(n, n ^ 1 << BIT) for n in range(lax.axis_siz...  8.02 us
    ppermute x6, starting transfers between devices, to_chip(): return lax.ppermute(block, 'col', CHIP)  7.84 us
    ppermute x15, starting transfers between devices, to_core(): return lax.ppermute(block, 'col', CORE)  4.02 us
    ppermute x4, starting transfers between devices, to_sibling(): lax.ppermute(block, 'row', [(n, n ^ 1 << BIT) for n in range(lax.axis_siz...  3.64 us
    ppermute x6, waiting for transfers between devices, to_chip(): return lax.ppermute(block, 'col', CHIP)  3.55 us
    pallas_call x3, Pallas kernels, merge(): call(functools.partial(merge_kernel, n), [shape((2, part, width), F32), s...  3.44 us
    ppermute x15, waiting for transfers between devices, to_core(): return lax.ppermute(block, 'col', CORE)  3.19 us
    unnamed x18, local copies, waits for them, and re-layouts  2.92 us
  transfers between devices with their start and end apart: 25, of which 12 were waited for; matrix products, arithmetic and copies ran while one was open for 11% of the time, Pallas kernels for 15%

profile of v3, /device:TPU:8, one launch (start us, length us, event | category | flops | bytes accessed | tf_op | source)
XLA Modules:
  0.0 46.9 jit_solution(17524614755818119493)
XLA Ops:
  0.8 1.1 %slice_bitcast_fusion.2 = bf16[512,256]{1,0:T(8,128)(2,1)S(1)} fusion(bf16[3,512,256]{2,1,0:T(8,128)(2,1)} %own.1), kind=kLoop, calls=%fused_computation.3 | loop fusion | bytes 524288 | tf_op jit(solution)/shard_map/squeeze | solution.py:128
  1.8 2.3 %collective-permute-start.1 = (bf16[512,256]{1,0:T(8,128)(2,1)S(1)}, bf16[512,256]{1,0:T(8,128)(2,1)S(1)}, u32[]{:S(2)}, u32[]{:S(2)}) collective-permute-start(bf16[512,256]{1,0:T(8,128)(2,1)S(1)} %slice_bitcast_fusion.2), channel_id=1, source_target_pairs={{0,2},{2,0},{1,3},{3,1},{4,6},{6,4},{5,7},{7,5},{8,10},{10,8},{9,1... | collective-permute-start | bytes 786440 | tf_op jit(solution)/shard_map/ppermute | solution.py:26
  4.1 0.7 %broadcast_compare_fusion = pred[3,64]{1,0:T(4,128)(4,1)S(1)} fusion(s32[64]{0:T(128)S(1)} %iota_add_fusion, s32[3]{0:T(128)} %ranks.5), kind=kLoop, calls=%fused_computation.20 | loop fusion | flops 192 | bytes 460 | tf_op jit(solution)/shard_map/lt | solution.py:132
  4.9 1.0 %bitcast_dynamic-update-slice_fusion.7 = (f16[8,3,64,256]{3,2,1,0:T(8,128)(2,1)S(1)}, f16[3,64,256]{2,1,0:T(8,128)(2,1)S(1)}) fusion(f32[3,64,256]{2,1,0:T(8,128)} %param.9, pred[3,64]{1,0:T(4,128)(4,1)S(1)} %broadcast_compare_fusion), kind=kLoop, calls=%fused_computation.16 | loop fusion | flops 147455 | bytes 393408
  6.0 1.7 %collective-permute-start.6 = (f16[3,64,256]{2,1,0:T(8,128)(2,1)S(1)}, f16[3,64,256]{2,1,0:T(8,128)(2,1)S(1)}, u32[]{:S(2)}, u32[]{:S(2)}) collective-permute-start(f16[3,64,256]{2,1,0:T(8,128)(2,1)S(1)} %get-tuple-element.43), channel_id=1, source_target_pairs={{0,16},{4,20},{8,24},{12,28},{16,0},{20,4},{24,8},{28,12},{32,48},... | collective-permute-start | bytes 294920 | tf_op jit(solution)/shard_map/ppermute | solution.py:30
  7.7 1.0 %slice_bitcast_fusion.1 = bf16[512,256]{1,0:T(8,128)(2,1)S(1)} fusion(bf16[3,512,256]{2,1,0:T(8,128)(2,1)} %own.1), kind=kLoop, calls=%fused_computation.2 | loop fusion | bytes 524288 | tf_op jit(solution)/shard_map/squeeze | solution.py:135
  8.7 2.1 %collective-permute-done.6 = f16[3,64,256]{2,1,0:T(8,128)(2,1)S(1)} collective-permute-done((f16[3,64,256]{2,1,0:T(8,128)(2,1)S(1)}, f16[3,64,256]{2,1,0:T(8,128)(2,1)S(1)}, u32[]{:S(2)}, u32[]{:S(2)}) %collective-permute-start.6) | collective-permute-done | bytes 98336 | tf_op jit(solution)/shard_map/ppermute | solution.py:30
  10.9 1.8 %collective-permute-start.13 = (bf16[512,256]{1,0:T(8,128)(2,1)S(1)}, bf16[512,256]{1,0:T(8,128)(2,1)S(1)}, u32[]{:S(2)}, u32[]{:S(2)}) collective-permute-start(bf16[512,256]{1,0:T(8,128)(2,1)S(1)} %slice_bitcast_fusion.1), channel_id=1, source_target_pairs={{0,2},{2,0},{1,3},{3,1},{4,6},{6,4},{5,7},{7,5},{8,10},{10,8},{9,1... | collective-permute-start | bytes 786440 | tf_op jit(solution)/shard_map/ppermute | solution.py:26
  12.8 1.3 %collective-permute-done.8 = f16[3,64,256]{2,1,0:T(8,128)(2,1)S(1)} collective-permute-done((f16[3,64,256]{2,1,0:T(8,128)(2,1)S(1)}, f16[3,64,256]{2,1,0:T(8,128)(2,1)S(1)}, u32[]{:S(2)}, u32[]{:S(2)}) %collective-permute-start.8) | collective-permute-done | bytes 98336 | tf_op jit(solution)/shard_map/ppermute | solution.py:22
  14.3 2.8 %copy-done = bf16[3,512,2048]{2,1,0:T(8,128)(2,1)S(1)} copy-done((bf16[3,512,2048]{2,1,0:T(8,128)(2,1)S(1)}, bf16[3,512,2048]{2,1,0:T(8,128)(2,1)}, u32[]{:S(2)}) %copy-start) | copy-done | bytes 6291480
  17.0 1.0 %begin.1 = (f32[3,512,256]{2,1,0:T(8,128)S(1)}, bf16[3,256,512]{2,1,0:T(8,128)(2,1)S(1)}) custom-call(bf16[3,512,2048]{2,1,0:T(8,128)(2,1)S(1)} %copy-done, bf16[3,512,256]{2,1,0:T(8,128)(2,1)S(1)} %copy-done.2, bf16[3,512,256]{2,1,0:T(8,128)(2,1)S(1)} %collective-permute-done.core, bf16[3,512,256]{2,1,0:T(8,128)(2,1)S(1)} %copy-done.3), custom_call_target="tpu_custom_call" | custom-call | flops 1 | bytes 1 | tf_op jit(solution)/shard_map/begin/pallas_call | solution.py:139
  18.7 1.5 %collective-permute-start.17 = (bf16[512,256]{1,0:T(8,128)(2,1)S(1)}, bf16[512,256]{1,0:T(8,128)(2,1)S(1)}, u32[]{:S(2)}, u32[]{:S(2)}) collective-permute-start(bf16[512,256]{1,0:T(8,128)(2,1)S(1)} %slice_bitcast_fusion), channel_id=1, source_target_pairs={{0,2},{2,0},{1,3},{3,1},{4,6},{6,4},{5,7},{7,5},{8,10},{10,8},{9,1... | collective-permute-start | bytes 786440 | tf_op jit(solution)/shard_map/ppermute | solution.py:26
  20.2 3.1 %collective-permute-done.9 = f16[3,64,256]{2,1,0:T(8,128)(2,1)S(1)} collective-permute-done((f16[3,64,256]{2,1,0:T(8,128)(2,1)S(1)}, f16[3,64,256]{2,1,0:T(8,128)(2,1)S(1)}, u32[]{:S(2)}, u32[]{:S(2)}) %collective-permute-start.9) | collective-permute-done | bytes 98336 | tf_op jit(solution)/shard_map/ppermute | solution.py:30
  23.9 0.7 %collective-permute-done.3.cross_a = bf16[256,256]{1,0:T(8,128)(2,1)S(1)} collective-permute-done((bf16[256,256]{1,0:T(8,128)(2,1)S(1)}, bf16[256,256]{1,0:T(8,128)(2,1)S(1)}, u32[]{:S(2)}, u32[]{:S(2)}) %collective-permute-start.3) | collective-permute-done | bytes 131104 | tf_op jit(solution)/shard_map/ppermute | solution.py:22
  26.6 0.8 %collective-permute-done.14.cross_a = bf16[256,256]{1,0:T(8,128)(2,1)S(1)} collective-permute-done((bf16[256,256]{1,0:T(8,128)(2,1)S(1)}, bf16[256,256]{1,0:T(8,128)(2,1)S(1)}, u32[]{:S(2)}, u32[]{:S(2)}) %collective-permute-start.14) | collective-permute-done | bytes 131104 | tf_op jit(solution)/shard_map/ppermute | solution.py:22
  29.7 0.7 %couple.1 = (bf16[3,768,256]{2,1,0:T(8,128)(2,1)S(1)}, bf16[3,128,768]{2,1,0:T(8,128)(2,1)S(1)}, f32[3,128,256]{2,1,0:T(8,128)S(1)}) custom-call(f32[4,2,3,64,256]{4,3,2,1,0:T(8,128)S(1)} %bitcast.36, f32[3,64,256]{2,1,0:T(8,128)S(1)} %copy-done.4, f32[3,64,256]{2,1,0:T(8,128)S(1)} %collective-permute-done.12.c_core), custom_call_target="tpu_custom_call" | custom-call | flops 1 | bytes 1 | tf_op jit(solution)/shard_map/couple/pallas_call | solution.py:179
  31.7 1.1 %merge0.1 = (f32[2,64,256]{2,1,0:T(8,128)S(1)}, bf16[2,64,256]{2,1,0:T(8,128)(2,1)S(1)}) custom-call(s32[3]{0:T(128)S(1)} %copy-done.5, f32[256,256]{1,0:T(8,128)S(1)} %eliminate0.1.s_own, f32[256,256]{1,0:T(8,128)S(1)} %collective-permute-done.5.s_core, bf16[3,768,256]{2,1,0:T(8,128)(2,1)S(1)} %get-tuple-element.28.m, ...), custom_call_target="tpu_custom_call" | custom-call | flops 1 | bytes 1 | tf_op jit(solution)/shard_map/merge0/pallas_call | solution.py:163
  32.8 1.1 %merge1.1 = (f32[2,64,256]{2,1,0:T(8,128)S(1)}, bf16[2,64,256]{2,1,0:T(8,128)(2,1)S(1)}) custom-call(s32[3]{0:T(128)S(1)} %copy-done.5, f32[256,256]{1,0:T(8,128)S(1)} %eliminate1.1.s_own, f32[256,256]{1,0:T(8,128)S(1)} %collective-permute-done.16.s_core, bf16[3,768,256]{2,1,0:T(8,128)(2,1)S(1)} %get-tuple-element.28.m, ...), custom_call_target="tpu_custom_call" | custom-call | flops 1 | bytes 1 | tf_op jit(solution)/shard_map/merge1/pallas_call | solution.py:163
  34.4 1.1 %merge2.1 = (f32[2,64,256]{2,1,0:T(8,128)S(1)}, bf16[2,64,256]{2,1,0:T(8,128)(2,1)S(1)}) custom-call(s32[3]{0:T(128)S(1)} %copy-done.5, f32[256,256]{1,0:T(8,128)S(1)} %eliminate2.1.s_own, f32[256,256]{1,0:T(8,128)S(1)} %collective-permute-done.20.s_core, bf16[3,768,256]{2,1,0:T(8,128)(2,1)S(1)} %get-tuple-element.28.m, ...), custom_call_target="tpu_custom_call" | custom-call | flops 1 | bytes 1 | tf_op jit(solution)/shard_map/merge2/pallas_call | solution.py:163
  35.6 1.8 %collective-permute-start.22 = (bf16[2,64,256]{2,1,0:T(8,128)(2,1)S(1)}, bf16[2,64,256]{2,1,0:T(8,128)(2,1)S(1)}, u32[]{:S(2)}, u32[]{:S(2)}) collective-permute-start(bf16[2,64,256]{2,1,0:T(8,128)(2,1)S(1)} %get-tuple-element.41), channel_id=1, source_target_pairs={{0,2},{2,0},{1,3},{3,1},{4,6},{6,4},{5,7},{7,5},{8,10},{10,8},{9,1... | collective-permute-start | bytes 196616 | tf_op jit(solution)/shard_map/ppermute | solution.py:26
  37.4 3.0 %collective-permute-done.21 = bf16[2,2,64,256]{3,2,0,1:T(8,128)(2,1)S(1)} collective-permute-done((bf16[2,2,64,256]{3,2,0,1:T(8,128)(2,1)S(1)}, bf16[2,2,64,256]{3,2,0,1:T(8,128)(2,1)S(1)}, u32[]{:S(2)}, u32[]{:S(2)}) %collective-permute-start.21) | collective-permute-done | bytes 131104 | tf_op jit(solution)/shard_map/ppermute | solution.py:26
  41.1 1.5 %collective-permute-start.24 = (f32[64,256]{1,0:T(8,128)S(1)}, f32[64,256]{1,0:T(8,128)S(1)}, u32[]{:S(2)}, u32[]{:S(2)}) collective-permute-start(f32[64,256]{1,0:T(8,128)S(1)} %get-tuple-element.54), channel_id=1, source_target_pairs={{0,16},{4,20},{8,24},{12,28},{16,0},{20,4},{24,8},{28,12},{32,48},... | collective-permute-start | bytes 196616 | tf_op jit(solution)/shard_map/ppermute | solution.py:30
  42.6 0.7 %maximum_add_fusion = f32[3,64,256]{2,1,0:T(8,128)} fusion(f32[1,64,256]{2,1,0:T(8,128)S(1)} %get-tuple-element.55, f32[1,64,256]{2,1,0:T(8,128)S(1)} %get-tuple-element.56, f32[1,64,256]{2,1,0:T(8,128)S(1)} %get-tuple-element.51, bf16[1,64,256]{2,1,0:T(8,128)(2,1)S(1)} %slice.76, bf16[2,64,256]{2,1,0:T(8,128)(2,1)S(1)} %slice_bitcast_fusion.3), kind=kLoop, calls=%fused_computation.4 | loop fusion | flops 245760 | bytes 491520 | tf_op jit(solution)/shard_map/add | solution.py:204
  43.3 2.1 %collective-permute-done.23 = f32[2,64,256]{2,1,0:T(8,128)S(1)} collective-permute-done((f32[2,64,256]{2,1,0:T(8,128)S(1)}, f32[2,64,256]{2,1,0:T(8,128)S(1)}, u32[]{:S(2)}, u32[]{:S(2)}) %collective-permute-start.23) | collective-permute-done | bytes 131104 | tf_op jit(solution)/shard_map/ppermute | solution.py:30
  (73 shorter events, 9.8 us)
Async XLA Ops:
  0.7 13.6 %collective-permute-start = (bf16[3,512,256]{2,1,0:T(8,128)(2,1)}, bf16[3,512,256]{2,1,0:T(8,128)(2,1)S(1)}, u32[]{:S(2)}, u32[]{:S(2)}) collective-permute-start(bf16[3,512,256]{2,1,0:T(8,128)(2,1)} %own.1), channel_id=1, source_target_pairs={{0,1},{1,0},{2,3},{3,2},{4,5},{5,4},{6,7},{7,6},{8,9},{9,8},{10,11... | collective-permute-start | bytes 2359304 | tf_op jit(solution)/shard_map/ppermute | solution.py:22
  1.8 16.2 %collective-permute-start.1 = (bf16[512,256]{1,0:T(8,128)(2,1)S(1)}, bf16[512,256]{1,0:T(8,128)(2,1)S(1)}, u32[]{:S(2)}, u32[]{:S(2)}) collective-permute-start(bf16[512,256]{1,0:T(8,128)(2,1)S(1)} %slice_bitcast_fusion.2), channel_id=1, source_target_pairs={{0,2},{2,0},{1,3},{3,1},{4,6},{6,4},{5,7},{7,5},{8,10},{10,8},{9,1... | collective-permute-start | bytes 786440 | tf_op jit(solution)/shard_map/ppermute | solution.py:26
  5.9 12.2 %collective-permute-start.2 = (f16[3,64,256]{2,1,0:T(8,128)(2,1)S(1)}, f16[3,64,256]{2,1,0:T(8,128)(2,1)S(1)}, u32[]{:S(2)}, u32[]{:S(2)}) collective-permute-start(f16[3,64,256]{2,1,0:T(8,128)(2,1)S(1)} %get-tuple-element.43), channel_id=1, source_target_pairs={{0,2},{2,0},{1,3},{3,1},{4,6},{6,4},{5,7},{7,5},{8,10},{10,8},{9,1... | collective-permute-start | bytes 294920 | tf_op jit(solution)/shard_map/ppermute | solution.py:26
  6.0 4.9 %collective-permute-start.6 = (f16[3,64,256]{2,1,0:T(8,128)(2,1)S(1)}, f16[3,64,256]{2,1,0:T(8,128)(2,1)S(1)}, u32[]{:S(2)}, u32[]{:S(2)}) collective-permute-start(f16[3,64,256]{2,1,0:T(8,128)(2,1)S(1)} %get-tuple-element.43), channel_id=1, source_target_pairs={{0,16},{4,20},{8,24},{12,28},{16,0},{20,4},{24,8},{28,12},{32,48},... | collective-permute-start | bytes 294920 | tf_op jit(solution)/shard_map/ppermute | solution.py:30
  7.7 4.9 %collective-permute-start.7 = (f16[3,64,256]{2,1,0:T(8,128)(2,1)S(1)}, f16[3,64,256]{2,1,0:T(8,128)(2,1)S(1)}, u32[]{:S(2)}, u32[]{:S(2)}) collective-permute-start(f16[3,64,256]{2,1,0:T(8,128)(2,1)S(1)} %get-tuple-element.43), channel_id=1, source_target_pairs={{0,1},{1,0},{2,3},{3,2},{4,5},{5,4},{6,7},{7,6},{8,9},{9,8},{10,11... | collective-permute-start | bytes 294920 | tf_op jit(solution)/shard_map/ppermute | solution.py:22
  10.9 15.1 %collective-permute-start.13 = (bf16[512,256]{1,0:T(8,128)(2,1)S(1)}, bf16[512,256]{1,0:T(8,128)(2,1)S(1)}, u32[]{:S(2)}, u32[]{:S(2)}) collective-permute-start(bf16[512,256]{1,0:T(8,128)(2,1)S(1)} %slice_bitcast_fusion.1), channel_id=1, source_target_pairs={{0,2},{2,0},{1,3},{3,1},{4,6},{6,4},{5,7},{7,5},{8,10},{10,8},{9,1... | collective-permute-start | bytes 786440 | tf_op jit(solution)/shard_map/ppermute | solution.py:26
  12.7 1.4 %collective-permute-start.8 = (f16[3,64,256]{2,1,0:T(8,128)(2,1)S(1)}, f16[3,64,256]{2,1,0:T(8,128)(2,1)S(1)}, u32[]{:S(2)}, u32[]{:S(2)}) collective-permute-start(f16[3,64,256]{2,1,0:T(8,128)(2,1)S(1)} %collective-permute-done.6), channel_id=1, source_target_pairs={{0,1},{1,0},{2,3},{3,2},{4,5},{5,4},{6,7},{7,6},{8,9},{9,8},{10,11... | collective-permute-start | bytes 294920 | tf_op jit(solution)/shard_map/ppermute | solution.py:22
  14.1 15.7 %collective-permute-start.12 = (f32[3,64,256]{2,1,0:T(8,128)S(1)}, f32[3,64,256]{2,1,0:T(8,128)S(1)}, u32[]{:S(2)}, u32[]{:S(2)}) collective-permute-start(f32[3,64,256]{2,1,0:T(8,128)S(1)} %copy-done.4), channel_id=1, source_target_pairs={{0,1},{1,0},{2,3},{3,2},{4,5},{5,4},{6,7},{7,6},{8,9},{9,8},{10,11... | collective-permute-start | bytes 589832 | tf_op jit(solution)/shard_map/ppermute | solution.py:22
  18.1 5.1 %collective-permute-start.9 = (f16[3,64,256]{2,1,0:T(8,128)(2,1)S(1)}, f16[3,64,256]{2,1,0:T(8,128)(2,1)S(1)}, u32[]{:S(2)}, u32[]{:S(2)}) collective-permute-start(f16[3,64,256]{2,1,0:T(8,128)(2,1)S(1)} %collective-permute-done.2), channel_id=1, source_target_pairs={{0,16},{4,20},{8,24},{12,28},{16,0},{20,4},{24,8},{28,12},{32,48},... | collective-permute-start | bytes 294920 | tf_op jit(solution)/shard_map/ppermute | solution.py:30
  18.4 4.9 %collective-permute-start.10 = (f16[3,64,256]{2,1,0:T(8,128)(2,1)S(1)}, f16[3,64,256]{2,1,0:T(8,128)(2,1)S(1)}, u32[]{:S(2)}, u32[]{:S(2)}) collective-permute-start(f16[3,64,256]{2,1,0:T(8,128)(2,1)S(1)} %collective-permute-done.2), channel_id=1, source_target_pairs={{0,1},{1,0},{2,3},{3,2},{4,5},{5,4},{6,7},{7,6},{8,9},{9,8},{10,11... | collective-permute-start | bytes 294920 | tf_op jit(solution)/shard_map/ppermute | solution.py:22
  18.7 10.3 %collective-permute-start.17 = (bf16[512,256]{1,0:T(8,128)(2,1)S(1)}, bf16[512,256]{1,0:T(8,128)(2,1)S(1)}, u32[]{:S(2)}, u32[]{:S(2)}) collective-permute-start(bf16[512,256]{1,0:T(8,128)(2,1)S(1)} %slice_bitcast_fusion), channel_id=1, source_target_pairs={{0,2},{2,0},{1,3},{3,1},{4,6},{6,4},{5,7},{7,5},{8,10},{10,8},{9,1... | collective-permute-start | bytes 786440 | tf_op jit(solution)/shard_map/ppermute | solution.py:26
  23.3 1.6 %collective-permute-start.4 = (bf16[256,256]{1,0:T(8,128)(2,1)S(1)}, bf16[256,256]{1,0:T(8,128)(2,1)S(1)}, u32[]{:S(2)}, u32[]{:S(2)}) collective-permute-start(bf16[256,256]{1,0:T(8,128)(2,1)S(1)} %get-tuple-element.48), channel_id=1, source_target_pairs={{0,1},{1,0},{2,3},{3,2},{4,5},{5,4},{6,7},{7,6},{8,9},{9,8},{10,11... | collective-permute-start | bytes 393224 | tf_op jit(solution)/shard_map/ppermute | solution.py:22
  24.6 1.7 %collective-permute-start.11 = (f16[3,64,256]{2,1,0:T(8,128)(2,1)S(1)}, f16[3,64,256]{2,1,0:T(8,128)(2,1)S(1)}, u32[]{:S(2)}, u32[]{:S(2)}) collective-permute-start(f16[3,64,256]{2,1,0:T(8,128)(2,1)S(1)} %collective-permute-done.9), channel_id=1, source_target_pairs={{0,1},{1,0},{2,3},{3,2},{4,5},{5,4},{6,7},{7,6},{8,9},{9,8},{10,11... | collective-permute-start | bytes 294920 | tf_op jit(solution)/shard_map/ppermute | solution.py:22
  25.5 6.1 %collective-permute-start.5 = (f32[256,256]{1,0:T(8,128)S(1)}, f32[256,256]{1,0:T(8,128)S(1)}, u32[]{:S(2)}, u32[]{:S(2)}) collective-permute-start(f32[256,256]{1,0:T(8,128)S(1)} %eliminate0.1.s_own), channel_id=1, source_target_pairs={{0,1},{1,0},{2,3},{3,2},{4,5},{5,4},{6,7},{7,6},{8,9},{9,8},{10,11... | collective-permute-start | bytes 786440 | tf_op jit(solution)/shard_map/ppermute | solution.py:22
  26.0 1.4 %collective-permute-start.14 = (bf16[256,256]{1,0:T(8,128)(2,1)S(1)}, bf16[256,256]{1,0:T(8,128)(2,1)S(1)}, u32[]{:S(2)}, u32[]{:S(2)}) collective-permute-start(bf16[256,256]{1,0:T(8,128)(2,1)S(1)} %get-tuple-element.47), channel_id=1, source_target_pairs={{0,1},{1,0},{2,3},{3,2},{4,5},{5,4},{6,7},{7,6},{8,9},{9,8},{10,11... | collective-permute-start | bytes 393224 | tf_op jit(solution)/shard_map/ppermute | solution.py:22
  26.3 1.4 %collective-permute-start.15 = (bf16[256,256]{1,0:T(8,128)(2,1)S(1)}, bf16[256,256]{1,0:T(8,128)(2,1)S(1)}, u32[]{:S(2)}, u32[]{:S(2)}) collective-permute-start(bf16[256,256]{1,0:T(8,128)(2,1)S(1)} %get-tuple-element.46), channel_id=1, source_target_pairs={{0,1},{1,0},{2,3},{3,2},{4,5},{5,4},{6,7},{7,6},{8,9},{9,8},{10,11... | collective-permute-start | bytes 393224 | tf_op jit(solution)/shard_map/ppermute | solution.py:22
  28.3 4.5 %collective-permute-start.16 = (f32[256,256]{1,0:T(8,128)S(1)}, f32[256,256]{1,0:T(8,128)S(1)}, u32[]{:S(2)}, u32[]{:S(2)}) collective-permute-start(f32[256,256]{1,0:T(8,128)S(1)} %eliminate1.1.s_own), channel_id=1, source_target_pairs={{0,1},{1,0},{2,3},{3,2},{4,5},{5,4},{6,7},{7,6},{8,9},{9,8},{10,11... | collective-permute-start | bytes 786440 | tf_op jit(solution)/shard_map/ppermute | solution.py:22
  29.0 1.5 %collective-permute-start.18 = (bf16[256,256]{1,0:T(8,128)(2,1)S(1)}, bf16[256,256]{1,0:T(8,128)(2,1)S(1)}, u32[]{:S(2)}, u32[]{:S(2)}) collective-permute-start(bf16[256,256]{1,0:T(8,128)(2,1)S(1)} %get-tuple-element.45), channel_id=1, source_target_pairs={{0,1},{1,0},{2,3},{3,2},{4,5},{5,4},{6,7},{7,6},{8,9},{9,8},{10,11... | collective-permute-start | bytes 393224 | tf_op jit(solution)/shard_map/ppermute | solution.py:22
  29.2 1.4 %collective-permute-start.19 = (bf16[256,256]{1,0:T(8,128)(2,1)S(1)}, bf16[256,256]{1,0:T(8,128)(2,1)S(1)}, u32[]{:S(2)}, u32[]{:S(2)}) collective-permute-start(bf16[256,256]{1,0:T(8,128)(2,1)S(1)} %get-tuple-element.44), channel_id=1, source_target_pairs={{0,1},{1,0},{2,3},{3,2},{4,5},{5,4},{6,7},{7,6},{8,9},{9,8},{10,11... | collective-permute-start | bytes 393224 | tf_op jit(solution)/shard_map/ppermute | solution.py:22
  31.3 3.2 %collective-permute-start.20 = (f32[256,256]{1,0:T(8,128)S(1)}, f32[256,256]{1,0:T(8,128)S(1)}, u32[]{:S(2)}, u32[]{:S(2)}) collective-permute-start(f32[256,256]{1,0:T(8,128)S(1)} %eliminate2.1.s_own), channel_id=1, source_target_pairs={{0,1},{1,0},{2,3},{3,2},{4,5},{5,4},{6,7},{7,6},{8,9},{9,8},{10,11... | collective-permute-start | bytes 786440 | tf_op jit(solution)/shard_map/ppermute | solution.py:22
  34.0 6.4 %collective-permute-start.21 = (bf16[2,2,64,256]{3,2,0,1:T(8,128)(2,1)S(1)}, bf16[2,2,64,256]{3,2,0,1:T(8,128)(2,1)S(1)}, u32[]{:S(2)}, u32[]{:S(2)}) collective-permute-start(bf16[2,2,64,256]{3,2,0,1:T(8,128)(2,1)S(1)} %pad_maximum_fusion.1), channel_id=1, source_target_pairs={{0,2},{2,0},{1,3},{3,1},{4,6},{6,4},{5,7},{7,5},{8,10},{10,8},{9,1... | collective-permute-start | bytes 393224 | tf_op jit(solution)/shard_map/ppermute | solution.py:26
  35.6 5.5 %collective-permute-start.22 = (bf16[2,64,256]{2,1,0:T(8,128)(2,1)S(1)}, bf16[2,64,256]{2,1,0:T(8,128)(2,1)S(1)}, u32[]{:S(2)}, u32[]{:S(2)}) collective-permute-start(bf16[2,64,256]{2,1,0:T(8,128)(2,1)S(1)} %get-tuple-element.41), channel_id=1, source_target_pairs={{0,2},{2,0},{1,3},{3,1},{4,6},{6,4},{5,7},{7,5},{8,10},{10,8},{9,1... | collective-permute-start | bytes 196616 | tf_op jit(solution)/shard_map/ppermute | solution.py:26
  40.4 5.1 %collective-permute-start.23 = (f32[2,64,256]{2,1,0:T(8,128)S(1)}, f32[2,64,256]{2,1,0:T(8,128)S(1)}, u32[]{:S(2)}, u32[]{:S(2)}) collective-permute-start(f32[2,64,256]{2,1,0:T(8,128)S(1)} %maximum_add_fusion.1), channel_id=1, source_target_pairs={{0,16},{4,20},{8,24},{12,28},{16,0},{20,4},{24,8},{28,12},{32,48},... | collective-permute-start | bytes 393224 | tf_op jit(solution)/shard_map/ppermute | solution.py:30
  41.1 5.1 %collective-permute-start.24 = (f32[64,256]{1,0:T(8,128)S(1)}, f32[64,256]{1,0:T(8,128)S(1)}, u32[]{:S(2)}, u32[]{:S(2)}) collective-permute-start(f32[64,256]{1,0:T(8,128)S(1)} %get-tuple-element.54), channel_id=1, source_target_pairs={{0,16},{4,20},{8,24},{12,28},{16,0},{20,4},{24,8},{28,12},{32,48},... | collective-permute-start | bytes 196616 | tf_op jit(solution)/shard_map/ppermute | solution.py:30
  (7 other events, 53.8 us)

commit v4 on v3

--- a/solution.py
+++ b/solution.py
@@ -57,32 +57,44 @@
     return jnp.concatenate([high, low, high], 0)
 
 
-def call(body, shapes, specs, flops, name, scratch=()):
+def call(body, shapes, specs, name, scratch=(), mib=8):
     return pl.pallas_call(
         body,
         out_shape=shapes,
         in_specs=specs,
         out_specs=jax.tree.map(lambda _: VMEM, shapes),
         scratch_shapes=scratch,
-        compiler_params=pltpu.CompilerParams(vmem_limit_bytes=8 << 20),
+        compiler_params=pltpu.CompilerParams(vmem_limit_bytes=mib << 20),
         cost_estimate=pl.CostEstimate(flops=1, bytes_accessed=1, transcendentals=0),
         name=name,
     )
 
 
-def begin_kernel(d, own, core, right, e_out, rt_out):
+def begin_kernel(d, own, core, right, e_out, rt_out, far_out, near, sem):
     q = lax.axis_index("col")
     nodes, depth, _ = own.shape
+    copies = [
+        pltpu.make_async_copy(d.at[n, :, band(q >> 1, 2 * depth)], near.at[n], sem.at[0, n]) for n in range(nodes)
+    ]
+    others = [
+        pltpu.make_async_copy(d.at[n, :, band(1 - (q >> 1), 2 * depth)], far_out.at[n], sem.at[1, n]) for n in range(nodes)
+    ]
+    for copy in copies + others:
+        copy.start()
     for n in range(nodes):
-        e_out[n] = dot(d[n, :, band(q, depth)], own[n]) + dot(d[n, :, band(q ^ 1, depth)], core[n])
         rt_out[n] = right[n].T
+    for n in range(nodes):
+        copies[n].wait()
+        e_out[n] = dot(near[n, :, band(q & 1, depth)], own[n]) + dot(near[n, :, band(1 - (q & 1), depth)], core[n])
+    for copy in others:
+        copy.wait()
 
 
 def eliminate_kernel(n, e, d, chip, cross_a, cross_b, rt, s_out):
     q = lax.axis_index("col")
     depth = chip.shape[0]
     cross = jnp.concatenate([cross_a[...], cross_b[...]], 0)
-    elim = e[n] + dot(d[n, :, band(q ^ 2, depth)], chip[...]) + dot(d[n, :, band(q ^ 3, depth)], cross)
+    elim = e[n] + dot(d[n, :, band(q & 1, depth)], chip[...]) + dot(d[n, :, band(1 - (q & 1), depth)], cross)
     s_out[...] = dot(rt[n], elim.astype(BF16))
 
 
@@ -131,40 +143,39 @@
     rows = q * part + jnp.arange(part, dtype=jnp.int32)
     live = (rows[None, :] < ranks_late[:, None])[:, :, None]
     m_own = jnp.where(live, transfer * SCALE, 0.0).astype(F16)
-    m_chip = to_chip(m_own)
+    m_chip, sib_own = to_chip(m_own), to_sibling(m_own)
     chip_left.append(to_chip(after(column_basis, m_own)[1]))
     core_left = to_core(column_basis)
     c_core = to_core(coupling)
 
-    e, rt = call(
+    e, rt, d = call(
         begin_kernel,
-        [shape((nodes, depth, width), F32), shape((nodes, width, depth), BF16)],
-        [VMEM] * 4,
-        2 * nodes * depth * 2 * depth * width,
+        [shape((nodes, depth, width), F32), shape((nodes, width, depth), BF16), shape((nodes, depth, 2 * depth), BF16)],
+        [pl.BlockSpec(memory_space=pltpu.HBM), VMEM, VMEM, VMEM],
         "begin",
+        [pltpu.VMEM((nodes, depth, 2 * depth), BF16), pltpu.SemaphoreType.DMA((2, nodes))],
+        45,
     )(diagonal_inverses, column_basis, core_left, row_basis)
-    chip_left[0], m_chip, last = lax.optimization_barrier((chip_left[0], m_chip, column_basis, e))[:3]
+    chip_left[0], m_chip, sib_own, last = lax.optimization_barrier((chip_left[0], m_chip, sib_own, column_basis, e))[:4]
     chip_left.append(to_chip(last[2]))
 
     def cross(left):
         half = depth // 2
         return to_core(left[:half]), to_core(left[half:])
 
-    def eliminate(n, chip):
+    def eliminate(n, chip, *earlier):
         return call(
             functools.partial(eliminate_kernel, n),
             shape((width, width), F32),
             [VMEM] * 6,
-            2 * depth * 2 * depth * width,
             f"eliminate{n}",
-        )(e, diagonal_inverses, chip, *cross(chip), rt)
+        )(after(e, *earlier), d, chip, *cross(chip), rt)
 
     def merge(n, s, s_core):
         return call(
             functools.partial(merge_kernel, n),
             [shape((2, part, width), F32), shape((2, part, width), BF16)],
             [SMEM] + [VMEM] * 5,
-            12 * width**3,
             f"merge{n}",
             [pltpu.VMEM((width, width), F32)],
         )(ranks, s, s_core, m, mt, cm)
@@ -173,7 +184,7 @@
     s1 = eliminate(1, after(chip_left[1], s0))
     s0_core, s1_core = to_core(s0), to_core(s1)
 
-    sib_own, sib_chip = to_sibling(m_own), to_sibling(m_chip)
+    sib_chip = after(to_sibling(m_chip), s0)
     pieces = [m_own, sib_own, to_core(m_own), to_core(sib_own), m_chip, sib_chip, to_core(m_chip), to_core(sib_chip)]
     blocks = (jnp.stack(pieces).astype(F32) * (1 / SCALE)).reshape((4, 2) + m_own.shape)
     m, mt, cm = call(
@@ -184,25 +195,21 @@
             shape((nodes, 2 * part, width), F32),
         ],
         [VMEM] * 3,
-        6 * nodes * 2 * part * width * width,
         "couple",
         [pltpu.VMEM((width, width), F32), pltpu.VMEM((width, width), F32), pltpu.VMEM((2 * part, width), F32)],
     )(blocks, coupling, c_core)
 
-    left2 = after(chip_left[2], s0, s1)
-    s2 = eliminate(2, left2)
     own0, send0 = merge(0, s0, s0_core)
+    left2 = after(chip_left[2], s1, own0)
     own1, send1 = merge(1, s1, s1_core)
-    got0 = to_chip(jnp.stack([send0, send1]))
+    s2 = eliminate(2, left2, own1)
+    got = to_chip(jnp.stack([send0, send1]))
     own2, send2 = merge(2, s2, to_core(s2))
     got2 = to_chip(send2)
-    got0 = after(got0, own2)
-    p01 = jnp.stack([own0[1], own1[1]]) + got0[:, 1].astype(F32)
-    p01_sib = to_sibling(p01)
-    p2 = own2[1] + got2[1].astype(F32)
-    p2_sib = to_sibling(p2)
-    merged = jnp.stack([own0[0], own1[0], own2[0]]) + jnp.concatenate([got0[:, 0], got2[:1]]).astype(F32)
-    parent = jnp.concatenate([p01 + p01_sib, (p2 + p2_sib)[None]])
+    got = after(got, got2)
+    own = jnp.stack([own0, own1, own2]) + jnp.concatenate([got, got2[None]]).astype(F32)
+    merged, share = own[:, 0], own[:, 1]
+    parent = share + to_sibling(share.astype(BF16)).astype(F32)
     return merged, parent
 
 

time: 47.1 us -> 43.4 us (0.921)
  waiting for transfers between devices: 14.8 us -> 12 us
  Pallas kernels: 7.19 us -> 9.32 us
  starting transfers between devices: 15.5 us -> 14 us
  local copies, waits for them, and re-layouts: 5.09 us -> 4.06 us
  other arithmetic: 3.38 us -> 2.68 us
    ppermute x4 -> x3, waiting for transfers between devices: 8.02 us -> 5.39 us  [to_sibling(): lax.ppermute(block, 'row', [(n, n ^ 1 << BIT) for n in range(lax.axis_siz...]
    pallas_call x1, Pallas kernels: 1.01 us -> 3.14 us  [shards(): call(begin_kernel, [shape((nodes, depth, width), F32), shape((nodes, widt...]
    unnamed x18 -> x14, local copies, waits for them, and re-layouts: 2.92 us -> 1.27 us
    ppermute x15, waiting for transfers between devices: 3.19 us -> 1.64 us  [to_core(): return lax.ppermute(block, 'col', CORE)]
    ppermute x6, waiting for transfers between devices: 3.55 us -> 4.97 us  [to_chip(): return lax.ppermute(block, 'col', CHIP)]
    ppermute x6, starting transfers between devices: 7.84 us -> 6.61 us  [to_chip(): return lax.ppermute(block, 'col', CHIP)]
    concatenate x1 -> x0, other arithmetic: 0.69 us -> none  [shards(): parent = jnp.concatenate([p01 + p01_sib, (p2 + p2_sib)[None]])]
    squeeze x1, local copies, waits for them, and re-layouts: 0.01 us -> 0.69 us  [shards(): merged, share = (own[:, 0], own[:, 1])]
  transfers between devices with their start and end apart: 25 -> 24, of which waited for: 12 -> 9; matrix products, arithmetic and copies ran while one was open for 11% -> 11% of each run, Pallas kernels for 15% -> 20%
where the time goes in v4:
time: 43.4 us; the launch traced here: 43 us
  starting transfers between devices  14 us (32%)
  waiting for transfers between devices  12 us (28%)
  Pallas kernels  9.32 us (21%)
  local copies, waits for them, and re-layouts  4.06 us (9%)
  other arithmetic  2.68 us (6%)
  between operations  0.93 us (2%)
    ppermute x6, starting transfers between devices, to_chip(): return lax.ppermute(block, 'col', CHIP)  6.61 us
    ppermute x3, waiting for transfers between devices, to_sibling(): lax.ppermute(block, 'row', [(n, n ^ 1 << BIT) for n in range(lax.axis_siz...  5.39 us
    ppermute x6, waiting for transfers between devices, to_chip(): return lax.ppermute(block, 'col', CHIP)  4.97 us
    ppermute x3, starting transfers between devices, to_sibling(): lax.ppermute(block, 'row', [(n, n ^ 1 << BIT) for n in range(lax.axis_siz...  3.78 us
    ppermute x15, starting transfers between devices, to_core(): return lax.ppermute(block, 'col', CORE)  3.62 us
    pallas_call x3, Pallas kernels, merge(): call(functools.partial(merge_kernel, n), [shape((2, part, width), F32), s...  3.44 us
    pallas_call x1, Pallas kernels, shards(): call(begin_kernel, [shape((nodes, depth, width), F32), shape((nodes, widt...  3.14 us
    pallas_call x3, Pallas kernels, eliminate(): call(functools.partial(eliminate_kernel, n), shape((width, width), F32),...  2.02 us
  transfers between devices with their start and end apart: 24, of which 9 were waited for; matrix products, arithmetic and copies ran while one was open for 11% of the time, Pallas kernels for 20%

profile of v4, /device:TPU:8, one launch (start us, length us, event | category | flops | bytes accessed | tf_op | source)
XLA Modules:
  0.0 43.0 jit_solution(8938682738846008792)
XLA Ops:
  0.7 1.0 %slice_bitcast_fusion.2 = bf16[512,256]{1,0:T(8,128)(2,1)S(1)} fusion(bf16[3,512,256]{2,1,0:T(8,128)(2,1)} %own.1), kind=kLoop, calls=%fused_computation.4 | loop fusion | bytes 524288 | tf_op jit(solution)/shard_map/squeeze | solution.py:140
  1.8 2.3 %collective-permute-start.1 = (bf16[512,256]{1,0:T(8,128)(2,1)S(1)}, bf16[512,256]{1,0:T(8,128)(2,1)S(1)}, u32[]{:S(2)}, u32[]{:S(2)}) collective-permute-start(bf16[512,256]{1,0:T(8,128)(2,1)S(1)} %slice_bitcast_fusion.2), channel_id=1, source_target_pairs={{0,2},{2,0},{1,3},{3,1},{4,6},{6,4},{5,7},{7,5},{8,10},{10,8},{9,1... | collective-permute-start | bytes 786440 | tf_op jit(solution)/shard_map/ppermute | solution.py:26
  4.0 0.7 %broadcast_compare_fusion = pred[3,64]{1,0:T(4,128)(4,1)S(1)} fusion(s32[64]{0:T(128)S(1)} %iota_add_fusion, s32[3]{0:T(128)} %ranks.5), kind=kLoop, calls=%fused_computation.19 | loop fusion | flops 192 | bytes 460 | tf_op jit(solution)/shard_map/lt | solution.py:144
  4.8 1.0 %bitcast_dynamic-update-slice_fusion.7 = (f16[8,3,64,256]{3,2,1,0:T(8,128)(2,1)S(1)}, f16[3,64,256]{2,1,0:T(8,128)(2,1)S(1)}) fusion(f32[3,64,256]{2,1,0:T(8,128)} %param.9, pred[3,64]{1,0:T(4,128)(4,1)S(1)} %broadcast_compare_fusion), kind=kLoop, calls=%fused_computation.18 | loop fusion | flops 147455 | bytes 393408
  5.9 1.7 %collective-permute-start.3 = (f16[3,64,256]{2,1,0:T(8,128)(2,1)S(1)}, f16[3,64,256]{2,1,0:T(8,128)(2,1)S(1)}, u32[]{:S(2)}, u32[]{:S(2)}) collective-permute-start(f16[3,64,256]{2,1,0:T(8,128)(2,1)S(1)} %get-tuple-element.51), channel_id=1, source_target_pairs={{0,16},{4,20},{8,24},{12,28},{16,0},{20,4},{24,8},{28,12},{32,48},... | collective-permute-start | bytes 294920 | tf_op jit(solution)/shard_map/ppermute | solution.py:30
  7.6 1.0 %slice_bitcast_fusion.1 = bf16[512,256]{1,0:T(8,128)(2,1)S(1)} fusion(bf16[3,512,256]{2,1,0:T(8,128)(2,1)} %own.1), kind=kLoop, calls=%fused_computation.3 | loop fusion | bytes 524288 | tf_op jit(solution)/shard_map/squeeze | solution.py:147
  9.2 1.1 %copy-done.1 = bf16[3,512,256]{2,1,0:T(8,128)(2,1)S(1)} copy-done((bf16[3,512,256]{2,1,0:T(8,128)(2,1)S(1)}, bf16[3,512,256]{2,1,0:T(8,128)(2,1)}, u32[]{:S(2)}) %copy-start.1) | copy-done | bytes 786456
  10.4 3.1 %begin.1 = (f32[3,512,256]{2,1,0:T(8,128)S(1)}, bf16[3,256,512]{2,1,0:T(8,128)(2,1)S(1)}, bf16[3,512,1024]{2,1,0:T(8,128)(2,1)S(1)}) custom-call(bf16[3,512,2048]{2,1,0:T(8,128)(2,1)} %d.1, bf16[3,512,256]{2,1,0:T(8,128)(2,1)S(1)} %copy-done, bf16[3,512,256]{2,1,0:T(8,128)(2,1)S(1)} %collective-permute-done.core, bf16[3,512,256]{2,1,0:T(8,128)(2,1)S(1)} %copy-done.1), custom_call_target="tpu_custom_call" | custom-call | flops 1 | bytes 1 | tf_op jit(solution)/shard_map/begin/pallas_call | solution.py:151
  13.5 1.3 %collective-permute-start.13 = (bf16[512,256]{1,0:T(8,128)(2,1)S(1)}, bf16[512,256]{1,0:T(8,128)(2,1)S(1)}, u32[]{:S(2)}, u32[]{:S(2)}) collective-permute-start(bf16[512,256]{1,0:T(8,128)(2,1)S(1)} %slice_bitcast_fusion.1), channel_id=1, source_target_pairs={{0,2},{2,0},{1,3},{3,1},{4,6},{6,4},{5,7},{7,5},{8,10},{10,8},{9,1... | collective-permute-start | bytes 786440 | tf_op jit(solution)/shard_map/ppermute | solution.py:26
  15.7 0.7 %collective-permute-done.8 = f16[3,64,256]{2,1,0:T(8,128)(2,1)S(1)} collective-permute-done((f16[3,64,256]{2,1,0:T(8,128)(2,1)S(1)}, f16[3,64,256]{2,1,0:T(8,128)(2,1)S(1)}, u32[]{:S(2)}, u32[]{:S(2)}) %collective-permute-start.8) | collective-permute-done | bytes 98336 | tf_op jit(solution)/shard_map/ppermute | solution.py:22
  16.4 1.1 %collective-permute-start.9 = (f16[3,64,256]{2,1,0:T(8,128)(2,1)S(1)}, f16[3,64,256]{2,1,0:T(8,128)(2,1)S(1)}, u32[]{:S(2)}, u32[]{:S(2)}) collective-permute-start(f16[3,64,256]{2,1,0:T(8,128)(2,1)S(1)} %collective-permute-done.2), channel_id=1, source_target_pairs={{0,16},{4,20},{8,24},{12,28},{16,0},{20,4},{24,8},{28,12},{32,48},... | collective-permute-start | bytes 294920 | tf_op jit(solution)/shard_map/ppermute | solution.py:30
  17.7 0.7 %collective-permute-start.17 = (bf16[512,256]{1,0:T(8,128)(2,1)S(1)}, bf16[512,256]{1,0:T(8,128)(2,1)S(1)}, u32[]{:S(2)}, u32[]{:S(2)}) collective-permute-start(bf16[512,256]{1,0:T(8,128)(2,1)S(1)} %slice_bitcast_fusion), channel_id=1, source_target_pairs={{0,2},{2,0},{1,3},{3,1},{4,6},{6,4},{5,7},{7,5},{8,10},{10,8},{9,1... | collective-permute-start | bytes 786440 | tf_op jit(solution)/shard_map/ppermute | solution.py:26
  19.1 2.3 %collective-permute-done.9 = f16[3,64,256]{2,1,0:T(8,128)(2,1)S(1)} collective-permute-done((f16[3,64,256]{2,1,0:T(8,128)(2,1)S(1)}, f16[3,64,256]{2,1,0:T(8,128)(2,1)S(1)}, u32[]{:S(2)}, u32[]{:S(2)}) %collective-permute-start.9) | collective-permute-done | bytes 98336 | tf_op jit(solution)/shard_map/ppermute | solution.py:30
  21.4 1.3 %collective-permute-done.13.chip = bf16[512,256]{1,0:T(8,128)(2,1)S(1)} collective-permute-done((bf16[512,256]{1,0:T(8,128)(2,1)S(1)}, bf16[512,256]{1,0:T(8,128)(2,1)S(1)}, u32[]{:S(2)}, u32[]{:S(2)}) %collective-permute-start.13) | collective-permute-done | bytes 262176 | tf_op jit(solution)/shard_map/ppermute | solution.py:26
  24.5 0.7 %couple.1 = (bf16[3,768,256]{2,1,0:T(8,128)(2,1)S(1)}, bf16[3,128,768]{2,1,0:T(8,128)(2,1)S(1)}, f32[3,128,256]{2,1,0:T(8,128)S(1)}) custom-call(f32[4,2,3,64,256]{4,3,2,1,0:T(8,128)S(1)} %bitcast.37, f32[3,64,256]{2,1,0:T(8,128)S(1)} %copy-done.2, f32[3,64,256]{2,1,0:T(8,128)S(1)} %collective-permute-done.12.c_core), custom_call_target="tpu_custom_call" | custom-call | flops 1 | bytes 1 | tf_op jit(solution)/shard_map/couple/pallas_call | solution.py:190
  26.4 1.1 %merge0.1 = (f32[2,64,256]{2,1,0:T(8,128)S(1)}, bf16[2,64,256]{2,1,0:T(8,128)(2,1)S(1)}) custom-call(s32[3]{0:T(128)S(1)} %copy-done.3, f32[256,256]{1,0:T(8,128)S(1)} %eliminate0.1.s_own, f32[256,256]{1,0:T(8,128)S(1)} %collective-permute-done.6.s_core, bf16[3,768,256]{2,1,0:T(8,128)(2,1)S(1)} %get-tuple-element.35.m, ...), custom_call_target="tpu_custom_call" | custom-call | flops 1 | bytes 1 | tf_op jit(solution)/shard_map/merge0/pallas_call | solution.py:175
  28.2 1.1 %merge1.1 = (f32[2,64,256]{2,1,0:T(8,128)S(1)}, bf16[2,64,256]{2,1,0:T(8,128)(2,1)S(1)}) custom-call(s32[3]{0:T(128)S(1)} %copy-done.3, f32[256,256]{1,0:T(8,128)S(1)} %eliminate1.1.s_own, f32[256,256]{1,0:T(8,128)S(1)} %collective-permute-done.16.s_core, bf16[3,768,256]{2,1,0:T(8,128)(2,1)S(1)} %get-tuple-element.35.m, ...), custom_call_target="tpu_custom_call" | custom-call | flops 1 | bytes 1 | tf_op jit(solution)/shard_map/merge1/pallas_call | solution.py:175
  30.5 1.1 %collective-permute-start.21 = (bf16[2,2,64,256]{3,2,1,0:T(8,128)(2,1)S(1)}, bf16[2,2,64,256]{3,2,1,0:T(8,128)(2,1)S(1)}, u32[]{:S(2)}, u32[]{:S(2)}) collective-permute-start(bf16[2,2,64,256]{3,2,1,0:T(8,128)(2,1)S(1)} %pad_maximum_fusion), channel_id=1, source_target_pairs={{0,2},{2,0},{1,3},{3,1},{4,6},{6,4},{5,7},{7,5},{8,10},{10,8},{9,1... | collective-permute-start | bytes 393224 | tf_op jit(solution)/shard_map/ppermute | solution.py:26
  31.6 1.1 %merge2.1 = (f32[2,64,256]{2,1,0:T(8,128)S(1)}, bf16[2,64,256]{2,1,0:T(8,128)(2,1)S(1)}) custom-call(s32[3]{0:T(128)S(1)} %copy-done.3, f32[256,256]{1,0:T(8,128)S(1)} %eliminate2.1.s_own, f32[256,256]{1,0:T(8,128)S(1)} %collective-permute-done.20.s_core, bf16[3,768,256]{2,1,0:T(8,128)(2,1)S(1)} %get-tuple-element.35.m, ...), custom_call_target="tpu_custom_call" | custom-call | flops 1 | bytes 1 | tf_op jit(solution)/shard_map/merge2/pallas_call | solution.py:175
  32.8 1.1 %collective-permute-start.22 = (bf16[2,64,256]{2,1,0:T(8,128)(2,1)S(1)}, bf16[2,64,256]{2,1,0:T(8,128)(2,1)S(1)}, u32[]{:S(2)}, u32[]{:S(2)}) collective-permute-start(bf16[2,64,256]{2,1,0:T(8,128)(2,1)S(1)} %get-tuple-element.48), channel_id=1, source_target_pairs={{0,2},{2,0},{1,3},{3,1},{4,6},{6,4},{5,7},{7,5},{8,10},{10,8},{9,1... | collective-permute-start | bytes 196616 | tf_op jit(solution)/shard_map/ppermute | solution.py:26
  33.9 2.4 %collective-permute-done.21 = bf16[2,2,64,256]{3,2,1,0:T(8,128)(2,1)S(1)} collective-permute-done((bf16[2,2,64,256]{3,2,1,0:T(8,128)(2,1)S(1)}, bf16[2,2,64,256]{3,2,1,0:T(8,128)(2,1)S(1)}, u32[]{:S(2)}, u32[]{:S(2)}) %collective-permute-start.21) | collective-permute-done | bytes 131104 | tf_op jit(solution)/shard_map/ppermute | solution.py:26
  36.4 1.2 %collective-permute-done.22 = bf16[2,64,256]{2,1,0:T(8,128)(2,1)S(1)} collective-permute-done((bf16[2,64,256]{2,1,0:T(8,128)(2,1)S(1)}, bf16[2,64,256]{2,1,0:T(8,128)(2,1)S(1)}, u32[]{:S(2)}, u32[]{:S(2)}) %collective-permute-start.22) | collective-permute-done | bytes 65568 | tf_op jit(solution)/shard_map/ppermute | solution.py:26
  37.6 0.9 %collective-permute-start.23 = (bf16[3,64,256]{2,1,0:T(8,128)(2,1)S(1)}, bf16[3,64,256]{2,1,0:T(8,128)(2,1)S(1)}, u32[]{:S(2)}, u32[]{:S(2)}) collective-permute-start(bf16[3,64,256]{2,1,0:T(8,128)(2,1)S(1)} %fusion), channel_id=1, source_target_pairs={{0,16},{4,20},{8,24},{12,28},{16,0},{20,4},{24,8},{28,12},{32,48},... | collective-permute-start | bytes 294920 | tf_op jit(solution)/shard_map/ppermute | solution.py:30
  39.2 3.1 %collective-permute-done.23 = bf16[3,64,256]{2,1,0:T(8,128)(2,1)S(1)} collective-permute-done((bf16[3,64,256]{2,1,0:T(8,128)(2,1)S(1)}, bf16[3,64,256]{2,1,0:T(8,128)(2,1)S(1)}, u32[]{:S(2)}, u32[]{:S(2)}) %collective-permute-start.23) | collective-permute-done | bytes 98336 | tf_op jit(solution)/shard_map/ppermute | solution.py:30
  (62 shorter events, 8.6 us)
Async XLA Ops:
  0.6 8.0 %collective-permute-start = (bf16[3,512,256]{2,1,0:T(8,128)(2,1)}, bf16[3,512,256]{2,1,0:T(8,128)(2,1)S(1)}, u32[]{:S(2)}, u32[]{:S(2)}) collective-permute-start(bf16[3,512,256]{2,1,0:T(8,128)(2,1)} %own.1), channel_id=1, source_target_pairs={{0,1},{1,0},{2,3},{3,2},{4,5},{5,4},{6,7},{7,6},{8,9},{9,8},{10,11... | collective-permute-start | bytes 2359304 | tf_op jit(solution)/shard_map/ppermute | solution.py:22
  1.8 13.0 %collective-permute-start.1 = (bf16[512,256]{1,0:T(8,128)(2,1)S(1)}, bf16[512,256]{1,0:T(8,128)(2,1)S(1)}, u32[]{:S(2)}, u32[]{:S(2)}) collective-permute-start(bf16[512,256]{1,0:T(8,128)(2,1)S(1)} %slice_bitcast_fusion.2), channel_id=1, source_target_pairs={{0,2},{2,0},{1,3},{3,1},{4,6},{6,4},{5,7},{7,5},{8,10},{10,8},{9,1... | collective-permute-start | bytes 786440 | tf_op jit(solution)/shard_map/ppermute | solution.py:26
  5.8 7.7 %collective-permute-start.2 = (f16[3,64,256]{2,1,0:T(8,128)(2,1)S(1)}, f16[3,64,256]{2,1,0:T(8,128)(2,1)S(1)}, u32[]{:S(2)}, u32[]{:S(2)}) collective-permute-start(f16[3,64,256]{2,1,0:T(8,128)(2,1)S(1)} %get-tuple-element.51), channel_id=1, source_target_pairs={{0,2},{2,0},{1,3},{3,1},{4,6},{6,4},{5,7},{7,5},{8,10},{10,8},{9,1... | collective-permute-start | bytes 294920 | tf_op jit(solution)/shard_map/ppermute | solution.py:26
  5.9 8.9 %collective-permute-start.3 = (f16[3,64,256]{2,1,0:T(8,128)(2,1)S(1)}, f16[3,64,256]{2,1,0:T(8,128)(2,1)S(1)}, u32[]{:S(2)}, u32[]{:S(2)}) collective-permute-start(f16[3,64,256]{2,1,0:T(8,128)(2,1)S(1)} %get-tuple-element.51), channel_id=1, source_target_pairs={{0,16},{4,20},{8,24},{12,28},{16,0},{20,4},{24,8},{28,12},{32,48},... | collective-permute-start | bytes 294920 | tf_op jit(solution)/shard_map/ppermute | solution.py:30
  7.6 7.8 %collective-permute-start.7 = (f16[3,64,256]{2,1,0:T(8,128)(2,1)S(1)}, f16[3,64,256]{2,1,0:T(8,128)(2,1)S(1)}, u32[]{:S(2)}, u32[]{:S(2)}) collective-permute-start(f16[3,64,256]{2,1,0:T(8,128)(2,1)S(1)} %get-tuple-element.51), channel_id=1, source_target_pairs={{0,1},{1,0},{2,3},{3,2},{4,5},{5,4},{6,7},{7,6},{8,9},{9,8},{10,11... | collective-permute-start | bytes 294920 | tf_op jit(solution)/shard_map/ppermute | solution.py:22
  8.6 15.8 %collective-permute-start.12 = (f32[3,64,256]{2,1,0:T(8,128)}, f32[3,64,256]{2,1,0:T(8,128)S(1)}, u32[]{:S(2)}, u32[]{:S(2)}) collective-permute-start(f32[3,64,256]{2,1,0:T(8,128)} %c_own.1), channel_id=1, source_target_pairs={{0,1},{1,0},{2,3},{3,2},{4,5},{5,4},{6,7},{7,6},{8,9},{9,8},{10,11... | collective-permute-start | bytes 589832 | tf_op jit(solution)/shard_map/ppermute | solution.py:22
  13.5 9.3 %collective-permute-start.13 = (bf16[512,256]{1,0:T(8,128)(2,1)S(1)}, bf16[512,256]{1,0:T(8,128)(2,1)S(1)}, u32[]{:S(2)}, u32[]{:S(2)}) collective-permute-start(bf16[512,256]{1,0:T(8,128)(2,1)S(1)} %slice_bitcast_fusion.1), channel_id=1, source_target_pairs={{0,2},{2,0},{1,3},{3,1},{4,6},{6,4},{5,7},{7,5},{8,10},{10,8},{9,1... | collective-permute-start | bytes 786440 | tf_op jit(solution)/shard_map/ppermute | solution.py:26
  14.8 2.7 %collective-permute-start.4 = (bf16[256,256]{1,0:T(8,128)(2,1)S(1)}, bf16[256,256]{1,0:T(8,128)(2,1)S(1)}, u32[]{:S(2)}, u32[]{:S(2)}) collective-permute-start(bf16[256,256]{1,0:T(8,128)(2,1)S(1)} %get-tuple-element.57), channel_id=1, source_target_pairs={{0,1},{1,0},{2,3},{3,2},{4,5},{5,4},{6,7},{7,6},{8,9},{9,8},{10,11... | collective-permute-start | bytes 393224 | tf_op jit(solution)/shard_map/ppermute | solution.py:22
  14.9 1.5 %collective-permute-start.8 = (f16[3,64,256]{2,1,0:T(8,128)(2,1)S(1)}, f16[3,64,256]{2,1,0:T(8,128)(2,1)S(1)}, u32[]{:S(2)}, u32[]{:S(2)}) collective-permute-start(f16[3,64,256]{2,1,0:T(8,128)(2,1)S(1)} %collective-permute-done.3), channel_id=1, source_target_pairs={{0,1},{1,0},{2,3},{3,2},{4,5},{5,4},{6,7},{7,6},{8,9},{9,8},{10,11... | collective-permute-start | bytes 294920 | tf_op jit(solution)/shard_map/ppermute | solution.py:22
  15.5 2.2 %collective-permute-start.5 = (bf16[256,256]{1,0:T(8,128)(2,1)S(1)}, bf16[256,256]{1,0:T(8,128)(2,1)S(1)}, u32[]{:S(2)}, u32[]{:S(2)}) collective-permute-start(bf16[256,256]{1,0:T(8,128)(2,1)S(1)} %get-tuple-element.56), channel_id=1, source_target_pairs={{0,1},{1,0},{2,3},{3,2},{4,5},{5,4},{6,7},{7,6},{8,9},{9,8},{10,11... | collective-permute-start | bytes 393224 | tf_op jit(solution)/shard_map/ppermute | solution.py:22
  16.4 5.0 %collective-permute-start.9 = (f16[3,64,256]{2,1,0:T(8,128)(2,1)S(1)}, f16[3,64,256]{2,1,0:T(8,128)(2,1)S(1)}, u32[]{:S(2)}, u32[]{:S(2)}) collective-permute-start(f16[3,64,256]{2,1,0:T(8,128)(2,1)S(1)} %collective-permute-done.2), channel_id=1, source_target_pairs={{0,16},{4,20},{8,24},{12,28},{16,0},{20,4},{24,8},{28,12},{32,48},... | collective-permute-start | bytes 294920 | tf_op jit(solution)/shard_map/ppermute | solution.py:30
  17.6 5.3 %collective-permute-start.10 = (f16[3,64,256]{2,1,0:T(8,128)(2,1)S(1)}, f16[3,64,256]{2,1,0:T(8,128)(2,1)S(1)}, u32[]{:S(2)}, u32[]{:S(2)}) collective-permute-start(f16[3,64,256]{2,1,0:T(8,128)(2,1)S(1)} %collective-permute-done.2), channel_id=1, source_target_pairs={{0,1},{1,0},{2,3},{3,2},{4,5},{5,4},{6,7},{7,6},{8,9},{9,8},{10,11... | collective-permute-start | bytes 294920 | tf_op jit(solution)/shard_map/ppermute | solution.py:22
  17.7 9.8 %collective-permute-start.17 = (bf16[512,256]{1,0:T(8,128)(2,1)S(1)}, bf16[512,256]{1,0:T(8,128)(2,1)S(1)}, u32[]{:S(2)}, u32[]{:S(2)}) collective-permute-start(bf16[512,256]{1,0:T(8,128)(2,1)S(1)} %slice_bitcast_fusion), channel_id=1, source_target_pairs={{0,2},{2,0},{1,3},{3,1},{4,6},{6,4},{5,7},{7,5},{8,10},{10,8},{9,1... | collective-permute-start | bytes 786440 | tf_op jit(solution)/shard_map/ppermute | solution.py:26
  21.4 4.9 %collective-permute-start.6 = (f32[256,256]{1,0:T(8,128)S(1)}, f32[256,256]{1,0:T(8,128)S(1)}, u32[]{:S(2)}, u32[]{:S(2)}) collective-permute-start(f32[256,256]{1,0:T(8,128)S(1)} %eliminate0.1.s_own), channel_id=1, source_target_pairs={{0,1},{1,0},{2,3},{3,2},{4,5},{5,4},{6,7},{7,6},{8,9},{9,8},{10,11... | collective-permute-start | bytes 786440 | tf_op jit(solution)/shard_map/ppermute | solution.py:22
  22.8 1.3 %collective-permute-start.11 = (f16[3,64,256]{2,1,0:T(8,128)(2,1)S(1)}, f16[3,64,256]{2,1,0:T(8,128)(2,1)S(1)}, u32[]{:S(2)}, u32[]{:S(2)}) collective-permute-start(f16[3,64,256]{2,1,0:T(8,128)(2,1)S(1)} %collective-permute-done.9), channel_id=1, source_target_pairs={{0,1},{1,0},{2,3},{3,2},{4,5},{5,4},{6,7},{7,6},{8,9},{9,8},{10,11... | collective-permute-start | bytes 294920 | tf_op jit(solution)/shard_map/ppermute | solution.py:22
  22.9 2.3 %collective-permute-start.14 = (bf16[256,256]{1,0:T(8,128)(2,1)S(1)}, bf16[256,256]{1,0:T(8,128)(2,1)S(1)}, u32[]{:S(2)}, u32[]{:S(2)}) collective-permute-start(bf16[256,256]{1,0:T(8,128)(2,1)S(1)} %get-tuple-element.55), channel_id=1, source_target_pairs={{0,1},{1,0},{2,3},{3,2},{4,5},{5,4},{6,7},{7,6},{8,9},{9,8},{10,11... | collective-permute-start | bytes 393224 | tf_op jit(solution)/shard_map/ppermute | solution.py:22
  24.1 1.3 %collective-permute-start.15 = (bf16[256,256]{1,0:T(8,128)(2,1)S(1)}, bf16[256,256]{1,0:T(8,128)(2,1)S(1)}, u32[]{:S(2)}, u32[]{:S(2)}) collective-permute-start(bf16[256,256]{1,0:T(8,128)(2,1)S(1)} %get-tuple-element.54), channel_id=1, source_target_pairs={{0,1},{1,0},{2,3},{3,2},{4,5},{5,4},{6,7},{7,6},{8,9},{9,8},{10,11... | collective-permute-start | bytes 393224 | tf_op jit(solution)/shard_map/ppermute | solution.py:22
  26.1 2.0 %collective-permute-start.16 = (f32[256,256]{1,0:T(8,128)S(1)}, f32[256,256]{1,0:T(8,128)S(1)}, u32[]{:S(2)}, u32[]{:S(2)}) collective-permute-start(f32[256,256]{1,0:T(8,128)S(1)} %eliminate1.1.s_own), channel_id=1, source_target_pairs={{0,1},{1,0},{2,3},{3,2},{4,5},{5,4},{6,7},{7,6},{8,9},{9,8},{10,11... | collective-permute-start | bytes 786440 | tf_op jit(solution)/shard_map/ppermute | solution.py:22
  27.6 1.8 %collective-permute-start.18 = (bf16[256,256]{1,0:T(8,128)(2,1)S(1)}, bf16[256,256]{1,0:T(8,128)(2,1)S(1)}, u32[]{:S(2)}, u32[]{:S(2)}) collective-permute-start(bf16[256,256]{1,0:T(8,128)(2,1)S(1)} %get-tuple-element.53), channel_id=1, source_target_pairs={{0,1},{1,0},{2,3},{3,2},{4,5},{5,4},{6,7},{7,6},{8,9},{9,8},{10,11... | collective-permute-start | bytes 393224 | tf_op jit(solution)/shard_map/ppermute | solution.py:22
  28.0 1.3 %collective-permute-start.19 = (bf16[256,256]{1,0:T(8,128)(2,1)S(1)}, bf16[256,256]{1,0:T(8,128)(2,1)S(1)}, u32[]{:S(2)}, u32[]{:S(2)}) collective-permute-start(bf16[256,256]{1,0:T(8,128)(2,1)S(1)} %get-tuple-element.52), channel_id=1, source_target_pairs={{0,1},{1,0},{2,3},{3,2},{4,5},{5,4},{6,7},{7,6},{8,9},{9,8},{10,11... | collective-permute-start | bytes 393224 | tf_op jit(solution)/shard_map/ppermute | solution.py:22
  30.0 1.6 %collective-permute-start.20 = (f32[256,256]{1,0:T(8,128)S(1)}, f32[256,256]{1,0:T(8,128)S(1)}, u32[]{:S(2)}, u32[]{:S(2)}) collective-permute-start(f32[256,256]{1,0:T(8,128)S(1)} %eliminate2.1.s_own), channel_id=1, source_target_pairs={{0,1},{1,0},{2,3},{3,2},{4,5},{5,4},{6,7},{7,6},{8,9},{9,8},{10,11... | collective-permute-start | bytes 786440 | tf_op jit(solution)/shard_map/ppermute | solution.py:22
  30.5 5.9 %collective-permute-start.21 = (bf16[2,2,64,256]{3,2,1,0:T(8,128)(2,1)S(1)}, bf16[2,2,64,256]{3,2,1,0:T(8,128)(2,1)S(1)}, u32[]{:S(2)}, u32[]{:S(2)}) collective-permute-start(bf16[2,2,64,256]{3,2,1,0:T(8,128)(2,1)S(1)} %pad_maximum_fusion), channel_id=1, source_target_pairs={{0,2},{2,0},{1,3},{3,1},{4,6},{6,4},{5,7},{7,5},{8,10},{10,8},{9,1... | collective-permute-start | bytes 393224 | tf_op jit(solution)/shard_map/ppermute | solution.py:26
  32.8 4.7 %collective-permute-start.22 = (bf16[2,64,256]{2,1,0:T(8,128)(2,1)S(1)}, bf16[2,64,256]{2,1,0:T(8,128)(2,1)S(1)}, u32[]{:S(2)}, u32[]{:S(2)}) collective-permute-start(bf16[2,64,256]{2,1,0:T(8,128)(2,1)S(1)} %get-tuple-element.48), channel_id=1, source_target_pairs={{0,2},{2,0},{1,3},{3,1},{4,6},{6,4},{5,7},{7,5},{8,10},{10,8},{9,1... | collective-permute-start | bytes 196616 | tf_op jit(solution)/shard_map/ppermute | solution.py:26
  37.6 4.7 %collective-permute-start.23 = (bf16[3,64,256]{2,1,0:T(8,128)(2,1)S(1)}, bf16[3,64,256]{2,1,0:T(8,128)(2,1)S(1)}, u32[]{:S(2)}, u32[]{:S(2)}) collective-permute-start(bf16[3,64,256]{2,1,0:T(8,128)(2,1)S(1)} %fusion), channel_id=1, source_target_pairs={{0,16},{4,20},{8,24},{12,28},{16,0},{20,4},{24,8},{28,12},{32,48},... | collective-permute-start | bytes 294920 | tf_op jit(solution)/shard_map/ppermute | solution.py:30
  (4 other events, 12.6 us)

commit v5 on v4

--- a/solution.py
+++ b/solution.py
@@ -140,8 +140,8 @@
     first = column_basis[0]
     chip_left = [to_chip(first)]
     transfer, ranks_late = lax.optimization_barrier((transfer, ranks, first))[:2]
-    rows = q * part + jnp.arange(part, dtype=jnp.int32)
-    live = (rows[None, :] < ranks_late[:, None])[:, :, None]
+    rows = lax.broadcasted_iota(jnp.int32, transfer.shape, 1) + q * part
+    live = rows < ranks_late[:, None, None]
     m_own = jnp.where(live, transfer * SCALE, 0.0).astype(F16)
     m_chip, sib_own = to_chip(m_own), to_sibling(m_own)
     chip_left.append(to_chip(after(column_basis, m_own)[1]))
@@ -156,7 +156,7 @@
         [pltpu.VMEM((nodes, depth, 2 * depth), BF16), pltpu.SemaphoreType.DMA((2, nodes))],
         45,
     )(diagonal_inverses, column_basis, core_left, row_basis)
-    chip_left[0], m_chip, sib_own, last = lax.optimization_barrier((chip_left[0], m_chip, sib_own, column_basis, e))[:4]
+    chip_left[0], sib_own, last = lax.optimization_barrier((chip_left[0], sib_own, column_basis, e))[:3]
     chip_left.append(to_chip(last[2]))
 
     def cross(left):

time: 43.4 us -> 42.6 us (0.982)
  starting transfers between devices: 14 us -> 12.8 us
  waiting for transfers between devices: 12 us -> 13.1 us
  other arithmetic: 2.68 us -> 1.95 us
    ppermute x3, waiting for transfers between devices: 5.39 us -> 3.07 us  [to_sibling(): lax.ppermute(block, 'row', [(n, n ^ 1 << BIT) for n in range(lax.axis_siz...]
    ppermute x6, waiting for transfers between devices: 4.97 us -> 6.97 us  [to_chip(): return lax.ppermute(block, 'col', CHIP)]
    ppermute x15, waiting for transfers between devices: 1.64 us -> 3.06 us  [to_core(): return lax.ppermute(block, 'col', CORE)]
    lt x1 -> x0, other arithmetic: 0.73 us -> none  [shards(): live = (rows[None, :] < ranks_late[:, None])[:, :, None]]
    ppermute x6, starting transfers between devices: 6.61 us -> 5.9 us  [to_chip(): return lax.ppermute(block, 'col', CHIP)]
    ppermute x3, starting transfers between devices: 3.78 us -> 3.07 us  [to_sibling(): lax.ppermute(block, 'row', [(n, n ^ 1 << BIT) for n in range(lax.axis_siz...]
  transfers between devices with their start and end apart: 24 -> 24, of which waited for: 9 -> 11; matrix products, arithmetic and copies ran while one was open for 11% -> 10% of each run, Pallas kernels for 20% -> 20%
where the time goes in v5:
time: 42.6 us; the launch traced here: 42.2 us
  waiting for transfers between devices  13.1 us (31%)
  starting transfers between devices  12.8 us (30%)
  Pallas kernels  9.31 us (22%)
  local copies, waits for them, and re-layouts  4.06 us (10%)
  other arithmetic  1.95 us (5%)
  between operations  0.93 us (2%)
    ppermute x6, waiting for transfers between devices, to_chip(): return lax.ppermute(block, 'col', CHIP)  6.97 us
    ppermute x6, starting transfers between devices, to_chip(): return lax.ppermute(block, 'col', CHIP)  5.9 us
    ppermute x15, starting transfers between devices, to_core(): return lax.ppermute(block, 'col', CORE)  3.87 us
    pallas_call x3, Pallas kernels, merge(): call(functools.partial(merge_kernel, n), [shape((2, part, width), F32), s...  3.44 us
    pallas_call x1, Pallas kernels, shards(): call(begin_kernel, [shape((nodes, depth, width), F32), shape((nodes, widt...  3.14 us
    ppermute x3, starting transfers between devices, to_sibling(): lax.ppermute(block, 'row', [(n, n ^ 1 << BIT) for n in range(lax.axis_siz...  3.07 us
    ppermute x3, waiting for transfers between devices, to_sibling(): lax.ppermute(block, 'row', [(n, n ^ 1 << BIT) for n in range(lax.axis_siz...  3.07 us
    ppermute x15, waiting for transfers between devices, to_core(): return lax.ppermute(block, 'col', CORE)  3.06 us
  transfers between devices with their start and end apart: 24, of which 11 were waited for; matrix products, arithmetic and copies ran while one was open for 10% of the time, Pallas kernels for 20%

profile of v5, /device:TPU:8, one launch (start us, length us, event | category | flops | bytes accessed | tf_op | source)
XLA Modules:
  0.0 42.2 jit_solution(5591762270997013408)
XLA Ops:
  0.7 1.0 %slice_bitcast_fusion.2 = bf16[512,256]{1,0:T(8,128)(2,1)S(1)} fusion(bf16[3,512,256]{2,1,0:T(8,128)(2,1)} %own.1), kind=kLoop, calls=%fused_computation.4 | loop fusion | bytes 524288 | tf_op jit(solution)/shard_map/squeeze | solution.py:140
  1.8 2.3 %collective-permute-start.1 = (bf16[512,256]{1,0:T(8,128)(2,1)S(1)}, bf16[512,256]{1,0:T(8,128)(2,1)S(1)}, u32[]{:S(2)}, u32[]{:S(2)}) collective-permute-start(bf16[512,256]{1,0:T(8,128)(2,1)S(1)} %slice_bitcast_fusion.2), channel_id=1, source_target_pairs={{0,2},{2,0},{1,3},{3,1},{4,6},{6,4},{5,7},{7,5},{8,10},{10,8},{9,1... | collective-permute-start | bytes 786440 | tf_op jit(solution)/shard_map/ppermute | solution.py:26
  4.0 1.0 %bitcast_dynamic-update-slice_fusion.7 = (f16[8,3,64,256]{3,2,1,0:T(8,128)(2,1)S(1)}, f16[3,64,256]{2,1,0:T(8,128)(2,1)S(1)}) fusion(f32[3,64,256]{2,1,0:T(8,128)} %param.9, s32[3]{0:T(128)} %ranks.5, s32[64]{0:T(128)S(1)} %iota_add_fusion), kind=kLoop, calls=%fused_computation.18 | loop fusion | flops 196607 | bytes 393484
  5.3 1.6 %collective-permute-start.8 = (f16[3,64,256]{2,1,0:T(8,128)(2,1)S(1)}, f16[3,64,256]{2,1,0:T(8,128)(2,1)S(1)}, u32[]{:S(2)}, u32[]{:S(2)}) collective-permute-start(f16[3,64,256]{2,1,0:T(8,128)(2,1)S(1)} %get-tuple-element.49), channel_id=1, source_target_pairs={{0,2},{2,0},{1,3},{3,1},{4,6},{6,4},{5,7},{7,5},{8,10},{10,8},{9,1... | collective-permute-start | bytes 294920 | tf_op jit(solution)/shard_map/ppermute | solution.py:26
  6.9 1.0 %slice_bitcast_fusion.1 = bf16[512,256]{1,0:T(8,128)(2,1)S(1)} fusion(bf16[3,512,256]{2,1,0:T(8,128)(2,1)} %own.1), kind=kLoop, calls=%fused_computation.3 | loop fusion | bytes 524288 | tf_op jit(solution)/shard_map/squeeze | solution.py:147
  8.5 1.1 %copy-done.1 = bf16[3,512,256]{2,1,0:T(8,128)(2,1)S(1)} copy-done((bf16[3,512,256]{2,1,0:T(8,128)(2,1)S(1)}, bf16[3,512,256]{2,1,0:T(8,128)(2,1)}, u32[]{:S(2)}) %copy-start.1) | copy-done | bytes 786456
  9.6 3.1 %begin.1 = (f32[3,512,256]{2,1,0:T(8,128)S(1)}, bf16[3,256,512]{2,1,0:T(8,128)(2,1)S(1)}, bf16[3,512,1024]{2,1,0:T(8,128)(2,1)S(1)}) custom-call(bf16[3,512,2048]{2,1,0:T(8,128)(2,1)} %d.1, bf16[3,512,256]{2,1,0:T(8,128)(2,1)S(1)} %copy-done, bf16[3,512,256]{2,1,0:T(8,128)(2,1)S(1)} %collective-permute-done.core, bf16[3,512,256]{2,1,0:T(8,128)(2,1)S(1)} %copy-done.1), custom_call_target="tpu_custom_call" | custom-call | flops 1 | bytes 1 | tf_op jit(solution)/shard_map/begin/pallas_call | solution.py:151
  13.3 1.8 %collective-permute-start.9 = (f16[3,64,256]{2,1,0:T(8,128)(2,1)S(1)}, f16[3,64,256]{2,1,0:T(8,128)(2,1)S(1)}, u32[]{:S(2)}, u32[]{:S(2)}) collective-permute-start(f16[3,64,256]{2,1,0:T(8,128)(2,1)S(1)} %collective-permute-done.8), channel_id=1, source_target_pairs={{0,16},{4,20},{8,24},{12,28},{16,0},{20,4},{24,8},{28,12},{32,48},... | collective-permute-start | bytes 294920 | tf_op jit(solution)/shard_map/ppermute | solution.py:30
  18.1 0.7 %eliminate0.1.s_own = f32[256,256]{1,0:T(8,128)S(1)} custom-call(f32[3,512,256]{2,1,0:T(8,128)S(1)} %get-tuple-element.40.e, bf16[3,512,1024]{2,1,0:T(8,128)(2,1)S(1)} %get-tuple-element.26.d, bf16[512,256]{1,0:T(8,128)(2,1)S(1)} %collective-permute-done.1.chip, bf16[256,256]{1,0:T(8,128)(2,1)S(1)} %collective-permute-done.3.cross_a, ...), custom_call_target="tpu_custom_call" | custom-call | flops 1 | bytes 1 | tf_op jit(solution)/shard_map/eliminate0/pallas_call | solution.py:167
  18.9 2.6 %collective-permute-done.13.chip = bf16[512,256]{1,0:T(8,128)(2,1)S(1)} collective-permute-done((bf16[512,256]{1,0:T(8,128)(2,1)S(1)}, bf16[512,256]{1,0:T(8,128)(2,1)S(1)}, u32[]{:S(2)}, u32[]{:S(2)}) %collective-permute-start.13) | collective-permute-done | bytes 262176 | tf_op jit(solution)/shard_map/ppermute | solution.py:26
  23.1 0.7 %couple.1 = (bf16[3,768,256]{2,1,0:T(8,128)(2,1)S(1)}, bf16[3,128,768]{2,1,0:T(8,128)(2,1)S(1)}, f32[3,128,256]{2,1,0:T(8,128)S(1)}) custom-call(f32[4,2,3,64,256]{4,3,2,1,0:T(8,128)S(1)} %bitcast.37, f32[3,64,256]{2,1,0:T(8,128)S(1)} %copy-done.2, f32[3,64,256]{2,1,0:T(8,128)S(1)} %collective-permute-done.12.c_core), custom_call_target="tpu_custom_call" | custom-call | flops 1 | bytes 1 | tf_op jit(solution)/shard_map/couple/pallas_call | solution.py:190
  24.1 0.7 %eliminate1.1.s_own = f32[256,256]{1,0:T(8,128)S(1)} custom-call(f32[3,512,256]{2,1,0:T(8,128)S(1)} %get-tuple-element.40.e, bf16[3,512,1024]{2,1,0:T(8,128)(2,1)S(1)} %get-tuple-element.26.d, bf16[512,256]{1,0:T(8,128)(2,1)S(1)} %collective-permute-done.13.chip, bf16[256,256]{1,0:T(8,128)(2,1)S(1)} %collective-permute-done.14.cross_a, ...), custom_call_target="tpu_custom_call" | custom-call | flops 1 | bytes 1 | tf_op jit(solution)/shard_map/eliminate1/pallas_call | solution.py:167
  25.0 1.1 %merge0.1 = (f32[2,64,256]{2,1,0:T(8,128)S(1)}, bf16[2,64,256]{2,1,0:T(8,128)(2,1)S(1)}) custom-call(s32[3]{0:T(128)S(1)} %copy-done.3, f32[256,256]{1,0:T(8,128)S(1)} %eliminate0.1.s_own, f32[256,256]{1,0:T(8,128)S(1)} %collective-permute-done.5.s_core, bf16[3,768,256]{2,1,0:T(8,128)(2,1)S(1)} %get-tuple-element.33.m, ...), custom_call_target="tpu_custom_call" | custom-call | flops 1 | bytes 1 | tf_op jit(solution)/shard_map/merge0/pallas_call | solution.py:175
  27.4 1.1 %merge1.1 = (f32[2,64,256]{2,1,0:T(8,128)S(1)}, bf16[2,64,256]{2,1,0:T(8,128)(2,1)S(1)}) custom-call(s32[3]{0:T(128)S(1)} %copy-done.3, f32[256,256]{1,0:T(8,128)S(1)} %eliminate1.1.s_own, f32[256,256]{1,0:T(8,128)S(1)} %collective-permute-done.16.s_core, bf16[3,768,256]{2,1,0:T(8,128)(2,1)S(1)} %get-tuple-element.33.m, ...), custom_call_target="tpu_custom_call" | custom-call | flops 1 | bytes 1 | tf_op jit(solution)/shard_map/merge1/pallas_call | solution.py:175
  28.5 0.7 %eliminate2.1.s_own = f32[256,256]{1,0:T(8,128)S(1)} custom-call(f32[3,512,256]{2,1,0:T(8,128)S(1)} %get-tuple-element.40.e, bf16[3,512,1024]{2,1,0:T(8,128)(2,1)S(1)} %get-tuple-element.26.d, bf16[512,256]{1,0:T(8,128)(2,1)S(1)} %collective-permute-done.17.chip, bf16[256,256]{1,0:T(8,128)(2,1)S(1)} %collective-permute-done.18.cross_a, ...), custom_call_target="tpu_custom_call" | custom-call | flops 1 | bytes 1 | tf_op jit(solution)/shard_map/eliminate2/pallas_call | solution.py:167
  30.0 0.8 %collective-permute-done.20.s_core = f32[256,256]{1,0:T(8,128)S(1)} collective-permute-done((f32[256,256]{1,0:T(8,128)S(1)}, f32[256,256]{1,0:T(8,128)S(1)}, u32[]{:S(2)}, u32[]{:S(2)}) %collective-permute-start.20) | collective-permute-done | bytes 262176 | tf_op jit(solution)/shard_map/ppermute | solution.py:22
  30.8 1.1 %merge2.1 = (f32[2,64,256]{2,1,0:T(8,128)S(1)}, bf16[2,64,256]{2,1,0:T(8,128)(2,1)S(1)}) custom-call(s32[3]{0:T(128)S(1)} %copy-done.3, f32[256,256]{1,0:T(8,128)S(1)} %eliminate2.1.s_own, f32[256,256]{1,0:T(8,128)S(1)} %collective-permute-done.20.s_core, bf16[3,768,256]{2,1,0:T(8,128)(2,1)S(1)} %get-tuple-element.33.m, ...), custom_call_target="tpu_custom_call" | custom-call | flops 1 | bytes 1 | tf_op jit(solution)/shard_map/merge2/pallas_call | solution.py:175
  32.0 0.9 %collective-permute-start.22 = (bf16[2,64,256]{2,1,0:T(8,128)(2,1)S(1)}, bf16[2,64,256]{2,1,0:T(8,128)(2,1)S(1)}, u32[]{:S(2)}, u32[]{:S(2)}) collective-permute-start(bf16[2,64,256]{2,1,0:T(8,128)(2,1)S(1)} %get-tuple-element.46), channel_id=1, source_target_pairs={{0,2},{2,0},{1,3},{3,1},{4,6},{6,4},{5,7},{7,5},{8,10},{10,8},{9,1... | collective-permute-start | bytes 196616 | tf_op jit(solution)/shard_map/ppermute | solution.py:26
  32.9 2.9 %collective-permute-done.21 = bf16[2,2,64,256]{3,2,1,0:T(8,128)(2,1)S(1)} collective-permute-done((bf16[2,2,64,256]{3,2,1,0:T(8,128)(2,1)S(1)}, bf16[2,2,64,256]{3,2,1,0:T(8,128)(2,1)S(1)}, u32[]{:S(2)}, u32[]{:S(2)}) %collective-permute-start.21) | collective-permute-done | bytes 131104 | tf_op jit(solution)/shard_map/ppermute | solution.py:26
  35.7 1.0 %collective-permute-done.22 = bf16[2,64,256]{2,1,0:T(8,128)(2,1)S(1)} collective-permute-done((bf16[2,64,256]{2,1,0:T(8,128)(2,1)S(1)}, bf16[2,64,256]{2,1,0:T(8,128)(2,1)S(1)}, u32[]{:S(2)}, u32[]{:S(2)}) %collective-permute-start.22) | collective-permute-done | bytes 65568 | tf_op jit(solution)/shard_map/ppermute | solution.py:26
  36.8 1.0 %collective-permute-start.23 = (bf16[3,64,256]{2,1,0:T(8,128)(2,1)S(1)}, bf16[3,64,256]{2,1,0:T(8,128)(2,1)S(1)}, u32[]{:S(2)}, u32[]{:S(2)}) collective-permute-start(bf16[3,64,256]{2,1,0:T(8,128)(2,1)S(1)} %fusion), channel_id=1, source_target_pairs={{0,16},{4,20},{8,24},{12,28},{16,0},{20,4},{24,8},{28,12},{32,48},... | collective-permute-start | bytes 294920 | tf_op jit(solution)/shard_map/ppermute | solution.py:30
  37.7 0.7 %slice_bitcast_fusion.4 = f32[3,64,256]{2,1,0:T(8,128)} fusion(f32[3,2,64,256]{3,2,1,0:T(8,128)S(1)} %maximum_add_fusion), kind=kLoop, calls=%fused_computation.6 | loop fusion | bytes 393216 | tf_op jit(solution)/shard_map/squeeze | solution.py:211
  38.4 3.1 %collective-permute-done.23 = bf16[3,64,256]{2,1,0:T(8,128)(2,1)S(1)} collective-permute-done((bf16[3,64,256]{2,1,0:T(8,128)(2,1)S(1)}, bf16[3,64,256]{2,1,0:T(8,128)(2,1)S(1)}, u32[]{:S(2)}, u32[]{:S(2)}) %collective-permute-start.23) | collective-permute-done | bytes 98336 | tf_op jit(solution)/shard_map/ppermute | solution.py:30
  41.5 0.7 %convert_add_fusion = f32[3,64,256]{2,1,0:T(8,128)} fusion(bf16[3,64,256]{2,1,0:T(8,128)(2,1)S(1)} %collective-permute-done.23, f32[3,2,64,256]{3,2,1,0:T(8,128)S(1)} %maximum_add_fusion), kind=kLoop, calls=%fused_computation.7 | loop fusion | flops 98304 | bytes 491520 | tf_op jit(solution)/shard_map/add | solution.py:212
  (61 shorter events, 8.6 us)
Async XLA Ops:
  0.6 7.3 %collective-permute-start = (bf16[3,512,256]{2,1,0:T(8,128)(2,1)}, bf16[3,512,256]{2,1,0:T(8,128)(2,1)S(1)}, u32[]{:S(2)}, u32[]{:S(2)}) collective-permute-start(bf16[3,512,256]{2,1,0:T(8,128)(2,1)} %own.1), channel_id=1, source_target_pairs={{0,1},{1,0},{2,3},{3,2},{4,5},{5,4},{6,7},{7,6},{8,9},{9,8},{10,11... | collective-permute-start | bytes 2359304 | tf_op jit(solution)/shard_map/ppermute | solution.py:22
  1.8 13.4 %collective-permute-start.1 = (bf16[512,256]{1,0:T(8,128)(2,1)S(1)}, bf16[512,256]{1,0:T(8,128)(2,1)S(1)}, u32[]{:S(2)}, u32[]{:S(2)}) collective-permute-start(bf16[512,256]{1,0:T(8,128)(2,1)S(1)} %slice_bitcast_fusion.2), channel_id=1, source_target_pairs={{0,2},{2,0},{1,3},{3,1},{4,6},{6,4},{5,7},{7,5},{8,10},{10,8},{9,1... | collective-permute-start | bytes 786440 | tf_op jit(solution)/shard_map/ppermute | solution.py:26
  5.1 7.7 %collective-permute-start.2 = (f16[3,64,256]{2,1,0:T(8,128)(2,1)S(1)}, f16[3,64,256]{2,1,0:T(8,128)(2,1)S(1)}, u32[]{:S(2)}, u32[]{:S(2)}) collective-permute-start(f16[3,64,256]{2,1,0:T(8,128)(2,1)S(1)} %get-tuple-element.49), channel_id=1, source_target_pairs={{0,16},{4,20},{8,24},{12,28},{16,0},{20,4},{24,8},{28,12},{32,48},... | collective-permute-start | bytes 294920 | tf_op jit(solution)/shard_map/ppermute | solution.py:30
  5.3 8.0 %collective-permute-start.8 = (f16[3,64,256]{2,1,0:T(8,128)(2,1)S(1)}, f16[3,64,256]{2,1,0:T(8,128)(2,1)S(1)}, u32[]{:S(2)}, u32[]{:S(2)}) collective-permute-start(f16[3,64,256]{2,1,0:T(8,128)(2,1)S(1)} %get-tuple-element.49), channel_id=1, source_target_pairs={{0,2},{2,0},{1,3},{3,1},{4,6},{6,4},{5,7},{7,5},{8,10},{10,8},{9,1... | collective-permute-start | bytes 294920 | tf_op jit(solution)/shard_map/ppermute | solution.py:26
  6.9 8.4 %collective-permute-start.6 = (f16[3,64,256]{2,1,0:T(8,128)(2,1)S(1)}, f16[3,64,256]{2,1,0:T(8,128)(2,1)S(1)}, u32[]{:S(2)}, u32[]{:S(2)}) collective-permute-start(f16[3,64,256]{2,1,0:T(8,128)(2,1)S(1)} %get-tuple-element.49), channel_id=1, source_target_pairs={{0,1},{1,0},{2,3},{3,2},{4,5},{5,4},{6,7},{7,6},{8,9},{9,8},{10,11... | collective-permute-start | bytes 294920 | tf_op jit(solution)/shard_map/ppermute | solution.py:22
  7.9 15.2 %collective-permute-start.12 = (f32[3,64,256]{2,1,0:T(8,128)}, f32[3,64,256]{2,1,0:T(8,128)S(1)}, u32[]{:S(2)}, u32[]{:S(2)}) collective-permute-start(f32[3,64,256]{2,1,0:T(8,128)} %c_own.1), channel_id=1, source_target_pairs={{0,1},{1,0},{2,3},{3,2},{4,5},{5,4},{6,7},{7,6},{8,9},{9,8},{10,11... | collective-permute-start | bytes 589832 | tf_op jit(solution)/shard_map/ppermute | solution.py:22
  12.8 8.7 %collective-permute-start.13 = (bf16[512,256]{1,0:T(8,128)(2,1)S(1)}, bf16[512,256]{1,0:T(8,128)(2,1)S(1)}, u32[]{:S(2)}, u32[]{:S(2)}) collective-permute-start(bf16[512,256]{1,0:T(8,128)(2,1)S(1)} %slice_bitcast_fusion.1), channel_id=1, source_target_pairs={{0,2},{2,0},{1,3},{3,1},{4,6},{6,4},{5,7},{7,5},{8,10},{10,8},{9,1... | collective-permute-start | bytes 786440 | tf_op jit(solution)/shard_map/ppermute | solution.py:26
  13.3 5.4 %collective-permute-start.9 = (f16[3,64,256]{2,1,0:T(8,128)(2,1)S(1)}, f16[3,64,256]{2,1,0:T(8,128)(2,1)S(1)}, u32[]{:S(2)}, u32[]{:S(2)}) collective-permute-start(f16[3,64,256]{2,1,0:T(8,128)(2,1)S(1)} %collective-permute-done.8), channel_id=1, source_target_pairs={{0,16},{4,20},{8,24},{12,28},{16,0},{20,4},{24,8},{28,12},{32,48},... | collective-permute-start | bytes 294920 | tf_op jit(solution)/shard_map/ppermute | solution.py:30
  15.2 1.4 %collective-permute-start.7 = (f16[3,64,256]{2,1,0:T(8,128)(2,1)S(1)}, f16[3,64,256]{2,1,0:T(8,128)(2,1)S(1)}, u32[]{:S(2)}, u32[]{:S(2)}) collective-permute-start(f16[3,64,256]{2,1,0:T(8,128)(2,1)S(1)} %collective-permute-done.2), channel_id=1, source_target_pairs={{0,1},{1,0},{2,3},{3,2},{4,5},{5,4},{6,7},{7,6},{8,9},{9,8},{10,11... | collective-permute-start | bytes 294920 | tf_op jit(solution)/shard_map/ppermute | solution.py:22
  15.4 1.6 %collective-permute-start.3 = (bf16[256,256]{1,0:T(8,128)(2,1)S(1)}, bf16[256,256]{1,0:T(8,128)(2,1)S(1)}, u32[]{:S(2)}, u32[]{:S(2)}) collective-permute-start(bf16[256,256]{1,0:T(8,128)(2,1)S(1)} %get-tuple-element.55), channel_id=1, source_target_pairs={{0,1},{1,0},{2,3},{3,2},{4,5},{5,4},{6,7},{7,6},{8,9},{9,8},{10,11... | collective-permute-start | bytes 393224 | tf_op jit(solution)/shard_map/ppermute | solution.py:22
  16.6 1.3 %collective-permute-start.4 = (bf16[256,256]{1,0:T(8,128)(2,1)S(1)}, bf16[256,256]{1,0:T(8,128)(2,1)S(1)}, u32[]{:S(2)}, u32[]{:S(2)}) collective-permute-start(bf16[256,256]{1,0:T(8,128)(2,1)S(1)} %get-tuple-element.54), channel_id=1, source_target_pairs={{0,1},{1,0},{2,3},{3,2},{4,5},{5,4},{6,7},{7,6},{8,9},{9,8},{10,11... | collective-permute-start | bytes 393224 | tf_op jit(solution)/shard_map/ppermute | solution.py:22
  16.9 4.6 %collective-permute-start.10 = (f16[3,64,256]{2,1,0:T(8,128)(2,1)S(1)}, f16[3,64,256]{2,1,0:T(8,128)(2,1)S(1)}, u32[]{:S(2)}, u32[]{:S(2)}) collective-permute-start(f16[3,64,256]{2,1,0:T(8,128)(2,1)S(1)} %collective-permute-done.8), channel_id=1, source_target_pairs={{0,1},{1,0},{2,3},{3,2},{4,5},{5,4},{6,7},{7,6},{8,9},{9,8},{10,11... | collective-permute-start | bytes 294920 | tf_op jit(solution)/shard_map/ppermute | solution.py:22
  17.9 8.8 %collective-permute-start.17 = (bf16[512,256]{1,0:T(8,128)(2,1)S(1)}, bf16[512,256]{1,0:T(8,128)(2,1)S(1)}, u32[]{:S(2)}, u32[]{:S(2)}) collective-permute-start(bf16[512,256]{1,0:T(8,128)(2,1)S(1)} %slice_bitcast_fusion), channel_id=1, source_target_pairs={{0,2},{2,0},{1,3},{3,1},{4,6},{6,4},{5,7},{7,5},{8,10},{10,8},{9,1... | collective-permute-start | bytes 786440 | tf_op jit(solution)/shard_map/ppermute | solution.py:26
  18.7 6.3 %collective-permute-start.5 = (f32[256,256]{1,0:T(8,128)S(1)}, f32[256,256]{1,0:T(8,128)S(1)}, u32[]{:S(2)}, u32[]{:S(2)}) collective-permute-start(f32[256,256]{1,0:T(8,128)S(1)} %eliminate0.1.s_own), channel_id=1, source_target_pairs={{0,1},{1,0},{2,3},{3,2},{4,5},{5,4},{6,7},{7,6},{8,9},{9,8},{10,11... | collective-permute-start | bytes 786440 | tf_op jit(solution)/shard_map/ppermute | solution.py:22
  21.5 1.3 %collective-permute-start.11 = (f16[3,64,256]{2,1,0:T(8,128)(2,1)S(1)}, f16[3,64,256]{2,1,0:T(8,128)(2,1)S(1)}, u32[]{:S(2)}, u32[]{:S(2)}) collective-permute-start(f16[3,64,256]{2,1,0:T(8,128)(2,1)S(1)} %collective-permute-done.9), channel_id=1, source_target_pairs={{0,1},{1,0},{2,3},{3,2},{4,5},{5,4},{6,7},{7,6},{8,9},{9,8},{10,11... | collective-permute-start | bytes 294920 | tf_op jit(solution)/shard_map/ppermute | solution.py:22
  21.5 2.3 %collective-permute-start.14 = (bf16[256,256]{1,0:T(8,128)(2,1)S(1)}, bf16[256,256]{1,0:T(8,128)(2,1)S(1)}, u32[]{:S(2)}, u32[]{:S(2)}) collective-permute-start(bf16[256,256]{1,0:T(8,128)(2,1)S(1)} %get-tuple-element.53), channel_id=1, source_target_pairs={{0,1},{1,0},{2,3},{3,2},{4,5},{5,4},{6,7},{7,6},{8,9},{9,8},{10,11... | collective-permute-start | bytes 393224 | tf_op jit(solution)/shard_map/ppermute | solution.py:22
  22.8 1.3 %collective-permute-start.15 = (bf16[256,256]{1,0:T(8,128)(2,1)S(1)}, bf16[256,256]{1,0:T(8,128)(2,1)S(1)}, u32[]{:S(2)}, u32[]{:S(2)}) collective-permute-start(bf16[256,256]{1,0:T(8,128)(2,1)S(1)} %get-tuple-element.52), channel_id=1, source_target_pairs={{0,1},{1,0},{2,3},{3,2},{4,5},{5,4},{6,7},{7,6},{8,9},{9,8},{10,11... | collective-permute-start | bytes 393224 | tf_op jit(solution)/shard_map/ppermute | solution.py:22
  24.8 2.6 %collective-permute-start.16 = (f32[256,256]{1,0:T(8,128)S(1)}, f32[256,256]{1,0:T(8,128)S(1)}, u32[]{:S(2)}, u32[]{:S(2)}) collective-permute-start(f32[256,256]{1,0:T(8,128)S(1)} %eliminate1.1.s_own), channel_id=1, source_target_pairs={{0,1},{1,0},{2,3},{3,2},{4,5},{5,4},{6,7},{7,6},{8,9},{9,8},{10,11... | collective-permute-start | bytes 786440 | tf_op jit(solution)/shard_map/ppermute | solution.py:22
  26.7 1.8 %collective-permute-start.18 = (bf16[256,256]{1,0:T(8,128)(2,1)S(1)}, bf16[256,256]{1,0:T(8,128)(2,1)S(1)}, u32[]{:S(2)}, u32[]{:S(2)}) collective-permute-start(bf16[256,256]{1,0:T(8,128)(2,1)S(1)} %get-tuple-element.51), channel_id=1, source_target_pairs={{0,1},{1,0},{2,3},{3,2},{4,5},{5,4},{6,7},{7,6},{8,9},{9,8},{10,11... | collective-permute-start | bytes 393224 | tf_op jit(solution)/shard_map/ppermute | solution.py:22
  26.9 1.7 %collective-permute-start.19 = (bf16[256,256]{1,0:T(8,128)(2,1)S(1)}, bf16[256,256]{1,0:T(8,128)(2,1)S(1)}, u32[]{:S(2)}, u32[]{:S(2)}) collective-permute-start(bf16[256,256]{1,0:T(8,128)(2,1)S(1)} %get-tuple-element.50), channel_id=1, source_target_pairs={{0,1},{1,0},{2,3},{3,2},{4,5},{5,4},{6,7},{7,6},{8,9},{9,8},{10,11... | collective-permute-start | bytes 393224 | tf_op jit(solution)/shard_map/ppermute | solution.py:22
  29.2 1.6 %collective-permute-start.20 = (f32[256,256]{1,0:T(8,128)S(1)}, f32[256,256]{1,0:T(8,128)S(1)}, u32[]{:S(2)}, u32[]{:S(2)}) collective-permute-start(f32[256,256]{1,0:T(8,128)S(1)} %eliminate2.1.s_own), channel_id=1, source_target_pairs={{0,1},{1,0},{2,3},{3,2},{4,5},{5,4},{6,7},{7,6},{8,9},{9,8},{10,11... | collective-permute-start | bytes 786440 | tf_op jit(solution)/shard_map/ppermute | solution.py:22
  29.5 6.2 %collective-permute-start.21 = (bf16[2,2,64,256]{3,2,1,0:T(8,128)(2,1)S(1)}, bf16[2,2,64,256]{3,2,1,0:T(8,128)(2,1)S(1)}, u32[]{:S(2)}, u32[]{:S(2)}) collective-permute-start(bf16[2,2,64,256]{3,2,1,0:T(8,128)(2,1)S(1)} %pad_maximum_fusion), channel_id=1, source_target_pairs={{0,2},{2,0},{1,3},{3,1},{4,6},{6,4},{5,7},{7,5},{8,10},{10,8},{9,1... | collective-permute-start | bytes 393224 | tf_op jit(solution)/shard_map/ppermute | solution.py:26
  32.0 4.7 %collective-permute-start.22 = (bf16[2,64,256]{2,1,0:T(8,128)(2,1)S(1)}, bf16[2,64,256]{2,1,0:T(8,128)(2,1)S(1)}, u32[]{:S(2)}, u32[]{:S(2)}) collective-permute-start(bf16[2,64,256]{2,1,0:T(8,128)(2,1)S(1)} %get-tuple-element.46), channel_id=1, source_target_pairs={{0,2},{2,0},{1,3},{3,1},{4,6},{6,4},{5,7},{7,5},{8,10},{10,8},{9,1... | collective-permute-start | bytes 196616 | tf_op jit(solution)/shard_map/ppermute | solution.py:26
  36.8 4.7 %collective-permute-start.23 = (bf16[3,64,256]{2,1,0:T(8,128)(2,1)S(1)}, bf16[3,64,256]{2,1,0:T(8,128)(2,1)S(1)}, u32[]{:S(2)}, u32[]{:S(2)}) collective-permute-start(bf16[3,64,256]{2,1,0:T(8,128)(2,1)S(1)} %fusion), channel_id=1, source_target_pairs={{0,16},{4,20},{8,24},{12,28},{16,0},{20,4},{24,8},{28,12},{32,48},... | collective-permute-start | bytes 294920 | tf_op jit(solution)/shard_map/ppermute | solution.py:30
  (4 other events, 11.8 us)

commit v6 on v5

--- a/solution.py
+++ b/solution.py
@@ -90,11 +90,10 @@
         copy.wait()
 
 
-def eliminate_kernel(n, e, d, chip, cross_a, cross_b, rt, s_out):
+def eliminate_kernel(n, e, d, chip, cross, rt, s_out):
     q = lax.axis_index("col")
     depth = chip.shape[0]
-    cross = jnp.concatenate([cross_a[...], cross_b[...]], 0)
-    elim = e[n] + dot(d[n, :, band(q & 1, depth)], chip[...]) + dot(d[n, :, band(1 - (q & 1), depth)], cross)
+    elim = e[n] + dot(d[n, :, band(q & 1, depth)], chip[...]) + dot(d[n, :, band(1 - (q & 1), depth)], cross[...])
     s_out[...] = dot(rt[n], elim.astype(BF16))
 
 
@@ -160,14 +159,13 @@
     chip_left.append(to_chip(last[2]))
 
     def cross(left):
-        half = depth // 2
-        return to_core(left[:half]), to_core(left[half:])
+        return (to_core(left),)
 
     def eliminate(n, chip, *earlier):
         return call(
             functools.partial(eliminate_kernel, n),
             shape((width, width), F32),
-            [VMEM] * 6,
+            [VMEM] * 5,
             f"eliminate{n}",
         )(after(e, *earlier), d, chip, *cross(chip), rt)
 

time: 42.6 us -> 42.3 us (level)
  waiting for transfers between devices: 13.1 us -> 14.4 us
  starting transfers between devices: 12.8 us -> 11.6 us
    ppermute x15 -> x12, waiting for transfers between devices: 3.06 us -> 3.82 us  [to_core(): return lax.ppermute(block, 'col', CORE)]
    ppermute x15 -> x12, starting transfers between devices: 3.87 us -> 3.13 us  [to_core(): return lax.ppermute(block, 'col', CORE)]
  transfers between devices with their start and end apart: 24 -> 21, of which waited for: 11 -> 10; matrix products, arithmetic and copies ran while one was open for 10% -> 10% of each run, Pallas kernels for 20% -> 21%
where the time goes in v6:
time: 42.3 us; the launch traced here: 42.1 us
  waiting for transfers between devices  14.4 us (34%)
  starting transfers between devices  11.6 us (27%)
  Pallas kernels  9.32 us (22%)
  local copies, waits for them, and re-layouts  4.01 us (9%)
  other arithmetic  1.95 us (5%)
  between operations  0.87 us (2%)
    ppermute x6, waiting for transfers between devices, to_chip(): return lax.ppermute(block, 'col', CHIP)  7.1 us
    ppermute x6, starting transfers between devices, to_chip(): return lax.ppermute(block, 'col', CHIP)  5.75 us
    ppermute x12, waiting for transfers between devices, to_core(): return lax.ppermute(block, 'col', CORE)  3.82 us
    ppermute x3, waiting for transfers between devices, to_sibling(): lax.ppermute(block, 'row', [(n, n ^ 1 << BIT) for n in range(lax.axis_siz...  3.45 us
    pallas_call x3, Pallas kernels, merge(): call(functools.partial(merge_kernel, n), [shape((2, part, width), F32), s...  3.44 us
    pallas_call x1, Pallas kernels, shards(): call(begin_kernel, [shape((nodes, depth, width), F32), shape((nodes, widt...  3.14 us
    ppermute x12, starting transfers between devices, to_core(): return lax.ppermute(block, 'col', CORE)  3.13 us
    ppermute x3, starting transfers between devices, to_sibling(): lax.ppermute(block, 'row', [(n, n ^ 1 << BIT) for n in range(lax.axis_siz...  2.68 us
  transfers between devices with their start and end apart: 21, of which 10 were waited for; matrix products, arithmetic and copies ran while one was open for 10% of the time, Pallas kernels for 21%

profile of v6, /device:TPU:8, one launch (start us, length us, event | category | flops | bytes accessed | tf_op | source)
XLA Modules:
  0.0 42.1 jit_solution(4452320761332097820)
XLA Ops:
  0.7 1.0 %slice_bitcast_fusion.2 = bf16[512,256]{1,0:T(8,128)(2,1)S(1)} fusion(bf16[3,512,256]{2,1,0:T(8,128)(2,1)} %own.1), kind=kLoop, calls=%fused_computation.4 | loop fusion | bytes 524288 | tf_op jit(solution)/shard_map/squeeze | solution.py:139
  1.8 2.3 %collective-permute-start.1 = (bf16[512,256]{1,0:T(8,128)(2,1)S(1)}, bf16[512,256]{1,0:T(8,128)(2,1)S(1)}, u32[]{:S(2)}, u32[]{:S(2)}) collective-permute-start(bf16[512,256]{1,0:T(8,128)(2,1)S(1)} %slice_bitcast_fusion.2), channel_id=1, source_target_pairs={{0,2},{2,0},{1,3},{3,1},{4,6},{6,4},{5,7},{7,5},{8,10},{10,8},{9,1... | collective-permute-start | bytes 786440 | tf_op jit(solution)/shard_map/ppermute | solution.py:26
  4.0 1.0 %bitcast_dynamic-update-slice_fusion.7 = (f16[8,3,64,256]{3,2,1,0:T(8,128)(2,1)S(1)}, f16[3,64,256]{2,1,0:T(8,128)(2,1)S(1)}) fusion(f32[3,64,256]{2,1,0:T(8,128)} %param.9, s32[3]{0:T(128)} %ranks.5, s32[64]{0:T(128)S(1)} %iota_add_fusion), kind=kLoop, calls=%fused_computation.18 | loop fusion | flops 196607 | bytes 393484
  5.3 1.6 %collective-permute-start.7 = (f16[3,64,256]{2,1,0:T(8,128)(2,1)S(1)}, f16[3,64,256]{2,1,0:T(8,128)(2,1)S(1)}, u32[]{:S(2)}, u32[]{:S(2)}) collective-permute-start(f16[3,64,256]{2,1,0:T(8,128)(2,1)S(1)} %get-tuple-element.49), channel_id=1, source_target_pairs={{0,2},{2,0},{1,3},{3,1},{4,6},{6,4},{5,7},{7,5},{8,10},{10,8},{9,1... | collective-permute-start | bytes 294920 | tf_op jit(solution)/shard_map/ppermute | solution.py:26
  6.9 1.0 %slice_bitcast_fusion.1 = bf16[512,256]{1,0:T(8,128)(2,1)S(1)} fusion(bf16[3,512,256]{2,1,0:T(8,128)(2,1)} %own.1), kind=kLoop, calls=%fused_computation.3 | loop fusion | bytes 524288 | tf_op jit(solution)/shard_map/squeeze | solution.py:146
  8.5 1.1 %copy-done.1 = bf16[3,512,256]{2,1,0:T(8,128)(2,1)S(1)} copy-done((bf16[3,512,256]{2,1,0:T(8,128)(2,1)S(1)}, bf16[3,512,256]{2,1,0:T(8,128)(2,1)}, u32[]{:S(2)}) %copy-start.1) | copy-done | bytes 786456
  9.6 3.1 %begin.1 = (f32[3,512,256]{2,1,0:T(8,128)S(1)}, bf16[3,256,512]{2,1,0:T(8,128)(2,1)S(1)}, bf16[3,512,1024]{2,1,0:T(8,128)(2,1)S(1)}) custom-call(bf16[3,512,2048]{2,1,0:T(8,128)(2,1)} %d.1, bf16[3,512,256]{2,1,0:T(8,128)(2,1)S(1)} %copy-done, bf16[3,512,256]{2,1,0:T(8,128)(2,1)S(1)} %collective-permute-done.core, bf16[3,512,256]{2,1,0:T(8,128)(2,1)S(1)} %copy-done.1), custom_call_target="tpu_custom_call" | custom-call | flops 1 | bytes 1 | tf_op jit(solution)/shard_map/begin/pallas_call | solution.py:150
  13.3 1.8 %collective-permute-start.8 = (f16[3,64,256]{2,1,0:T(8,128)(2,1)S(1)}, f16[3,64,256]{2,1,0:T(8,128)(2,1)S(1)}, u32[]{:S(2)}, u32[]{:S(2)}) collective-permute-start(f16[3,64,256]{2,1,0:T(8,128)(2,1)S(1)} %collective-permute-done.7), channel_id=1, source_target_pairs={{0,16},{4,20},{8,24},{12,28},{16,0},{20,4},{24,8},{28,12},{32,48},... | collective-permute-start | bytes 294920 | tf_op jit(solution)/shard_map/ppermute | solution.py:30
  15.9 0.9 %collective-permute-done.6 = f16[3,64,256]{2,1,0:T(8,128)(2,1)S(1)} collective-permute-done((f16[3,64,256]{2,1,0:T(8,128)(2,1)S(1)}, f16[3,64,256]{2,1,0:T(8,128)(2,1)S(1)}, u32[]{:S(2)}, u32[]{:S(2)}) %collective-permute-start.6) | collective-permute-done | bytes 98336 | tf_op jit(solution)/shard_map/ppermute | solution.py:22
  17.2 1.1 %collective-permute-done.3.cross = bf16[512,256]{1,0:T(8,128)(2,1)S(1)} collective-permute-done((bf16[512,256]{1,0:T(8,128)(2,1)S(1)}, bf16[512,256]{1,0:T(8,128)(2,1)S(1)}, u32[]{:S(2)}, u32[]{:S(2)}) %collective-permute-start.3) | collective-permute-done | bytes 262176 | tf_op jit(solution)/shard_map/ppermute | solution.py:22
  19.5 1.6 %collective-permute-done.12.chip = bf16[512,256]{1,0:T(8,128)(2,1)S(1)} collective-permute-done((bf16[512,256]{1,0:T(8,128)(2,1)S(1)}, bf16[512,256]{1,0:T(8,128)(2,1)S(1)}, u32[]{:S(2)}, u32[]{:S(2)}) %collective-permute-start.12) | collective-permute-done | bytes 262176 | tf_op jit(solution)/shard_map/ppermute | solution.py:26
  21.9 0.7 %couple.1 = (bf16[3,768,256]{2,1,0:T(8,128)(2,1)S(1)}, bf16[3,128,768]{2,1,0:T(8,128)(2,1)S(1)}, f32[3,128,256]{2,1,0:T(8,128)S(1)}) custom-call(f32[4,2,3,64,256]{4,3,2,1,0:T(8,128)S(1)} %bitcast.37, f32[3,64,256]{2,1,0:T(8,128)S(1)} %copy-done.2, f32[3,64,256]{2,1,0:T(8,128)S(1)} %collective-permute-done.11.c_core), custom_call_target="tpu_custom_call" | custom-call | flops 1 | bytes 1 | tf_op jit(solution)/shard_map/couple/pallas_call | solution.py:188
  24.1 1.1 %merge0.1 = (f32[2,64,256]{2,1,0:T(8,128)S(1)}, bf16[2,64,256]{2,1,0:T(8,128)(2,1)S(1)}) custom-call(s32[3]{0:T(128)S(1)} %copy-done.3, f32[256,256]{1,0:T(8,128)S(1)} %eliminate0.1.s_own, f32[256,256]{1,0:T(8,128)S(1)} %collective-permute-done.4.s_core, bf16[3,768,256]{2,1,0:T(8,128)(2,1)S(1)} %get-tuple-element.33.m, ...), custom_call_target="tpu_custom_call" | custom-call | flops 1 | bytes 1 | tf_op jit(solution)/shard_map/merge0/pallas_call | solution.py:173
  25.3 1.6 %collective-permute-done.15.chip = bf16[512,256]{1,0:T(8,128)(2,1)S(1)} collective-permute-done((bf16[512,256]{1,0:T(8,128)(2,1)S(1)}, bf16[512,256]{1,0:T(8,128)(2,1)S(1)}, u32[]{:S(2)}, u32[]{:S(2)}) %collective-permute-start.15) | collective-permute-done | bytes 262176 | tf_op jit(solution)/shard_map/ppermute | solution.py:26
  26.9 1.1 %merge1.1 = (f32[2,64,256]{2,1,0:T(8,128)S(1)}, bf16[2,64,256]{2,1,0:T(8,128)(2,1)S(1)}) custom-call(s32[3]{0:T(128)S(1)} %copy-done.3, f32[256,256]{1,0:T(8,128)S(1)} %eliminate1.1.s_own, f32[256,256]{1,0:T(8,128)S(1)} %collective-permute-done.14.s_core, bf16[3,768,256]{2,1,0:T(8,128)(2,1)S(1)} %get-tuple-element.33.m, ...), custom_call_target="tpu_custom_call" | custom-call | flops 1 | bytes 1 | tf_op jit(solution)/shard_map/merge1/pallas_call | solution.py:173
  28.4 0.7 %eliminate2.1.s_own = f32[256,256]{1,0:T(8,128)S(1)} custom-call(f32[3,512,256]{2,1,0:T(8,128)S(1)} %get-tuple-element.40.e, bf16[3,512,1024]{2,1,0:T(8,128)(2,1)S(1)} %get-tuple-element.26.d, bf16[512,256]{1,0:T(8,128)(2,1)S(1)} %collective-permute-done.15.chip, bf16[512,256]{1,0:T(8,128)(2,1)S(1)} %collective-permute-done.16.cross, ...), custom_call_target="tpu_custom_call" | custom-call | flops 1 | bytes 1 | tf_op jit(solution)/shard_map/eliminate2/pallas_call | solution.py:165
  29.8 1.0 %collective-permute-done.17.s_core = f32[256,256]{1,0:T(8,128)S(1)} collective-permute-done((f32[256,256]{1,0:T(8,128)S(1)}, f32[256,256]{1,0:T(8,128)S(1)}, u32[]{:S(2)}, u32[]{:S(2)}) %collective-permute-start.17) | collective-permute-done | bytes 262176 | tf_op jit(solution)/shard_map/ppermute | solution.py:22
  30.7 1.1 %merge2.1 = (f32[2,64,256]{2,1,0:T(8,128)S(1)}, bf16[2,64,256]{2,1,0:T(8,128)(2,1)S(1)}) custom-call(s32[3]{0:T(128)S(1)} %copy-done.3, f32[256,256]{1,0:T(8,128)S(1)} %eliminate2.1.s_own, f32[256,256]{1,0:T(8,128)S(1)} %collective-permute-done.17.s_core, bf16[3,768,256]{2,1,0:T(8,128)(2,1)S(1)} %get-tuple-element.33.m, ...), custom_call_target="tpu_custom_call" | custom-call | flops 1 | bytes 1 | tf_op jit(solution)/shard_map/merge2/pallas_call | solution.py:173
  31.9 0.9 %collective-permute-start.19 = (bf16[2,64,256]{2,1,0:T(8,128)(2,1)S(1)}, bf16[2,64,256]{2,1,0:T(8,128)(2,1)S(1)}, u32[]{:S(2)}, u32[]{:S(2)}) collective-permute-start(bf16[2,64,256]{2,1,0:T(8,128)(2,1)S(1)} %get-tuple-element.46), channel_id=1, source_target_pairs={{0,2},{2,0},{1,3},{3,1},{4,6},{6,4},{5,7},{7,5},{8,10},{10,8},{9,1... | collective-permute-start | bytes 196616 | tf_op jit(solution)/shard_map/ppermute | solution.py:26
  32.7 2.9 %collective-permute-done.18 = bf16[2,2,64,256]{3,2,1,0:T(8,128)(2,1)S(1)} collective-permute-done((bf16[2,2,64,256]{3,2,1,0:T(8,128)(2,1)S(1)}, bf16[2,2,64,256]{3,2,1,0:T(8,128)(2,1)S(1)}, u32[]{:S(2)}, u32[]{:S(2)}) %collective-permute-start.18) | collective-permute-done | bytes 131104 | tf_op jit(solution)/shard_map/ppermute | solution.py:26
  35.7 1.0 %collective-permute-done.19 = bf16[2,64,256]{2,1,0:T(8,128)(2,1)S(1)} collective-permute-done((bf16[2,64,256]{2,1,0:T(8,128)(2,1)S(1)}, bf16[2,64,256]{2,1,0:T(8,128)(2,1)S(1)}, u32[]{:S(2)}, u32[]{:S(2)}) %collective-permute-start.19) | collective-permute-done | bytes 65568 | tf_op jit(solution)/shard_map/ppermute | solution.py:26
  37.3 0.7 %slice_bitcast_fusion.4 = f32[3,64,256]{2,1,0:T(8,128)} fusion(f32[3,2,64,256]{3,2,1,0:T(8,128)S(1)} %maximum_add_fusion), kind=kLoop, calls=%fused_computation.6 | loop fusion | bytes 393216 | tf_op jit(solution)/shard_map/squeeze | solution.py:209
  38.0 3.4 %collective-permute-done.20 = bf16[3,64,256]{2,1,0:T(8,128)(2,1)S(1)} collective-permute-done((bf16[3,64,256]{2,1,0:T(8,128)(2,1)S(1)}, bf16[3,64,256]{2,1,0:T(8,128)(2,1)S(1)}, u32[]{:S(2)}, u32[]{:S(2)}) %collective-permute-start.20) | collective-permute-done | bytes 98336 | tf_op jit(solution)/shard_map/ppermute | solution.py:30
  41.4 0.7 %convert_add_fusion = f32[3,64,256]{2,1,0:T(8,128)} fusion(bf16[3,64,256]{2,1,0:T(8,128)(2,1)S(1)} %collective-permute-done.20, f32[3,2,64,256]{3,2,1,0:T(8,128)S(1)} %maximum_add_fusion), kind=kLoop, calls=%fused_computation.7 | loop fusion | flops 98304 | bytes 491520 | tf_op jit(solution)/shard_map/add | solution.py:210
  (52 shorter events, 7.6 us)
Async XLA Ops:
  0.6 7.9 %copy-start = (bf16[3,512,256]{2,1,0:T(8,128)(2,1)S(1)}, bf16[3,512,256]{2,1,0:T(8,128)(2,1)}, u32[]{:S(2)}) copy-start(bf16[3,512,256]{2,1,0:T(8,128)(2,1)} %own.1) | copy-start | bytes 2359300
  0.6 7.3 %collective-permute-start = (bf16[3,512,256]{2,1,0:T(8,128)(2,1)}, bf16[3,512,256]{2,1,0:T(8,128)(2,1)S(1)}, u32[]{:S(2)}, u32[]{:S(2)}) collective-permute-start(bf16[3,512,256]{2,1,0:T(8,128)(2,1)} %own.1), channel_id=1, source_target_pairs={{0,1},{1,0},{2,3},{3,2},{4,5},{5,4},{6,7},{7,6},{8,9},{9,8},{10,11... | collective-permute-start | bytes 2359304 | tf_op jit(solution)/shard_map/ppermute | solution.py:22
  1.8 13.4 %collective-permute-start.1 = (bf16[512,256]{1,0:T(8,128)(2,1)S(1)}, bf16[512,256]{1,0:T(8,128)(2,1)S(1)}, u32[]{:S(2)}, u32[]{:S(2)}) collective-permute-start(bf16[512,256]{1,0:T(8,128)(2,1)S(1)} %slice_bitcast_fusion.2), channel_id=1, source_target_pairs={{0,2},{2,0},{1,3},{3,1},{4,6},{6,4},{5,7},{7,5},{8,10},{10,8},{9,1... | collective-permute-start | bytes 786440 | tf_op jit(solution)/shard_map/ppermute | solution.py:26
  5.1 7.7 %collective-permute-start.2 = (f16[3,64,256]{2,1,0:T(8,128)(2,1)S(1)}, f16[3,64,256]{2,1,0:T(8,128)(2,1)S(1)}, u32[]{:S(2)}, u32[]{:S(2)}) collective-permute-start(f16[3,64,256]{2,1,0:T(8,128)(2,1)S(1)} %get-tuple-element.49), channel_id=1, source_target_pairs={{0,16},{4,20},{8,24},{12,28},{16,0},{20,4},{24,8},{28,12},{32,48},... | collective-permute-start | bytes 294920 | tf_op jit(solution)/shard_map/ppermute | solution.py:30
  5.3 8.0 %collective-permute-start.7 = (f16[3,64,256]{2,1,0:T(8,128)(2,1)S(1)}, f16[3,64,256]{2,1,0:T(8,128)(2,1)S(1)}, u32[]{:S(2)}, u32[]{:S(2)}) collective-permute-start(f16[3,64,256]{2,1,0:T(8,128)(2,1)S(1)} %get-tuple-element.49), channel_id=1, source_target_pairs={{0,2},{2,0},{1,3},{3,1},{4,6},{6,4},{5,7},{7,5},{8,10},{10,8},{9,1... | collective-permute-start | bytes 294920 | tf_op jit(solution)/shard_map/ppermute | solution.py:26
  6.9 8.3 %collective-permute-start.5 = (f16[3,64,256]{2,1,0:T(8,128)(2,1)S(1)}, f16[3,64,256]{2,1,0:T(8,128)(2,1)S(1)}, u32[]{:S(2)}, u32[]{:S(2)}) collective-permute-start(f16[3,64,256]{2,1,0:T(8,128)(2,1)S(1)} %get-tuple-element.49), channel_id=1, source_target_pairs={{0,1},{1,0},{2,3},{3,2},{4,5},{5,4},{6,7},{7,6},{8,9},{9,8},{10,11... | collective-permute-start | bytes 294920 | tf_op jit(solution)/shard_map/ppermute | solution.py:22
  7.9 14.0 %collective-permute-start.11 = (f32[3,64,256]{2,1,0:T(8,128)}, f32[3,64,256]{2,1,0:T(8,128)S(1)}, u32[]{:S(2)}, u32[]{:S(2)}) collective-permute-start(f32[3,64,256]{2,1,0:T(8,128)} %c_own.1), channel_id=1, source_target_pairs={{0,1},{1,0},{2,3},{3,2},{4,5},{5,4},{6,7},{7,6},{8,9},{9,8},{10,11... | collective-permute-start | bytes 589832 | tf_op jit(solution)/shard_map/ppermute | solution.py:22
  12.8 8.3 %collective-permute-start.12 = (bf16[512,256]{1,0:T(8,128)(2,1)S(1)}, bf16[512,256]{1,0:T(8,128)(2,1)S(1)}, u32[]{:S(2)}, u32[]{:S(2)}) collective-permute-start(bf16[512,256]{1,0:T(8,128)(2,1)S(1)} %slice_bitcast_fusion.1), channel_id=1, source_target_pairs={{0,2},{2,0},{1,3},{3,1},{4,6},{6,4},{5,7},{7,5},{8,10},{10,8},{9,1... | collective-permute-start | bytes 786440 | tf_op jit(solution)/shard_map/ppermute | solution.py:26
  13.3 5.8 %collective-permute-start.8 = (f16[3,64,256]{2,1,0:T(8,128)(2,1)S(1)}, f16[3,64,256]{2,1,0:T(8,128)(2,1)S(1)}, u32[]{:S(2)}, u32[]{:S(2)}) collective-permute-start(f16[3,64,256]{2,1,0:T(8,128)(2,1)S(1)} %collective-permute-done.7), channel_id=1, source_target_pairs={{0,16},{4,20},{8,24},{12,28},{16,0},{20,4},{24,8},{28,12},{32,48},... | collective-permute-start | bytes 294920 | tf_op jit(solution)/shard_map/ppermute | solution.py:30
  15.2 5.9 %collective-permute-start.9 = (f16[3,64,256]{2,1,0:T(8,128)(2,1)S(1)}, f16[3,64,256]{2,1,0:T(8,128)(2,1)S(1)}, u32[]{:S(2)}, u32[]{:S(2)}) collective-permute-start(f16[3,64,256]{2,1,0:T(8,128)(2,1)S(1)} %collective-permute-done.7), channel_id=1, source_target_pairs={{0,1},{1,0},{2,3},{3,2},{4,5},{5,4},{6,7},{7,6},{8,9},{9,8},{10,11... | collective-permute-start | bytes 294920 | tf_op jit(solution)/shard_map/ppermute | solution.py:22
  15.3 1.5 %collective-permute-start.6 = (f16[3,64,256]{2,1,0:T(8,128)(2,1)S(1)}, f16[3,64,256]{2,1,0:T(8,128)(2,1)S(1)}, u32[]{:S(2)}, u32[]{:S(2)}) collective-permute-start(f16[3,64,256]{2,1,0:T(8,128)(2,1)S(1)} %collective-permute-done.2), channel_id=1, source_target_pairs={{0,1},{1,0},{2,3},{3,2},{4,5},{5,4},{6,7},{7,6},{8,9},{9,8},{10,11... | collective-permute-start | bytes 294920 | tf_op jit(solution)/shard_map/ppermute | solution.py:22
  16.8 1.5 %collective-permute-start.3 = (bf16[512,256]{1,0:T(8,128)(2,1)S(1)}, bf16[512,256]{1,0:T(8,128)(2,1)S(1)}, u32[]{:S(2)}, u32[]{:S(2)}) collective-permute-start(bf16[512,256]{1,0:T(8,128)(2,1)S(1)} %collective-permute-done.1.chip), channel_id=1, source_target_pairs={{0,1},{1,0},{2,3},{3,2},{4,5},{5,4},{6,7},{7,6},{8,9},{9,8},{10,11... | collective-permute-start | bytes 786440 | tf_op jit(solution)/shard_map/ppermute | solution.py:22
  18.3 8.6 %collective-permute-start.15 = (bf16[512,256]{1,0:T(8,128)(2,1)S(1)}, bf16[512,256]{1,0:T(8,128)(2,1)S(1)}, u32[]{:S(2)}, u32[]{:S(2)}) collective-permute-start(bf16[512,256]{1,0:T(8,128)(2,1)S(1)} %slice_bitcast_fusion), channel_id=1, source_target_pairs={{0,2},{2,0},{1,3},{3,1},{4,6},{6,4},{5,7},{7,5},{8,10},{10,8},{9,1... | collective-permute-start | bytes 786440 | tf_op jit(solution)/shard_map/ppermute | solution.py:26
  19.1 2.8 %copy-start.2 = (f32[3,64,256]{2,1,0:T(8,128)S(1)}, f32[3,64,256]{2,1,0:T(8,128)}, u32[]{:S(2)}) copy-start(f32[3,64,256]{2,1,0:T(8,128)} %c_own.1) | copy-start | bytes 589828
  19.2 2.5 %collective-permute-start.10 = (f16[3,64,256]{2,1,0:T(8,128)(2,1)S(1)}, f16[3,64,256]{2,1,0:T(8,128)(2,1)S(1)}, u32[]{:S(2)}, u32[]{:S(2)}) collective-permute-start(f16[3,64,256]{2,1,0:T(8,128)(2,1)S(1)} %collective-permute-done.8), channel_id=1, source_target_pairs={{0,1},{1,0},{2,3},{3,2},{4,5},{5,4},{6,7},{7,6},{8,9},{9,8},{10,11... | collective-permute-start | bytes 294920 | tf_op jit(solution)/shard_map/ppermute | solution.py:22
  21.1 3.0 %collective-permute-start.4 = (f32[256,256]{1,0:T(8,128)S(1)}, f32[256,256]{1,0:T(8,128)S(1)}, u32[]{:S(2)}, u32[]{:S(2)}) collective-permute-start(f32[256,256]{1,0:T(8,128)S(1)} %eliminate0.1.s_own), channel_id=1, source_target_pairs={{0,1},{1,0},{2,3},{3,2},{4,5},{5,4},{6,7},{7,6},{8,9},{9,8},{10,11... | collective-permute-start | bytes 786440 | tf_op jit(solution)/shard_map/ppermute | solution.py:22
  21.1 1.9 %collective-permute-start.13 = (bf16[512,256]{1,0:T(8,128)(2,1)S(1)}, bf16[512,256]{1,0:T(8,128)(2,1)S(1)}, u32[]{:S(2)}, u32[]{:S(2)}) collective-permute-start(bf16[512,256]{1,0:T(8,128)(2,1)S(1)} %collective-permute-done.12.chip), channel_id=1, source_target_pairs={{0,1},{1,0},{2,3},{3,2},{4,5},{5,4},{6,7},{7,6},{8,9},{9,8},{10,11... | collective-permute-start | bytes 786440 | tf_op jit(solution)/shard_map/ppermute | solution.py:22
  22.6 1.5 %copy-start.3 = (s32[3]{0:T(128)S(1)}, s32[3]{0:T(128)}, u32[]{:S(2)}) copy-start(s32[3]{0:T(128)} %ranks.5) | copy-start | bytes 40
  23.7 3.2 %collective-permute-start.14 = (f32[256,256]{1,0:T(8,128)S(1)}, f32[256,256]{1,0:T(8,128)S(1)}, u32[]{:S(2)}, u32[]{:S(2)}) collective-permute-start(f32[256,256]{1,0:T(8,128)S(1)} %eliminate1.1.s_own), channel_id=1, source_target_pairs={{0,1},{1,0},{2,3},{3,2},{4,5},{5,4},{6,7},{7,6},{8,9},{9,8},{10,11... | collective-permute-start | bytes 786440 | tf_op jit(solution)/shard_map/ppermute | solution.py:22
  26.9 1.5 %collective-permute-start.16 = (bf16[512,256]{1,0:T(8,128)(2,1)S(1)}, bf16[512,256]{1,0:T(8,128)(2,1)S(1)}, u32[]{:S(2)}, u32[]{:S(2)}) collective-permute-start(bf16[512,256]{1,0:T(8,128)(2,1)S(1)} %collective-permute-done.15.chip), channel_id=1, source_target_pairs={{0,1},{1,0},{2,3},{3,2},{4,5},{5,4},{6,7},{7,6},{8,9},{9,8},{10,11... | collective-permute-start | bytes 786440 | tf_op jit(solution)/shard_map/ppermute | solution.py:22
  29.1 1.6 %collective-permute-start.17 = (f32[256,256]{1,0:T(8,128)S(1)}, f32[256,256]{1,0:T(8,128)S(1)}, u32[]{:S(2)}, u32[]{:S(2)}) collective-permute-start(f32[256,256]{1,0:T(8,128)S(1)} %eliminate2.1.s_own), channel_id=1, source_target_pairs={{0,1},{1,0},{2,3},{3,2},{4,5},{5,4},{6,7},{7,6},{8,9},{9,8},{10,11... | collective-permute-start | bytes 786440 | tf_op jit(solution)/shard_map/ppermute | solution.py:22
  29.4 6.3 %collective-permute-start.18 = (bf16[2,2,64,256]{3,2,1,0:T(8,128)(2,1)S(1)}, bf16[2,2,64,256]{3,2,1,0:T(8,128)(2,1)S(1)}, u32[]{:S(2)}, u32[]{:S(2)}) collective-permute-start(bf16[2,2,64,256]{3,2,1,0:T(8,128)(2,1)S(1)} %pad_maximum_fusion), channel_id=1, source_target_pairs={{0,2},{2,0},{1,3},{3,1},{4,6},{6,4},{5,7},{7,5},{8,10},{10,8},{9,1... | collective-permute-start | bytes 393224 | tf_op jit(solution)/shard_map/ppermute | solution.py:26
  31.9 4.7 %collective-permute-start.19 = (bf16[2,64,256]{2,1,0:T(8,128)(2,1)S(1)}, bf16[2,64,256]{2,1,0:T(8,128)(2,1)S(1)}, u32[]{:S(2)}, u32[]{:S(2)}) collective-permute-start(bf16[2,64,256]{2,1,0:T(8,128)(2,1)S(1)} %get-tuple-element.46), channel_id=1, source_target_pairs={{0,2},{2,0},{1,3},{3,1},{4,6},{6,4},{5,7},{7,5},{8,10},{10,8},{9,1... | collective-permute-start | bytes 196616 | tf_op jit(solution)/shard_map/ppermute | solution.py:26
  36.7 4.7 %collective-permute-start.20 = (bf16[3,64,256]{2,1,0:T(8,128)(2,1)S(1)}, bf16[3,64,256]{2,1,0:T(8,128)(2,1)S(1)}, u32[]{:S(2)}, u32[]{:S(2)}) collective-permute-start(bf16[3,64,256]{2,1,0:T(8,128)(2,1)S(1)} %fusion), channel_id=1, source_target_pairs={{0,16},{4,20},{8,24},{12,28},{16,0},{20,4},{24,8},{28,12},{32,48},... | collective-permute-start | bytes 294920 | tf_op jit(solution)/shard_map/ppermute | solution.py:30
  (1 other events, 1.1 us)
